TPU v7x, 32 devices: a whole 2x2x4 slice. The times are simulated.
32 devices in a mesh: period: 4 (over y, x), row: 2 (over core), col: 4 (over z).
Axes of the slice: x: 2, y: 2, z: 4, core: 2. Of those that a mesh axis runs over, the one named last changes fastest.
Arguments:
- primal_start: float32 [512, 512], P(('period', 'row'), 'col'), may hold values from 0 to 1
- dual_start: float32 [512, 256], P(('period', 'col'), 'row'), may hold values from -3 to 3
- objective: float32 [512, 512], P(('period', 'row'), 'col'), may hold values from -28.8 to 28.8
- right_side: float32 [512, 256], P(('period', 'col'), 'row'), may hold values from -28.8 to 28.8
- upper_bound: float32 [512, 512], P(('period', 'row'), 'col'), may hold values from 0.5 to 4
- column_kind: int32 [512, 512], P(('period', 'row'), 'col'), may hold values from 0 to 2
- row_kind: int32 [512, 256], P(('period', 'col'), 'row'), may hold values from 0 to 1
- tile_values: float32 [4, 2, 4, 32, 128, 128], P('period', 'row', 'col'), may hold values from -0.5 to 0.5
- tile_rows: int32 [4, 2, 4, 32], P('period', 'row', 'col'), may hold values from 0 to 127
- tile_cols: int32 [4, 2, 4, 32], P('period', 'row', 'col'), may hold values from 0 to 127
- coupling: float32 [4, 2, 4, 128, 128], P('period', 'row', 'col'), may hold values from -0.5 to 0.5
Outputs:
- primal_final: float32 [512, 512], P(('period', 'row'), 'col')
- dual_final: float32 [512, 256], P(('period', 'col'), 'row')
- primal_weight: float32 [], replicated
Inputs may be any that keep to these rules, and one draw needn't show every extreme that they name: `column_kind`: 0: the variable is at least 0; 1: it lies between 0 and its upper_bound; 2: it is free. `row_kind`: 0: the row is an inequality (A x >= right_side, multiplier at least 0); 1: an equality. `tile_rows`: tiles listed twice for the same place add.
All inputs are finite; a program needn't handle non-finite values.
Results may differ from a plain program's by a relative error of at most 0.0001.
Values sent between devices are 32-bit elements; how exact they have to be, the bound alone decides.
No kernel may reach another device: no remote copies, remote signals or barrier semaphores. Data moves between devices by JAX's collectives and lax.ppermute only.
A program may use at most 64 MiB of HBM per device.

v0:
```python
import jax
import jax.numpy as jnp
from jax import lax
from jax.sharding import PartitionSpec as P

ROUNDS = 2
INNER = 2


HIGHEST_MODE = lax.Precision.HIGHEST
STEP_SCALE = 0.15
EPSILON = 1e-06


def shifted(x, axis, by):
    peers = lax.axis_size(axis)
    pairs = [(i, i + by) for i in range(peers) if 0 <= i + by < peers]
    return lax.ppermute(x, axis, pairs)


def project_primal(values, column_kind, upper_bound):
    lifted = jnp.maximum(values, 0.0)
    boxed = jnp.minimum(lifted, upper_bound)
    return jnp.where(column_kind == 2, values, jnp.where(column_kind == 1, boxed, lifted))


def project_dual(values, row_kind):
    return jnp.where(row_kind == 0, jnp.maximum(values, 0.0), values)


def per_device(
    primal_start,
    dual_start,
    objective,
    right_side,
    upper_bound,
    column_kind,
    row_kind,
    tile_values,
    tile_rows,
    tile_cols,
    coupling,
):
    tile_size = tile_values.shape[-1]
    tiles_here = tile_values.reshape(tile_values.shape[3:])
    row_list = tile_rows.reshape(-1)
    col_list = tile_cols.reshape(-1)
    link_tile = coupling.reshape(tile_size, tile_size)
    col_share = primal_start.shape[0]
    row_share = dual_start.shape[0]
    col_blocks = col_share * lax.axis_size("row")
    row_blocks = row_share * lax.axis_size("col")
    row_onehot = (row_list[:, None] == jnp.arange(row_blocks, dtype=jnp.int32)[None, :]).astype(
        jnp.float32
    )
    col_onehot = (col_list[:, None] == jnp.arange(col_blocks, dtype=jnp.int32)[None, :]).astype(
        jnp.float32
    )
    scale_totals = lax.psum(
        (jnp.sum(objective * objective), jnp.sum(right_side * right_side)), ("period", "row", "col")
    )
    weight = jnp.sqrt((scale_totals[0] + EPSILON) / (scale_totals[1] + EPSILON))
    primal, cost_block, upper_block, kind_block = (
        primal_start,
        objective,
        upper_bound,
        column_kind,
    )
    dual, rhs_block, row_kind_block = (dual_start, right_side, row_kind)
    for round_index in range(ROUNDS):
        primal_step = STEP_SCALE / weight
        dual_step = STEP_SCALE * weight
        primal_begin = primal
        dual_begin = dual
        primal_total = jnp.zeros_like(primal)
        dual_total = jnp.zeros_like(dual)
        for inner_index in range(INNER):
            rows_all = lax.all_gather(dual, "col", axis=0, tiled=True)
            first_tile = dual[0:1]
            outflow = jnp.einsum("ai,ij->aj", first_tile, link_tile, precision=HIGHEST_MODE)
            later = shifted(outflow, "period", -1)
            picked = jnp.take(rows_all, row_list, axis=0)
            products = jnp.einsum("nij,ni->nj", tiles_here, picked, precision=HIGHEST_MODE)
            partial_value = jnp.einsum("nt,nj->tj", col_onehot, products, precision=HIGHEST_MODE)
            summed = lax.psum_scatter(partial_value, "row", scatter_dimension=0, tiled=True)
            gradient = cost_block - summed.at[col_share - 1 :].add(later)
            primal_next = project_primal(primal - primal_step * gradient, kind_block, upper_block)
            forward_vector = 2.0 * primal_next - primal
            columns_all = lax.all_gather(forward_vector, "row", axis=0, tiled=True)
            last_tile = forward_vector[col_share - 1 :]
            earlier = shifted(last_tile, "period", 1)
            inflow = jnp.einsum("ij,aj->ai", link_tile, earlier, precision=HIGHEST_MODE)
            forward_picked = jnp.take(columns_all, col_list, axis=0)
            forward_products = jnp.einsum(
                "nij,nj->ni", tiles_here, forward_picked, precision=HIGHEST_MODE
            )
            forward_partial_value = jnp.einsum(
                "ns,ni->si", row_onehot, forward_products, precision=HIGHEST_MODE
            )
            forward_summed = lax.psum_scatter(
                forward_partial_value, "col", scatter_dimension=0, tiled=True
            )
            residual = rhs_block - forward_summed.at[0:1].add(inflow)
            dual = project_dual(dual + dual_step * residual, row_kind_block)
            primal = primal_next
            primal_total = primal_total + primal
            dual_total = dual_total + dual
        primal = primal_total / INNER
        dual = dual_total / INNER
        primal_moved = primal - primal_begin
        dual_moved = dual - dual_begin
        moves = lax.psum(
            (jnp.sum(primal_moved * primal_moved), jnp.sum(dual_moved * dual_moved)),
            ("period", "row", "col"),
        )
        weight = jnp.sqrt(weight * jnp.sqrt((moves[0] + EPSILON) / (moves[1] + EPSILON)))
    return (primal, dual, weight)


def solution(mesh):
    in_specs = (
        P(("period", "row"), "col"),
        P(("period", "col"), "row"),
        P(("period", "row"), "col"),
        P(("period", "col"), "row"),
        P(("period", "row"), "col"),
        P(("period", "row"), "col"),
        P(("period", "col"), "row"),
        P("period", "row", "col", None, None, None),
        P("period", "row", "col", None),
        P("period", "row", "col", None),
        P("period", "row", "col", None, None),
    )
    out_specs = (P(("period", "row"), "col"), P(("period", "col"), "row"), P())
    return jax.shard_map(
        per_device, mesh=mesh, in_specs=in_specs, out_specs=out_specs, check_vma=False
    )
```

profile of v0, /device:TPU:0, one launch (start us, length us, event | category | flops | bytes accessed | tf_op | source)
XLA Modules:
  0.0 361.1 jit_solution(18046558239013948703)
XLA Ops:
  11.1 15.1 %all_gather.24 = f32[128,128]{1,0:T(8,128)S(1)} all-gather(f32[32,128]{1,0:T(8,128)} %param.30), channel_id=1, replica_groups=mesh['period'=4,'row'=2,'col'=4] {'col'}, dimensions={0}, use_global_device_ids=true | all-gather | bytes 81920 | tf_op jit(solution)/shard_map/all_gather | solution.py:78
  26.8 1.9 fusion.14
  31.0 41.6 %all-reduce.2 = (f32[]{:T(128)}, f32[]{:T(128)}) all-reduce(f32[]{:T(128)} %multiply_reduce_fusion.2, f32[]{:T(128)} %multiply_reduce_fusion.5), channel_id=1, replica_groups=mesh['period'=4,'row'=2,'col'=4] {'period','row','col'}, use_global_device_ids=true, to_apply=%region_1.0 | all-reduce | flops 2 | bytes 16 | tf_op jit(solution)/shard_map/psum | solution.py:59
  76.8 1.9 all_gather.25
  79.3 3.4 fusion.12
  83.7 4.2 %collective-permute-start.1 = (f32[1,128]{1,0:T(1,128)S(1)}, f32[1,128]{1,0:T(1,128)S(1)}, u32[]{:S(2)}, u32[]{:S(2)}) collective-permute-start(f32[1,128]{1,0:T(1,128)S(1)} %slice.210), channel_id=1, source_target_pairs={{0,8},{8,16},{16,24},{1,9},{9,17},{17,25},{2,10},{10,18},{18,26},{... | collective-permute-start | bytes 1544 | tf_op jit(solution)/shard_map/ppermute | solution.py:18
  89.2 14.6 %reduce-scatter.11.cloned.1.call-done = f32[32,128]{1,0:T(8,128)} async-done(((f32[128,128]{1,0:T(8,128)}), f32[32,128]{1,0:T(8,128)}) %reduce-scatter.11.cloned.1.call-update) | async-done | bytes 16400 | tf_op jit(solution)/shard_map/reduce_scatter | solution.py:100
  106.7 13.1 %all_gather.26 = f32[128,128]{1,0:T(8,128)S(1)} all-gather(f32[32,128]{1,0:T(8,128)S(1)} %get-tuple-element.114), channel_id=1, replica_groups=mesh['period'=4,'row'=2,'col'=4] {'col'}, dimensions={0}, use_global_device_ids=true | all-gather | bytes 81920 | tf_op jit(solution)/shard_map/all_gather | solution.py:78
  120.5 1.9 fusion.10
  124.8 4.1 %collective-permute-done.2 = f32[1,128]{1,0:T(1,128)S(1)} collective-permute-done((f32[1,128]{1,0:T(1,128)S(1)}, f32[1,128]{1,0:T(1,128)S(1)}, u32[]{:S(2)}, u32[]{:S(2)}) %collective-permute-start.2) | collective-permute-done | bytes 544 | tf_op jit(solution)/shard_map/ppermute | solution.py:18
  131.0 1.4 multiply_reduce_fusion.1
  132.4 1.8 all_gather.27
  134.9 3.4 fusion.8
  139.3 4.1 %collective-permute-start.3 = (f32[1,128]{1,0:T(1,128)S(1)}, f32[1,128]{1,0:T(1,128)S(1)}, u32[]{:S(2)}, u32[]{:S(2)}) collective-permute-start(f32[1,128]{1,0:T(1,128)S(1)} %slice.214), channel_id=1, source_target_pairs={{0,8},{8,16},{16,24},{1,9},{9,17},{17,25},{2,10},{10,18},{18,26},{... | collective-permute-start | bytes 1544 | tf_op jit(solution)/shard_map/ppermute | solution.py:18
  144.7 14.9 %reduce-scatter.15.cloned.1.call-done = f32[32,128]{1,0:T(8,128)} async-done(((f32[128,128]{1,0:T(8,128)}), f32[32,128]{1,0:T(8,128)}) %reduce-scatter.15.cloned.1.call-update) | async-done | bytes 16400 | tf_op jit(solution)/shard_map/reduce_scatter | solution.py:100
  163.1 13.3 %all_gather.28 = f32[128,128]{1,0:T(8,128)S(1)} all-gather(f32[32,128]{1,0:T(8,128)S(1)} %get-tuple-element.111), channel_id=1, replica_groups=mesh['period'=4,'row'=2,'col'=4] {'col'}, dimensions={0}, use_global_device_ids=true | all-gather | bytes 81920 | tf_op jit(solution)/shard_map/all_gather | solution.py:78
  177.0 1.9 fusion.6
  181.4 39.9 %all-reduce.1 = (f32[]{:T(128)}, f32[]{:T(128)}) all-reduce(f32[]{:T(128)} %get-tuple-element.112, f32[]{:T(128)} %get-tuple-element.110), channel_id=1, replica_groups=mesh['period'=4,'row'=2,'col'=4] {'period','row','col'}, use_global_device_ids=true, to_apply=%region_8.10 | all-reduce | flops 2 | bytes 16 | tf_op jit(solution)/shard_map/psum | solution.py:112
  225.6 1.9 all_gather.29
  228.1 3.4 fusion.4
  232.5 4.2 %collective-permute-start.5 = (f32[1,128]{1,0:T(1,128)S(1)}, f32[1,128]{1,0:T(1,128)S(1)}, u32[]{:S(2)}, u32[]{:S(2)}) collective-permute-start(f32[1,128]{1,0:T(1,128)S(1)} %slice.218), channel_id=1, source_target_pairs={{0,8},{8,16},{16,24},{1,9},{9,17},{17,25},{2,10},{10,18},{18,26},{... | collective-permute-start | bytes 1544 | tf_op jit(solution)/shard_map/ppermute | solution.py:18
  237.9 14.5 %reduce-scatter.19.cloned.1.call-done = f32[32,128]{1,0:T(8,128)} async-done(((f32[128,128]{1,0:T(8,128)}), f32[32,128]{1,0:T(8,128)}) %reduce-scatter.19.cloned.1.call-update) | async-done | bytes 16400 | tf_op jit(solution)/shard_map/reduce_scatter | solution.py:100
  255.3 13.1 %all_gather.30 = f32[128,128]{1,0:T(8,128)S(1)} all-gather(f32[32,128]{1,0:T(8,128)S(1)} %maximum_select_fusion.1), channel_id=1, replica_groups=mesh['period'=4,'row'=2,'col'=4] {'col'}, dimensions={0}, use_global_device_ids=true | all-gather | bytes 81920 | tf_op jit(solution)/shard_map/all_gather | solution.py:78
  269.1 1.9 fusion.2
  273.5 4.1 %collective-permute-done.6 = f32[1,128]{1,0:T(1,128)S(1)} collective-permute-done((f32[1,128]{1,0:T(1,128)S(1)}, f32[1,128]{1,0:T(1,128)S(1)}, u32[]{:S(2)}, u32[]{:S(2)}) %collective-permute-start.6) | collective-permute-done | bytes 544 | tf_op jit(solution)/shard_map/ppermute | solution.py:18
  279.8 2.0 multiply_reduce_fusion
  281.8 1.8 all_gather.31
  284.2 3.4 fusion
  288.6 4.1 %collective-permute-start.7 = (f32[1,128]{1,0:T(1,128)S(1)}, f32[1,128]{1,0:T(1,128)S(1)}, u32[]{:S(2)}, u32[]{:S(2)}) collective-permute-start(f32[1,128]{1,0:T(1,128)S(1)} %slice.222), channel_id=1, source_target_pairs={{0,8},{8,16},{16,24},{1,9},{9,17},{17,25},{2,10},{10,18},{18,26},{... | collective-permute-start | bytes 1544 | tf_op jit(solution)/shard_map/ppermute | solution.py:18
  294.0 14.9 %reduce-scatter.23.cloned.1.call-done = f32[32,128]{1,0:T(8,128)} async-done(((f32[128,128]{1,0:T(8,128)}), f32[32,128]{1,0:T(8,128)}) %reduce-scatter.23.cloned.1.call-update) | async-done | bytes 16400 | tf_op jit(solution)/shard_map/reduce_scatter | solution.py:100
  311.1 2.0 multiply_reduce_fusion.3
  313.0 38.7 %all-reduce = (f32[]{:T(128)}, f32[]{:T(128)}) all-reduce(f32[]{:T(128)} %get-tuple-element.108, f32[]{:T(128)} %get-tuple-element.106), channel_id=1, replica_groups=mesh['period'=4,'row'=2,'col'=4] {'period','row','col'}, use_global_device_ids=true, to_apply=%region_17.19 | all-reduce | flops 2 | bytes 16 | tf_op jit(solution)/shard_map/psum | solution.py:112
  (117 shorter events, 48.9 us)
Async XLA Ops:
  7.2 19.6 %copy-start = (f32[1,1,1,32,128,128]{5,4,3,2,1,0:T(8,128)S(1)}, f32[1,1,1,32,128,128]{5,4,3,2,1,0:T(8,128)}, u32[]{:S(2)}) copy-start(f32[1,1,1,32,128,128]{5,4,3,2,1,0:T(8,128)} %param.36) | copy-start | bytes 6291460
  7.2 21.5 %copy-start.11 = (s32[1,1,1,32]{3,2,1,0:T(1,128)S(1)}, s32[1,1,1,32]{3,2,1,0:T(1,128)}, u32[]{:S(2)}) copy-start(s32[1,1,1,32]{3,2,1,0:T(1,128)} %param.38) | copy-start | bytes 388
  7.2 22.6 %copy-start.2 = (f32[64,128]{1,0:T(8,128)S(1)}, f32[64,128]{1,0:T(8,128)}, u32[]{:S(2)}) copy-start(f32[64,128]{1,0:T(8,128)} %param.31) | copy-start | bytes 98308
  7.2 23.2 %copy-start.4 = (f32[32,128]{1,0:T(8,128)S(1)}, f32[32,128]{1,0:T(8,128)}, u32[]{:S(2)}) copy-start(f32[32,128]{1,0:T(8,128)} %param.32) | copy-start | bytes 49156
  7.2 68.8 %copy-start.3 = (f32[64,128]{1,0:T(8,128)S(1)}, f32[64,128]{1,0:T(8,128)}, u32[]{:S(2)}) copy-start(f32[64,128]{1,0:T(8,128)} %param.33) | copy-start | bytes 98308
  7.2 68.8 %copy-start.6 = (f32[64,128]{1,0:T(8,128)S(1)}, f32[64,128]{1,0:T(8,128)}, u32[]{:S(2)}) copy-start(f32[64,128]{1,0:T(8,128)} %param.29) | copy-start | bytes 98308
  7.2 68.8 %copy-start.9 = (s32[64,128]{1,0:T(8,128)S(1)}, s32[64,128]{1,0:T(8,128)}, u32[]{:S(2)}) copy-start(s32[64,128]{1,0:T(8,128)} %param.34) | copy-start | bytes 98308
  7.2 66.8 %reduce-scatter.9.cloned.1.call-start = ((), (), s32[]{:S(2)}) async-start(), calls=%async_computation.8 | async-start | bytes 98304 | tf_op jit(solution)/shard_map/reduce_scatter | solution.py:85
  8.4 65.6 %collective-permute-start = (f32[1,128]{1,0:T(1,128)S(1)}, f32[1,128]{1,0:T(1,128)S(1)}, u32[]{:S(2)}, u32[]{:S(2)}) collective-permute-start(f32[1,128]{1,0:T(1,128)S(1)} %fusion.26), channel_id=1, source_target_pairs={{8,0},{16,8},{24,16},{9,1},{17,9},{25,17},{10,2},{18,10},{26,18},{... | collective-permute-start | bytes 1544 | tf_op jit(solution)/shard_map/ppermute | solution.py:18
  26.8 55.9 %copy-start.12 = (s32[1,1,1,32]{3,2,1,0:T(1,128)S(1)}, s32[1,1,1,32]{3,2,1,0:T(1,128)}, u32[]{:S(2)}) copy-start(s32[1,1,1,32]{3,2,1,0:T(1,128)} %param.37) | copy-start | bytes 388
  26.8 77.0 %copy-start.1 = (f32[1,1,1,128,128]{4,3,2,1,0:T(8,128)S(1)}, f32[1,1,1,128,128]{4,3,2,1,0:T(8,128)}, u32[]{:S(2)}) copy-start(f32[1,1,1,128,128]{4,3,2,1,0:T(8,128)} %param.39) | copy-start | bytes 196612
  26.8 79.1 %copy-start.5 = (f32[32,128]{1,0:T(8,128)S(1)}, f32[32,128]{1,0:T(8,128)}, u32[]{:S(2)}) copy-start(f32[32,128]{1,0:T(8,128)} %param.30) | copy-start | bytes 49156
  26.8 79.1 %copy-start.10 = (s32[32,128]{1,0:T(8,128)S(1)}, s32[32,128]{1,0:T(8,128)}, u32[]{:S(2)}) copy-start(s32[32,128]{1,0:T(8,128)} %param.35) | copy-start | bytes 49156
  29.7 74.1 %reduce-scatter.11.cloned.1.call-start = ((), (), s32[]{:S(2)}) async-start(), calls=%async_computation.9 | async-start | bytes 81920 | tf_op jit(solution)/shard_map/reduce_scatter | solution.py:100
  79.3 51.7 %copy-start.8 = (f32[64,128]{1,0:T(8,128)S(1)}, f32[64,128]{1,0:T(8,128)}, u32[]{:S(2)}) copy-start(f32[64,128]{1,0:T(8,128)} %scatter-add.26) | copy-start | bytes 98308
  83.7 45.4 %reduce-scatter.13.cloned.1.call-start = ((), (), s32[]{:S(2)}) async-start(), calls=%async_computation.10 | async-start | bytes 98304 | tf_op jit(solution)/shard_map/reduce_scatter | solution.py:85
  83.7 5.5 %collective-permute-start.1 = (f32[1,128]{1,0:T(1,128)S(1)}, f32[1,128]{1,0:T(1,128)S(1)}, u32[]{:S(2)}, u32[]{:S(2)}) collective-permute-start(f32[1,128]{1,0:T(1,128)S(1)} %slice.210), channel_id=1, source_target_pairs={{0,8},{8,16},{16,24},{1,9},{9,17},{17,25},{2,10},{10,18},{18,26},{... | collective-permute-start | bytes 1544 | tf_op jit(solution)/shard_map/ppermute | solution.py:18
  123.3 36.3 %reduce-scatter.15.cloned.1.call-start = ((), (), s32[]{:S(2)}) async-start(), calls=%async_computation.11 | async-start | bytes 81920 | tf_op jit(solution)/shard_map/reduce_scatter | solution.py:100
  123.5 5.4 %collective-permute-start.2 = (f32[1,128]{1,0:T(1,128)S(1)}, f32[1,128]{1,0:T(1,128)S(1)}, u32[]{:S(2)}, u32[]{:S(2)}) collective-permute-start(f32[1,128]{1,0:T(1,128)S(1)} %fusion.23), channel_id=1, source_target_pairs={{8,0},{16,8},{24,16},{9,1},{17,9},{25,17},{10,2},{18,10},{26,18},{... | collective-permute-start | bytes 1544 | tf_op jit(solution)/shard_map/ppermute | solution.py:18
  139.3 83.6 %reduce-scatter.17.cloned.1.call-start = ((), (), s32[]{:S(2)}) async-start(), calls=%async_computation.12 | async-start | bytes 98304 | tf_op jit(solution)/shard_map/reduce_scatter | solution.py:85
  139.3 5.4 %collective-permute-start.3 = (f32[1,128]{1,0:T(1,128)S(1)}, f32[1,128]{1,0:T(1,128)S(1)}, u32[]{:S(2)}, u32[]{:S(2)}) collective-permute-start(f32[1,128]{1,0:T(1,128)S(1)} %slice.214), channel_id=1, source_target_pairs={{0,8},{8,16},{16,24},{1,9},{9,17},{17,25},{2,10},{10,18},{18,26},{... | collective-permute-start | bytes 1544 | tf_op jit(solution)/shard_map/ppermute | solution.py:18
  179.9 72.6 %reduce-scatter.19.cloned.1.call-start = ((), (), s32[]{:S(2)}) async-start(), calls=%async_computation.13 | async-start | bytes 81920 | tf_op jit(solution)/shard_map/reduce_scatter | solution.py:100
  180.1 42.7 %collective-permute-start.4 = (f32[1,128]{1,0:T(1,128)S(1)}, f32[1,128]{1,0:T(1,128)S(1)}, u32[]{:S(2)}, u32[]{:S(2)}) collective-permute-start(f32[1,128]{1,0:T(1,128)S(1)} %fusion.20), channel_id=1, source_target_pairs={{8,0},{16,8},{24,16},{9,1},{17,9},{25,17},{10,2},{18,10},{26,18},{... | collective-permute-start | bytes 1544 | tf_op jit(solution)/shard_map/ppermute | solution.py:18
  228.1 51.7 %copy-start.7 = (f32[64,128]{1,0:T(8,128)S(1)}, f32[64,128]{1,0:T(8,128)}, u32[]{:S(2)}) copy-start(f32[64,128]{1,0:T(8,128)} %scatter-add.34) | copy-start | bytes 98308
  232.4 45.4 %reduce-scatter.21.cloned.1.call-start = ((), (), s32[]{:S(2)}) async-start(), calls=%async_computation.14 | async-start | bytes 98304 | tf_op jit(solution)/shard_map/reduce_scatter | solution.py:85
  232.5 5.5 %collective-permute-start.5 = (f32[1,128]{1,0:T(1,128)S(1)}, f32[1,128]{1,0:T(1,128)S(1)}, u32[]{:S(2)}, u32[]{:S(2)}) collective-permute-start(f32[1,128]{1,0:T(1,128)S(1)} %slice.218), channel_id=1, source_target_pairs={{0,8},{8,16},{16,24},{1,9},{9,17},{17,25},{2,10},{10,18},{18,26},{... | collective-permute-start | bytes 1544 | tf_op jit(solution)/shard_map/ppermute | solution.py:18
  271.9 37.0 %reduce-scatter.23.cloned.1.call-start = ((), (), s32[]{:S(2)}) async-start(), calls=%async_computation.15 | async-start | bytes 81920 | tf_op jit(solution)/shard_map/reduce_scatter | solution.py:100
  272.1 5.4 %collective-permute-start.6 = (f32[1,128]{1,0:T(1,128)S(1)}, f32[1,128]{1,0:T(1,128)S(1)}, u32[]{:S(2)}, u32[]{:S(2)}) collective-permute-start(f32[1,128]{1,0:T(1,128)S(1)} %fusion.17), channel_id=1, source_target_pairs={{8,0},{16,8},{24,16},{9,1},{17,9},{25,17},{10,2},{18,10},{26,18},{... | collective-permute-start | bytes 1544 | tf_op jit(solution)/shard_map/ppermute | solution.py:18
  288.6 5.4 %collective-permute-start.7 = (f32[1,128]{1,0:T(1,128)S(1)}, f32[1,128]{1,0:T(1,128)S(1)}, u32[]{:S(2)}, u32[]{:S(2)}) collective-permute-start(f32[1,128]{1,0:T(1,128)S(1)} %slice.222), channel_id=1, source_target_pairs={{0,8},{8,16},{16,24},{1,9},{9,17},{17,25},{2,10},{10,18},{18,26},{... | collective-permute-start | bytes 1544 | tf_op jit(solution)/shard_map/ppermute | solution.py:18
Sparse Core Ops, SparseCore 0:
  29.8 9.5 reduce-scatter.8
  83.8 19.9 reduce-scatter.10
  123.4 5.5 reduce-scatter.12
  139.4 20.1 reduce-scatter.14
  180.0 5.6 reduce-scatter.16
  232.5 19.9 reduce-scatter.18
  272.1 5.6 reduce-scatter.20
  288.7 20.1 reduce-scatter.22
where the time goes:
time: 363 us; the launch traced here: 361 us
  blocking collectives  182 us (50%)
  waiting for transfers between devices  72.7 us (20%)
  matrix products  33.4 us (9%)
  starting transfers between devices  22.1 us (6%)
  between operations  19.8 us (5%)
  other arithmetic  15.6 us (4%)
  local copies, waits for them, and re-layouts  15.1 us (4%)
    psum x2, blocking collectives, per_device(): lax.psum((jnp.sum(primal_moved * primal_moved), jnp.sum(dual_moved * dual...  78.6 us
    reduce_scatter x4, waiting for transfers between devices, per_device(): lax.psum_scatter(forward_partial_value, 'col', scatter_dimension=0, tiled...  58.9 us
    all_gather x4, blocking collectives, per_device(): rows_all = lax.all_gather(dual, 'col', axis=0, tiled=True)  54.6 us
    psum x1, blocking collectives, per_device(): lax.psum((jnp.sum(objective * objective), jnp.sum(right_side * right_side...  41.6 us
    ppermute x8, starting transfers between devices, shifted(): return lax.ppermute(x, axis, pairs)  21.8 us
    dot_general x4, matrix products, per_device(): jnp.einsum('nij,nj->ni', tiles_here, forward_picked, precision=HIGHEST_MODE)  13.4 us
    ppermute x8, waiting for transfers between devices, shifted(): return lax.ppermute(x, axis, pairs)  13.4 us
    dot_general x4, matrix products, per_device(): jnp.einsum('nij,ni->nj', tiles_here, picked, precision=HIGHEST_MODE)  7.47 us
  transfers between devices with their start and end apart: 16, of which 12 were waited for; matrix products, arithmetic and copies ran while one was open for 2% of the time, Pallas kernels for 0%

commit v1 on v0

v1 whole, which is shorter than its diff:
```python
import functools
import jax
import jax.numpy as jnp
from jax import lax
from jax.experimental import pallas as pl
from jax.experimental.pallas import tpu as pltpu
from jax.sharding import PartitionSpec as P

ROUNDS = 2
INNER = 2
STEP_SCALE = 0.15
EPSILON = 1e-06
F32 = jnp.float32
BF16 = jnp.bfloat16


def up(n, m):
    return -(-n // m) * m


def peer(me, j, n):
    return me ^ j if n & (n - 1) == 0 else lax.rem(me + j, n)


def from_peer(x, axis, j):
    n = lax.axis_size(axis)
    pairs = [((i ^ j) if n & (n - 1) == 0 else (i + j) % n, i) for i in range(n)]
    return lax.ppermute(x, axis, pairs)


def exchange(x, axis):
    return [x] + [from_peer(x, axis, j) for j in range(1, lax.axis_size(axis))]


def period_exchange(x, all_of_them):
    n = lax.axis_size("period")
    if n % 2 == 0 and n > 2:
        even = {i: i ^ 1 for i in range(n)}
        odd = {i: ((i - 1) if i % 2 == 0 else (i + 1)) % n for i in range(n)}
        got = [lax.ppermute(x, "period", [(m[i], i) for i in range(n)]) for m in (even, odd)]
    else:
        got = [lax.ppermute(x, "period", [((i + s) % n, i) for i in range(n)]) for s in (1, n - 1)]
    if all_of_them:
        got += [
            lax.ppermute(x, "period", [((i + s) % n, i) for i in range(n)]) for s in range(2, n - 1)
        ]
    return got


def next_and_previous(first, second, size, me):
    if size % 2 == 0 and size > 2:
        is_even = lax.rem(me, 2) == 0
        return jnp.where(is_even, first, second), jnp.where(is_even, second, first)
    return first, second


def exact_dot(chosen, values):
    head = values.astype(BF16)
    rest = values - head.astype(F32)
    middle = rest.astype(BF16)
    tail = (rest - middle.astype(F32)).astype(BF16)
    dot = functools.partial(jnp.dot, preferred_element_type=F32)
    return dot(chosen, head) + (dot(chosen, middle) + dot(chosen, tail))


def onehot(lists, first, count, height):
    spots = lax.broadcasted_iota(jnp.int32, (height, count), 0).astype(F32)
    return jnp.where(spots == lists[:, first : first + count], 1.0, 0.0).astype(BF16)


def total(x):
    return jnp.sum(jnp.sum(x, axis=0, keepdims=True), axis=1, keepdims=True)


class Sizes:
    def __init__(self, mesh_period, mesh_row, mesh_col, tile, listed, col_share, row_share):
        self.np, self.nr, self.nc = mesh_period, mesh_row, mesh_col
        self.tile, self.nt = tile, listed
        self.cs, self.rs = col_share, row_share
        self.cols, self.rows = col_share * mesh_row, row_share * mesh_col
        self.listed = self.nr * self.nt
        self.products = self.listed + self.nr
        self.blocks = -(-self.products // tile)
        self.zrows = up(self.products + 1, 8)
        self.ghosts = up(self.nr, 8)
        self.xrows = self.cols + self.ghosts
        self.hop = up(2 * self.nr + 2, 8)
        self.hop_first = self.hop + up(4 * self.nr, 8)
        self.group = tile // self.nt
        self.row_lists = -(-self.nc // self.group)
        self.setup = 3 * self.rows + up(self.row_lists + 2, 8)
        self.limit = (self.nr * listed * tile * tile * 4 * 3) // 2 + (10 << 20)


def prepare_kernel(z, dual, rhs, rkind, x, obj, ub, ckind, rlist, clist, zmsg, xmsg):
    rs, cs = z.rs, z.cs
    zmsg[0:rs, :] = dual[...]
    zmsg[rs : 2 * rs, :] = rhs[...]
    zmsg[2 * rs : 3 * rs, :] = jnp.where(rkind[...] == 0, 0.0, -jnp.inf)
    zmsg[3 * rs : 3 * rs + 8, :] = jnp.zeros((8, z.tile), F32)
    zmsg[3 * rs : 3 * rs + 1, :] = rlist[...].astype(F32)
    ones = jnp.ones((1, z.tile), F32)
    zmsg[3 * rs + 1 : 3 * rs + 2, :] = total(obj[...] * obj[...]) * ones
    zmsg[3 * rs + 2 : 3 * rs + 3, :] = total(rhs[...] * rhs[...]) * ones
    kind = ckind[...]
    xmsg[0:cs, :] = x[...]
    xmsg[cs : 2 * cs, :] = obj[...]
    xmsg[2 * cs : 3 * cs, :] = jnp.where(kind == 2, -jnp.inf, 0.0)
    xmsg[3 * cs : 4 * cs, :] = jnp.where(kind == 1, ub[...], jnp.inf)
    xmsg[4 * cs : 4 * cs + 8, :] = jnp.broadcast_to(clist[...].astype(F32), (8, z.tile))


def assemble_kernel(z, *refs):
    slots, out = refs[:-1], refs[-1]
    me = lax.axis_index("col")
    lane = lax.broadcasted_iota(jnp.int32, (1, z.tile), 1)
    base = 3 * z.rows
    out[base:, :] = jnp.zeros((z.setup - base, z.tile), F32)
    sums = jnp.zeros((2, z.tile), F32)
    lists = [jnp.zeros((1, z.tile), F32) for _ in range(z.row_lists)]
    for d, slot in enumerate(slots):
        at = peer(me, d, z.nc) * z.rs
        for part in range(3):
            spot = pl.ds(pl.multiple_of(part * z.rows + at, z.rs), z.rs)
            out[spot, :] = slot[part * z.rs : (part + 1) * z.rs, :]
        mine = lane // z.nt == d % z.group
        q = d // z.group
        lists[q] = jnp.where(mine, slot[3 * z.rs : 3 * z.rs + 1, :], lists[q])
        sums = sums + slot[3 * z.rs + 1 : 3 * z.rs + 3, :]
    for q in range(z.row_lists):
        out[base + q : base + q + 1, :] = lists[q]
    out[base + z.row_lists : base + z.row_lists + 2, :] = sums


def transposed_products(z, y_at, rlists, tiles, links, picked):
    me = lax.axis_index("col")
    picked[...] = jnp.zeros_like(picked)
    for j in range(z.nr):
        for n in range(z.nt):
            k = j * z.nt + n
            picked[k : k + 1, :] = y_at[pl.ds(j * z.rows + rlists[j, n], 1), :]
        k = z.listed + j
        picked[k : k + 1, :] = y_at[pl.ds(j * z.rows + me * z.rs, 1), :]
    turned = [picked[b * z.tile : (b + 1) * z.tile, :].T for b in range(z.blocks)]
    for k in range(z.products):
        if k < z.listed:
            tile = tiles[k // z.nt][k % z.nt]
        else:
            tile = links[k - z.listed][...]
        column = turned[k // z.tile][:, k % z.tile : k % z.tile + 1]
        picked[k : k + 1, :] = jnp.sum(tile * column, axis=0, keepdims=True)


def gradient_part(z, products, clists, g, msg, sums):
    row = lax.axis_index("row")
    full = jnp.zeros((z.cols, z.tile), F32)
    for q in range(-(-z.listed // z.tile)):
        count = min(z.tile, z.listed - q * z.tile)
        lane = lax.broadcasted_iota(jnp.int32, (1, z.tile), 1)
        lists = jnp.zeros((1, z.tile), F32)
        for i in range(count // z.nt):
            lists = jnp.where(lane // z.nt == i, clists[q * z.group + i][0:1, :], lists)
        chosen = onehot(lists, 0, count, z.cols)
        full = full + exact_dot(chosen, products[q * z.tile : q * z.tile + count, :])
    g[0 : z.cols, :] = full
    g[z.cols :, :] = jnp.zeros((z.ghosts, z.tile), F32)
    msg[...] = jnp.zeros_like(msg)
    for j in range(z.nr):
        outflow = products[z.listed + j : z.listed + j + 1, :]
        g[z.cols + j : z.cols + j + 1, :] = outflow
        msg[j : j + 1, :] = outflow
        last = peer(row, j, z.nr) * z.cs + z.cs - 1
        msg[z.nr + j : z.nr + j + 1, :] = g[pl.ds(last, 1), :]
    for i, value in enumerate(sums):
        msg[2 * z.nr + i : 2 * z.nr + i + 1, :] = value


def first_kernel(z, *refs):
    rlists, refs = refs[0], refs[1:]
    shared, refs = refs[: z.nr], refs[z.nr :]
    halves, refs = refs[: z.nr], refs[z.nr :]
    tiles, refs = refs[: z.nr], refs[z.nr :]
    links, refs = refs[: z.nr], refs[z.nr :]
    y, xs, g, msg, picked = refs
    row = lax.axis_index("row")
    for j in range(z.nr):
        y[j * z.rows : (j + 1) * z.rows, :] = shared[j][0 : z.rows, :]
        at = peer(row, j, z.nr) * z.cs
        for part in range(4):
            spot = pl.ds(pl.multiple_of(part * z.xrows + at, 8), z.cs)
            xs[spot, :] = halves[j][part * z.cs : (part + 1) * z.cs, :]
    transposed_products(z, y, rlists, tiles, links, picked)
    base = 3 * z.rows + z.row_lists
    sums = [sum(s[base + i : base + i + 1, :] for s in shared) for i in range(2)]
    gradient_part(
        z, picked, [h.at[4 * z.cs : 4 * z.cs + 8, :] for h in halves], g, msg, sums
    )
    for part in range(4):
        xs[part * z.xrows + z.cols : (part + 1) * z.xrows, :] = jnp.zeros((z.ghosts, z.tile), F32)
        for j in range(z.nr):
            to = z.hop + part * z.nr + j
            msg[to : to + 1, :] = halves[j][(part + 1) * z.cs - 1 : (part + 1) * z.cs, :]


def dual_part(z, w, slots, shared, y_old, y_out):
    me = lax.axis_index("col")
    sigma = STEP_SCALE * w[0:1, :]
    for j in range(z.nr):
        summed = jnp.zeros((z.rows, z.tile), F32)
        for q in range(z.row_lists):
            ds = range(q * z.group, min((q + 1) * z.group, z.nc))
            lists = shared[j][3 * z.rows + q : 3 * z.rows + q + 1, :]
            chosen = onehot(lists, 0, len(ds) * z.nt, z.rows)
            parts = [slots[d][j * z.nt : (j + 1) * z.nt, :] for d in ds]
            summed = summed + exact_dot(chosen, jnp.concatenate(parts, axis=0))
        spot = slice(j * z.rows, (j + 1) * z.rows)
        y_out[spot, :] = summed
        for d in range(z.nc):
            at = pl.ds(j * z.rows + peer(me, d, z.nc) * z.rs, 1)
            y_out[at, :] = y_out[at, :] + slots[d][z.listed + j : z.listed + j + 1, :]
        moved = y_old[spot, :] + sigma * (shared[j][z.rows : 2 * z.rows, :] - y_out[spot, :])
        y_out[spot, :] = jnp.maximum(moved, shared[j][2 * z.rows : 3 * z.rows, :])


def mean_and_move(now, before, begin):
    mean = (now + before) * (1.0 / INNER)
    return mean, total((mean - begin) * (mean - begin))


def dual_kernel(z, ends, *refs):
    rlists, w, refs = refs[0], refs[1], refs[2:]
    slots, refs = refs[: z.nc], refs[z.nc :]
    shared, refs = refs[: z.nr], refs[z.nr :]
    halves, refs = refs[: z.nr], refs[z.nr :]
    tiles, refs = refs[: z.nr], refs[z.nr :]
    links, refs = refs[: z.nr], refs[z.nr :]
    y_old = refs[0]
    y_begin = refs[1] if ends else None
    y_out, g, msg, picked = refs[-4:]
    dual_part(z, w, slots, shared, y_old, y_out)
    sums = []
    if ends:
        mean, move = mean_and_move(y_out[...], y_old[...], y_begin[...])
        y_out[...] = mean
        moved = sum(s[z.products : z.products + 1, :] for s in slots)
        sums = [moved, move * jnp.ones((1, z.tile), F32)]
    transposed_products(z, y_out, rlists, tiles, links, picked)
    gradient_part(
        z, picked, [h.at[4 * z.cs : 4 * z.cs + 8, :] for h in halves], g, msg, sums
    )


def last_kernel(z, *refs):
    w, refs = refs[0], refs[1:]
    slots, refs = refs[: z.nc], refs[z.nc :]
    shared, refs = refs[: z.nr], refs[z.nr :]
    y_old, y_begin, out, msg, y_new = refs
    dual_part(z, w, slots, shared, y_old, y_new)
    mean, move = mean_and_move(y_new[...], y_old[...], y_begin[...])
    y_new[...] = mean
    me = lax.axis_index("col")
    out[...] = y_new[pl.ds(pl.multiple_of(me * z.rs, z.rs), z.rs), :]
    msg[...] = jnp.zeros_like(msg)
    msg[0:1, :] = sum(s[z.products : z.products + 1, :] for s in slots)
    msg[1:2, :] = move * jnp.ones((1, z.tile), F32)


def weight_kernel(z, *refs):
    w, msgs, out = refs[0], refs[1:-1], refs[-1]
    dx = sum(m[0:1, :] for m in msgs)
    dy = sum(m[1:2, :] for m in msgs)
    new = jnp.sqrt(w[0:1, :] * jnp.sqrt((dx + EPSILON) / (dy + EPSILON)))
    out[...] = jnp.broadcast_to(new, out.shape)


def primal_kernel(z, starts, first, ends, last, *refs):
    clists, refs = refs[0], refs[1:]
    w_old, refs = (None, refs) if first else (refs[0], refs[1:])
    g, own, refs = refs[0], refs[1], refs[2:]
    count = (z.np - 1) if starts else 2
    got, refs = refs[:count], refs[count:]
    xs, refs = refs[0], refs[1:]
    x_old, refs = (None, refs) if first else (refs[0], refs[1:])
    x_begin, refs = (refs[0], refs[1:]) if ends else (None, refs)
    tiles, refs = refs[: z.nr], refs[z.nr :]
    links, refs = refs[: z.nr], refs[z.nr :]
    x_out, zmsg, refs = refs[0], refs[1], refs[2:]
    w_out, refs = (refs[0], refs[1:]) if starts else (None, refs)
    xs_out, refs = (refs[0], refs[1:]) if first else (None, refs)
    work, v = refs
    period, row = lax.axis_index("period"), lax.axis_index("row")

    if starts:
        s1 = own[2 * z.nr : 2 * z.nr + 1, :]
        s2 = own[2 * z.nr + 1 : 2 * z.nr + 2, :]
        for m in got:
            s1 = s1 + m[2 * z.nr : 2 * z.nr + 1, :]
            s2 = s2 + m[2 * z.nr + 1 : 2 * z.nr + 2, :]
        ratio = (s1 + EPSILON) / (s2 + EPSILON)
        weight = jnp.sqrt(ratio) if first else jnp.sqrt(w_old[0:1, :] * jnp.sqrt(ratio))
        w_out[...] = jnp.broadcast_to(weight, w_out.shape)
    else:
        weight = w_old[0:1, :]
    tau = STEP_SCALE / weight

    after, before = next_and_previous(got[0][...], got[1][...], z.np, period)
    has_next = period < z.np - 1
    has_previous = period > 0
    work[...] = g[...]
    for j in range(z.nr):
        last_row = pl.ds(peer(row, j, z.nr) * z.cs + z.cs - 1, 1)
        outflow = jnp.where(has_next, after[j : j + 1, :], 0.0)
        work[last_row, :] = work[last_row, :] + outflow
        ghost = slice(z.cols + j, z.cols + j + 1)
        work[ghost, :] = work[ghost, :] + before[z.nr + j : z.nr + j + 1, :]
    if first:
        xs_out[...] = xs[...]
        for part in range(4):
            for j in range(z.nr):
                to = part * z.xrows + z.cols + j
                at = z.hop + part * z.nr + j
                xs_out[to : to + 1, :] = before[at : at + 1, :]
        data = xs_out
        x_now = xs_out[0 : z.xrows, :]
    else:
        data = xs
        x_now = x_old[...]
    obj = data[z.xrows : 2 * z.xrows, :]
    low = data[2 * z.xrows : 3 * z.xrows, :]
    high = data[3 * z.xrows : 4 * z.xrows, :]
    x_new = jnp.minimum(jnp.maximum(x_now - tau * (obj - work[...]), low), high)
    v[...] = 2.0 * x_new - x_now
    v[z.cols :, :] = jnp.where(has_previous, v[z.cols :, :], 0.0)
    move = None
    if ends:
        mean = (x_new + x_now) * (1.0 / INNER)
        moved = mean[0 : z.cols, :] - x_begin[0 : z.cols, :]
        move = total(moved * moved)
        if last:
            work[...] = mean
            x_out[...] = work[pl.ds(pl.multiple_of(row * z.cs, z.cs), z.cs), :]
        else:
            x_out[...] = mean
    else:
        x_out[...] = x_new

    lane = lax.broadcasted_iota(jnp.int32, (z.tile, z.tile), 1)
    for b in range(z.blocks):
        columns = jnp.zeros((z.tile, z.tile), F32)
        for k in range(b * z.tile, min((b + 1) * z.tile, z.products)):
            if k < z.listed:
                tile = tiles[k // z.nt][k % z.nt]
                vector = v[pl.ds(clists[k // z.nt, k % z.nt], 1), :]
            else:
                tile = links[k - z.listed][...]
                vector = v[z.cols + k - z.listed : z.cols + k - z.listed + 1, :]
            column = jnp.sum(tile * vector, axis=1, keepdims=True)
            columns = jnp.where(lane == k % z.tile, column, columns)
        rows = min(z.zrows - b * z.tile, z.tile)
        zmsg[b * z.tile : b * z.tile + rows, :] = columns.T[0:rows, :]
    if ends:
        zmsg[z.products : z.products + 1, :] = move * jnp.ones((1, z.tile), F32)


def call(z, kernel, operands, shapes, scratch=(), smem=0):
    spaces = [pltpu.SMEM] * smem + [pltpu.VMEM] * (len(operands) - smem)
    return pl.pallas_call(
        kernel,
        out_shape=[jax.ShapeDtypeStruct(s, F32) for s in shapes],
        in_specs=[pl.BlockSpec(memory_space=s) for s in spaces],
        out_specs=[pl.BlockSpec(memory_space=pltpu.VMEM) for _ in shapes],
        scratch_shapes=[pltpu.VMEM(s, F32) for s in scratch],
        compiler_params=pltpu.CompilerParams(vmem_limit_bytes=z.limit),
    )(*operands)


def per_device(
    primal_start,
    dual_start,
    objective,
    right_side,
    upper_bound,
    column_kind,
    row_kind,
    tile_values,
    tile_rows,
    tile_cols,
    coupling,
):
    tile = tile_values.shape[-1]
    listed = tile_values.shape[3]
    z = Sizes(
        lax.axis_size("period"),
        lax.axis_size("row"),
        lax.axis_size("col"),
        tile,
        listed,
        primal_start.shape[0],
        dual_start.shape[0],
    )
    part = functools.partial
    line = lambda rows: (rows, tile)
    row_list = tile_rows.reshape(1, listed)
    col_list = tile_cols.reshape(1, listed)
    tiles = exchange(tile_values.reshape(listed, tile, tile), "row")
    links = exchange(coupling.reshape(tile, tile), "row")
    both = jnp.concatenate([row_list, col_list], axis=0)
    lists = exchange(both, "row")
    rlists = jnp.concatenate([b[0:1] for b in lists], axis=0)
    clists = jnp.concatenate([b[1:2] for b in lists], axis=0)

    zmsg, xmsg = call(
        z,
        part(prepare_kernel, z),
        (
            dual_start,
            right_side,
            row_kind,
            primal_start,
            objective,
            upper_bound,
            column_kind,
            jnp.tile(row_list, (1, z.group)),
            jnp.tile(col_list, (1, z.group)),
        ),
        [line(3 * z.rs + 8), line(4 * z.cs + 8)],
    )
    slots = exchange(zmsg, "col")
    halves = exchange(xmsg, "row")
    (gathered,) = call(z, part(assemble_kernel, z), slots, [line(z.setup)])
    shared = exchange(gathered, "row")

    picked = line(z.blocks * tile)
    y, xs, g, msg = call(
        z,
        part(first_kernel, z),
        (rlists, *shared, *halves, *tiles, *links),
        [line(z.nr * z.rows), line(4 * z.xrows), line(z.xrows), line(z.hop_first)],
        [picked],
        smem=1,
    )
    x = None
    weight = None
    y_begin, x_begin = y, None
    for step in range(ROUNDS * INNER):
        starts = step % INNER == 0
        ends = step % INNER == INNER - 1
        first, last = step == 0, step == ROUNDS * INNER - 1
        got = period_exchange(msg, starts)
        operands = [clists] + ([] if first else [weight]) + [g, msg, *got, xs]
        operands += ([] if first else [x]) + ([x_begin] if ends else []) + [*tiles, *links]
        shapes = [line(z.cs if last else z.xrows), line(z.zrows)]
        shapes += ([line(8)] if starts else []) + ([line(4 * z.xrows)] if first else [])
        outs = call(
            z,
            part(primal_kernel, z, starts, first, ends, last),
            operands,
            shapes,
            [line(z.xrows), line(z.xrows)],
            smem=1,
        )
        x_next, zmsg = outs[:2]
        if starts:
            weight = outs[2]
        if first:
            xs = outs[3]
            x = xs[0 : z.xrows]
        if starts:
            x_begin = x
        x = x_next
        slots = exchange(zmsg, "col")
        if last:
            break
        operands = [rlists, weight, *slots, *shared, *halves, *tiles, *links, y]
        y_next, g, msg = call(
            z,
            part(dual_kernel, z, ends),
            operands + ([y_begin] if ends else []),
            [line(z.nr * z.rows), line(z.xrows), line(z.hop)],
            [picked],
            smem=1,
        )
        y = y_next
        if ends:
            y_begin = y
    dual, sums = call(
        z,
        part(last_kernel, z),
        (weight, *slots, *shared, y, y_begin),
        [line(z.rs), line(8)],
        [line(z.nr * z.rows)],
    )
    (final,) = call(
        z,
        part(weight_kernel, z),
        (weight, sums, *period_exchange(sums, True)),
        [line(8)],
    )
    return (x, dual, final[0, 0])


def solution(mesh):
    in_specs = (
        P(("period", "row"), "col"),
        P(("period", "col"), "row"),
        P(("period", "row"), "col"),
        P(("period", "col"), "row"),
        P(("period", "row"), "col"),
        P(("period", "row"), "col"),
        P(("period", "col"), "row"),
        P("period", "row", "col", None, None, None),
        P("period", "row", "col", None),
        P("period", "row", "col", None),
        P("period", "row", "col", None, None),
    )
    out_specs = (P(("period", "row"), "col"), P(("period", "col"), "row"), P())
    return jax.shard_map(
        per_device, mesh=mesh, in_specs=in_specs, out_specs=out_specs, check_vma=False
    )
```

time: 363 us -> 99.5 us (0.27)
  blocking collectives: 182 us -> 0 us
  waiting for transfers between devices: 72.7 us -> 28.6 us
  matrix products: 33.4 us -> 0 us
  between operations: 19.8 us -> 0.73 us
  Pallas kernels: 0 us -> 18.8 us
  starting transfers between devices: 22.1 us -> 39.8 us
  other arithmetic: 15.6 us -> 1.36 us
  local copies, waits for them, and re-layouts: 15.1 us -> 9.64 us
    psum x3 -> x0, blocking collectives: 120 us -> none  [the longest x2 78.6 us: per_device(): lax.psum((jnp.sum(primal_moved * primal_moved), jnp.sum(dual_moved * dual...]
    all_gather x8 -> x0, blocking collectives: 62 us -> none  [the longest x4 54.6 us: per_device(): rows_all = lax.all_gather(dual, 'col', axis=0, tiled=True)]
    reduce_scatter x8 -> x0, waiting for transfers between devices: 59.2 us -> none  [the longest x4 58.9 us: per_device(): lax.psum_scatter(forward_partial_value, 'col', scatter_dimension=0, tiled...]
    dot_general x24 -> x0, matrix products: 33.4 us -> none  [the longest x4 13.4 us: per_device(): jnp.einsum('nij,nj->ni', tiles_here, forward_picked, precision=HIGHEST_MODE)]
    pallas_call x0 -> x12, Pallas kernels: none -> 18.8 us  [call(): pl.pallas_call(kernel, out_shape=[jax.ShapeDtypeStruct(s, F32) for s in s...]
    ppermute x8 -> x33, starting transfers between devices: 21.8 us -> 39.8 us  [the longest x20 24.1 us: from_peer(): return lax.ppermute(x, axis, pairs)]
    ppermute x8 -> x33, waiting for transfers between devices: 13.4 us -> 28.6 us  [the longest x20 15.1 us: from_peer(): return lax.ppermute(x, axis, pairs)]
    scatter-add x8 -> x0, local copies, waits for them, and re-layouts: 10.4 us -> none  [the longest x4 5.28 us: per_device(): residual = rhs_block - forward_summed.at[0:1].add(inflow)]
  transfers between devices with their start and end apart: 16 -> 33, of which waited for: 12 -> 24; matrix products, arithmetic and copies ran while one was open for 2% -> 3% of each run, Pallas kernels for 0% -> 0%
where the time goes in v1:
time: 99.5 us; the launch traced here: 98.9 us
  starting transfers between devices  39.8 us (40%)
  waiting for transfers between devices  28.6 us (29%)
  Pallas kernels  18.8 us (19%)
  local copies, waits for them, and re-layouts  9.64 us (10%)
  other arithmetic  1.36 us (1%)
    ppermute x20, starting transfers between devices, from_peer(): return lax.ppermute(x, axis, pairs)  24.1 us
    pallas_call x12, Pallas kernels, call(): pl.pallas_call(kernel, out_shape=[jax.ShapeDtypeStruct(s, F32) for s in s...  18.8 us
    ppermute x20, waiting for transfers between devices, from_peer(): return lax.ppermute(x, axis, pairs)  15.1 us
    ppermute x10, waiting for transfers between devices, period_exchange(): lax.ppermute(x, 'period', [(m[i], i) for i in range(n)])  13.1 us
    ppermute x10, starting transfers between devices, period_exchange(): lax.ppermute(x, 'period', [(m[i], i) for i in range(n)])  12 us
    unnamed x24, local copies, waits for them, and re-layouts  7.62 us
    ppermute x3, starting transfers between devices, period_exchange(): lax.ppermute(x, 'period', [((i + s) % n, i) for i in range(n)])  3.69 us
  transfers between devices with their start and end apart: 33, of which 24 were waited for; matrix products, arithmetic and copies ran while one was open for 3% of the time, Pallas kernels for 0%

profile of v1, /device:TPU:0, one launch (start us, length us, event | category | flops | bytes accessed | tf_op | source)
XLA Modules:
  0.0 98.9 jit_solution(17800682569312648986)
XLA Ops:
  7.9 4.6 %collective-permute-start.3 = (f32[104,128]{1,0:T(8,128)S(1)}, f32[104,128]{1,0:T(8,128)S(1)}, u32[]{:S(2)}, u32[]{:S(2)}) collective-permute-start(f32[104,128]{1,0:T(8,128)S(1)} %get-tuple-element.31.refs_0_), channel_id=1, source_target_pairs={{3,0},{2,1},{1,2},{0,3},{7,4},{6,5},{5,6},{4,7},{11,8},{10,9},{9,1... | collective-permute-start | bytes 159752 | tf_op jit(solution)/shard_map/ppermute | solution.py:28
  15.1 2.7 %collective-permute-done.2.refs_2_ = f32[104,128]{1,0:T(8,128)S(1)} collective-permute-done((f32[104,128]{1,0:T(8,128)S(1)}, f32[104,128]{1,0:T(8,128)S(1)}, u32[]{:S(2)}, u32[]{:S(2)}) %collective-permute-start.2) | collective-permute-done | bytes 53280 | tf_op jit(solution)/shard_map/ppermute | solution.py:28
  19.5 1.6 %copy-done = f32[1,1,1,32,128,128]{5,4,3,2,1,0:T(8,128)S(1)} copy-done((f32[1,1,1,32,128,128]{5,4,3,2,1,0:T(8,128)S(1)}, f32[1,1,1,32,128,128]{5,4,3,2,1,0:T(8,128)}, u32[]{:S(2)}) %copy-start) | copy-done | bytes 2097176
  21.9 2.2 %shard_map.132 = (f32[256,128]{1,0:T(8,128)S(1)}, f32[544,128]{1,0:T(8,128)S(1)}, f32[136,128]{1,0:T(8,128)S(1)}, f32[16,128]{1,0:T(8,128)S(1)}) custom-call(s32[2,32]{1,0:T(2,128)S(1)} %pad_add_fusion.refs_0_, f32[392,128]{1,0:T(8,128)S(1)} %shard_map.131.refs_1_.refs_6_.refs_5_, f32[392,128]{1,0:T(8,128)S(1)} %collective-permute-done.4.refs_2_.refs_7_.refs_6_, ...), custom_call_target="tpu_custom_call" | custom-call | tf_op jit(solution)/shard_map/pallas_call | solution.py:367
  24.1 1.6 %collective-permute-start.10 = (f32[16,128]{1,0:T(8,128)S(1)}, f32[16,128]{1,0:T(8,128)S(1)}, u32[]{:S(2)}, u32[]{:S(2)}) collective-permute-start(f32[16,128]{1,0:T(8,128)S(1)} %get-tuple-element.34.refs_2_), channel_id=1, source_target_pairs={{16,0},{24,8},{0,16},{8,24},{17,1},{25,9},{1,17},{9,25},{18,2},{26... | collective-permute-start | bytes 24584 | tf_op jit(solution)/shard_map/ppermute | solution.py:45
  25.7 1.4 %collective-permute-start.9 = (f32[16,128]{1,0:T(8,128)S(1)}, f32[16,128]{1,0:T(8,128)S(1)}, u32[]{:S(2)}, u32[]{:S(2)}) collective-permute-start(f32[16,128]{1,0:T(8,128)S(1)} %get-tuple-element.34.refs_2_), channel_id=1, source_target_pairs={{24,0},{16,8},{8,16},{0,24},{25,1},{17,9},{9,17},{1,25},{26,2},{18... | collective-permute-start | bytes 24584 | tf_op jit(solution)/shard_map/ppermute | solution.py:40
  27.8 2.4 %collective-permute-done.9.refs_4_ = f32[16,128]{1,0:T(8,128)S(1)} collective-permute-done((f32[16,128]{1,0:T(8,128)S(1)}, f32[16,128]{1,0:T(8,128)S(1)}, u32[]{:S(2)}, u32[]{:S(2)}) %collective-permute-start.9) | collective-permute-done | bytes 8224 | tf_op jit(solution)/shard_map/ppermute | solution.py:40
  30.8 1.8 %shard_map.133 = (f32[136,128]{1,0:T(8,128)S(1)}, f32[72,128]{1,0:T(8,128)S(1)}, f32[8,128]{1,0:T(8,128)S(1)}, f32[544,128]{1,0:T(8,128)S(1)}) custom-call(s32[2,32]{1,0:T(2,128)S(1)} %pad_add_fusion.2.refs_0_, f32[136,128]{1,0:T(8,128)S(1)} %get-tuple-element.33.refs_1_, f32[16,128]{1,0:T(8,128)S(1)} %get-tuple-element.34.refs_2_, ...), custom_call_target="tpu_custom_call" | custom-call | tf_op jit(solution)/shard_map/pallas_call | solution.py:367
  32.6 2.3 %collective-permute-start.13 = (f32[72,128]{1,0:T(8,128)S(1)}, f32[72,128]{1,0:T(8,128)S(1)}, u32[]{:S(2)}, u32[]{:S(2)}) collective-permute-start(f32[72,128]{1,0:T(8,128)S(1)} %get-tuple-element.37.refs_2_), channel_id=1, source_target_pairs={{3,0},{2,1},{1,2},{0,3},{7,4},{6,5},{5,6},{4,7},{11,8},{10,9},{9,1... | collective-permute-start | bytes 110600 | tf_op jit(solution)/shard_map/ppermute | solution.py:28
  35.3 1.8 %collective-permute-start.11 = (f32[72,128]{1,0:T(8,128)S(1)}, f32[72,128]{1,0:T(8,128)S(1)}, u32[]{:S(2)}, u32[]{:S(2)}) collective-permute-start(f32[72,128]{1,0:T(8,128)S(1)} %get-tuple-element.37.refs_2_), channel_id=1, source_target_pairs={{1,0},{0,1},{3,2},{2,3},{5,4},{4,5},{7,6},{6,7},{9,8},{8,9},{11,10... | collective-permute-start | bytes 110600 | tf_op jit(solution)/shard_map/ppermute | solution.py:28
  37.1 1.6 %collective-permute-done.13.refs_5_ = f32[72,128]{1,0:T(8,128)S(1)} collective-permute-done((f32[72,128]{1,0:T(8,128)S(1)}, f32[72,128]{1,0:T(8,128)S(1)}, u32[]{:S(2)}, u32[]{:S(2)}) %collective-permute-start.13) | collective-permute-done | bytes 36896 | tf_op jit(solution)/shard_map/ppermute | solution.py:28
  39.8 2.5 %shard_map.134 = (f32[256,128]{1,0:T(8,128)S(1)}, f32[136,128]{1,0:T(8,128)S(1)}, f32[8,128]{1,0:T(8,128)S(1)}) custom-call(s32[2,32]{1,0:T(2,128)S(1)} %pad_add_fusion.refs_0_, f32[8,128]{1,0:T(8,128)S(1)} %get-tuple-element.36.refs_1_, f32[72,128]{1,0:T(8,128)S(1)} %get-tuple-element.37.refs_2_, f32[72,128]{1,0:T(8,128)S(1)} %collective-permute-done.11.refs_3_, ...), custom_call_target="tpu_custom_call" | custom-call | tf_op jit(solution)/shard_map/pallas_call | solution.py:367
  42.3 1.6 %collective-permute-start.15 = (f32[8,128]{1,0:T(8,128)S(1)}, f32[8,128]{1,0:T(8,128)S(1)}, u32[]{:S(2)}, u32[]{:S(2)}) collective-permute-start(f32[8,128]{1,0:T(8,128)S(1)} %get-tuple-element.40.refs_3_), channel_id=1, source_target_pairs={{24,0},{16,8},{8,16},{0,24},{25,1},{17,9},{9,17},{1,25},{26,2},{18... | collective-permute-start | bytes 12296 | tf_op jit(solution)/shard_map/ppermute | solution.py:40
  43.8 1.5 %collective-permute-start.14 = (f32[8,128]{1,0:T(8,128)S(1)}, f32[8,128]{1,0:T(8,128)S(1)}, u32[]{:S(2)}, u32[]{:S(2)}) collective-permute-start(f32[8,128]{1,0:T(8,128)S(1)} %get-tuple-element.40.refs_3_), channel_id=1, source_target_pairs={{8,0},{0,8},{24,16},{16,24},{9,1},{1,9},{25,17},{17,25},{10,2},{2,... | collective-permute-start | bytes 12296 | tf_op jit(solution)/shard_map/ppermute | solution.py:40
  45.3 1.5 %collective-permute-done.15.refs_5_ = f32[8,128]{1,0:T(8,128)S(1)} collective-permute-done((f32[8,128]{1,0:T(8,128)S(1)}, f32[8,128]{1,0:T(8,128)S(1)}, u32[]{:S(2)}, u32[]{:S(2)}) %collective-permute-start.15) | collective-permute-done | bytes 4128 | tf_op jit(solution)/shard_map/ppermute | solution.py:40
  47.5 1.8 %shard_map.135 = (f32[136,128]{1,0:T(8,128)S(1)}, f32[72,128]{1,0:T(8,128)S(1)}) custom-call(s32[2,32]{1,0:T(2,128)S(1)} %pad_add_fusion.2.refs_0_, f32[8,128]{1,0:T(8,128)S(1)} %get-tuple-element.36.refs_1_, f32[136,128]{1,0:T(8,128)S(1)} %get-tuple-element.39.refs_2_, f32[8,128]{1,0:T(8,128)S(1)} %get-tuple-element.40.refs_3_, ...), custom_call_target="tpu_custom_call" | custom-call | tf_op jit(solution)/shard_map/pallas_call | solution.py:367
  49.3 1.9 %collective-permute-start.18 = (f32[72,128]{1,0:T(8,128)S(1)}, f32[72,128]{1,0:T(8,128)S(1)}, u32[]{:S(2)}, u32[]{:S(2)}) collective-permute-start(f32[72,128]{1,0:T(8,128)S(1)} %get-tuple-element.43.refs_2_), channel_id=1, source_target_pairs={{3,0},{2,1},{1,2},{0,3},{7,4},{6,5},{5,6},{4,7},{11,8},{10,9},{9,1... | collective-permute-start | bytes 110600 | tf_op jit(solution)/shard_map/ppermute | solution.py:28
  52.1 1.6 %collective-permute-start.16 = (f32[72,128]{1,0:T(8,128)S(1)}, f32[72,128]{1,0:T(8,128)S(1)}, u32[]{:S(2)}, u32[]{:S(2)}) collective-permute-start(f32[72,128]{1,0:T(8,128)S(1)} %get-tuple-element.43.refs_2_), channel_id=1, source_target_pairs={{1,0},{0,1},{3,2},{2,3},{5,4},{4,5},{7,6},{6,7},{9,8},{8,9},{11,10... | collective-permute-start | bytes 110600 | tf_op jit(solution)/shard_map/ppermute | solution.py:28
  56.5 2.6 %shard_map.136 = (f32[256,128]{1,0:T(8,128)S(1)}, f32[136,128]{1,0:T(8,128)S(1)}, f32[8,128]{1,0:T(8,128)S(1)}) custom-call(s32[2,32]{1,0:T(2,128)S(1)} %pad_add_fusion.refs_0_, f32[8,128]{1,0:T(8,128)S(1)} %get-tuple-element.36.refs_1_, f32[72,128]{1,0:T(8,128)S(1)} %get-tuple-element.43.refs_2_, f32[72,128]{1,0:T(8,128)S(1)} %collective-permute-done.16.refs_3_, ...), custom_call_target="tpu_custom_call" | custom-call | tf_op jit(solution)/shard_map/pallas_call | solution.py:367
  60.1 2.0 %collective-permute-start.20 = (f32[8,128]{1,0:T(8,128)S(1)}, f32[8,128]{1,0:T(8,128)S(1)}, u32[]{:S(2)}, u32[]{:S(2)}) collective-permute-start(f32[8,128]{1,0:T(8,128)S(1)} %get-tuple-element.46.refs_3_), channel_id=1, source_target_pairs={{24,0},{16,8},{8,16},{0,24},{25,1},{17,9},{9,17},{1,25},{26,2},{18... | collective-permute-start | bytes 12296 | tf_op jit(solution)/shard_map/ppermute | solution.py:40
  62.8 1.8 %collective-permute-done.20.refs_5_ = f32[8,128]{1,0:T(8,128)S(1)} collective-permute-done((f32[8,128]{1,0:T(8,128)S(1)}, f32[8,128]{1,0:T(8,128)S(1)}, u32[]{:S(2)}, u32[]{:S(2)}) %collective-permute-start.20) | collective-permute-done | bytes 4128 | tf_op jit(solution)/shard_map/ppermute | solution.py:40
  65.7 1.8 %shard_map.137 = (f32[136,128]{1,0:T(8,128)S(1)}, f32[72,128]{1,0:T(8,128)S(1)}, f32[8,128]{1,0:T(8,128)S(1)}) custom-call(s32[2,32]{1,0:T(2,128)S(1)} %pad_add_fusion.2.refs_0_, f32[8,128]{1,0:T(8,128)S(1)} %get-tuple-element.36.refs_1_, f32[136,128]{1,0:T(8,128)S(1)} %get-tuple-element.45.refs_2_, f32[8,128]{1,0:T(8,128)S(1)} %get-tuple-element.46.refs_3_, ...), custom_call_target="tpu_custom_call" | custom-call | tf_op jit(solution)/shard_map/pallas_call | solution.py:367
  67.6 2.2 %collective-permute-start.24 = (f32[72,128]{1,0:T(8,128)S(1)}, f32[72,128]{1,0:T(8,128)S(1)}, u32[]{:S(2)}, u32[]{:S(2)}) collective-permute-start(f32[72,128]{1,0:T(8,128)S(1)} %get-tuple-element.49.refs_2_), channel_id=1, source_target_pairs={{3,0},{2,1},{1,2},{0,3},{7,4},{6,5},{5,6},{4,7},{11,8},{10,9},{9,1... | collective-permute-start | bytes 110600 | tf_op jit(solution)/shard_map/ppermute | solution.py:28
  70.3 1.7 %collective-permute-start.22 = (f32[72,128]{1,0:T(8,128)S(1)}, f32[72,128]{1,0:T(8,128)S(1)}, u32[]{:S(2)}, u32[]{:S(2)}) collective-permute-start(f32[72,128]{1,0:T(8,128)S(1)} %get-tuple-element.49.refs_2_), channel_id=1, source_target_pairs={{1,0},{0,1},{3,2},{2,3},{5,4},{4,5},{7,6},{6,7},{9,8},{8,9},{11,10... | collective-permute-start | bytes 110600 | tf_op jit(solution)/shard_map/ppermute | solution.py:28
  74.7 2.5 %shard_map.138 = (f32[256,128]{1,0:T(8,128)S(1)}, f32[136,128]{1,0:T(8,128)S(1)}, f32[8,128]{1,0:T(8,128)S(1)}) custom-call(s32[2,32]{1,0:T(2,128)S(1)} %pad_add_fusion.refs_0_, f32[8,128]{1,0:T(8,128)S(1)} %get-tuple-element.48.refs_1_.refs_0_, f32[72,128]{1,0:T(8,128)S(1)} %get-tuple-element.49.refs_2_, f32[72,128]{1,0:T(8,128)S(1)} %collective-permute-done.22.refs_3_, ...), custom_call_target="tpu_custom_call" | custom-call | tf_op jit(solution)/shard_map/pallas_call | solution.py:367
  79.2 2.5 %collective-permute-done.26.refs_5_ = f32[8,128]{1,0:T(8,128)S(1)} collective-permute-done((f32[8,128]{1,0:T(8,128)S(1)}, f32[8,128]{1,0:T(8,128)S(1)}, u32[]{:S(2)}, u32[]{:S(2)}) %collective-permute-start.26) | collective-permute-done | bytes 4128 | tf_op jit(solution)/shard_map/ppermute | solution.py:40
  81.8 2.4 %shard_map.139 = (f32[64,128]{1,0:T(8,128)}, f32[72,128]{1,0:T(8,128)S(1)}) custom-call(s32[2,32]{1,0:T(2,128)S(1)} %pad_add_fusion.2.refs_0_, f32[8,128]{1,0:T(8,128)S(1)} %get-tuple-element.48.refs_1_.refs_0_, f32[136,128]{1,0:T(8,128)S(1)} %get-tuple-element.51.refs_2_, f32[8,128]{1,0:T(8,128)S(1)} %get-tuple-element.52.refs_3_, ...), custom_call_target="tpu_custom_call" | custom-call | tf_op jit(solution)/shard_map/pallas_call | solution.py:367
  84.1 1.9 %collective-permute-start.29 = (f32[72,128]{1,0:T(8,128)S(1)}, f32[72,128]{1,0:T(8,128)S(1)}, u32[]{:S(2)}, u32[]{:S(2)}) collective-permute-start(f32[72,128]{1,0:T(8,128)S(1)} %get-tuple-element.55.refs_1_), channel_id=1, source_target_pairs={{3,0},{2,1},{1,2},{0,3},{7,4},{6,5},{5,6},{4,7},{11,8},{10,9},{9,1... | collective-permute-start | bytes 110600 | tf_op jit(solution)/shard_map/ppermute | solution.py:28
  86.9 1.6 %collective-permute-start.27 = (f32[72,128]{1,0:T(8,128)S(1)}, f32[72,128]{1,0:T(8,128)S(1)}, u32[]{:S(2)}, u32[]{:S(2)}) collective-permute-start(f32[72,128]{1,0:T(8,128)S(1)} %get-tuple-element.55.refs_1_), channel_id=1, source_target_pairs={{1,0},{0,1},{3,2},{2,3},{5,4},{4,5},{7,6},{6,7},{9,8},{8,9},{11,10... | collective-permute-start | bytes 110600 | tf_op jit(solution)/shard_map/ppermute | solution.py:28
  89.9 1.4 %collective-permute-done.28.refs_3_ = f32[72,128]{1,0:T(8,128)S(1)} collective-permute-done((f32[72,128]{1,0:T(8,128)S(1)}, f32[72,128]{1,0:T(8,128)S(1)}, u32[]{:S(2)}, u32[]{:S(2)}) %collective-permute-start.28) | collective-permute-done | bytes 36896 | tf_op jit(solution)/shard_map/ppermute | solution.py:28
  93.3 1.4 %collective-permute-start.31 = (f32[8,128]{1,0:T(8,128)S(1)}, f32[8,128]{1,0:T(8,128)S(1)}, u32[]{:S(2)}, u32[]{:S(2)}) collective-permute-start(f32[8,128]{1,0:T(8,128)S(1)} %get-tuple-element.58.refs_1_), channel_id=1, source_target_pairs={{24,0},{16,8},{8,16},{0,24},{25,1},{17,9},{9,17},{1,25},{26,2},{18... | collective-permute-start | bytes 12296 | tf_op jit(solution)/shard_map/ppermute | solution.py:40
  95.8 2.0 %collective-permute-done.31.refs_3_ = f32[8,128]{1,0:T(8,128)S(1)} collective-permute-done((f32[8,128]{1,0:T(8,128)S(1)}, f32[8,128]{1,0:T(8,128)S(1)}, u32[]{:S(2)}, u32[]{:S(2)}) %collective-permute-start.31) | collective-permute-done | bytes 4128 | tf_op jit(solution)/shard_map/ppermute | solution.py:40
  (80 shorter events, 33.7 us)
Async XLA Ops:
  0.6 18.9 %collective-permute-start.6 = (f32[32,128,128]{2,1,0:T(8,128)}, f32[32,128,128]{2,1,0:T(8,128)S(1)}, u32[]{:S(2)}, u32[]{:S(2)}) collective-permute-start(f32[32,128,128]{2,1,0:T(8,128)} %bitcast.7), channel_id=1, source_target_pairs={{4,0},{0,4},{5,1},{1,5},{6,2},{2,6},{7,3},{3,7},{12,8},{8,12},{13,... | collective-permute-start | bytes 6291464 | tf_op jit(solution)/shard_map/ppermute | solution.py:28
  7.9 7.2 %collective-permute-start.3 = (f32[104,128]{1,0:T(8,128)S(1)}, f32[104,128]{1,0:T(8,128)S(1)}, u32[]{:S(2)}, u32[]{:S(2)}) collective-permute-start(f32[104,128]{1,0:T(8,128)S(1)} %get-tuple-element.31.refs_0_), channel_id=1, source_target_pairs={{3,0},{2,1},{1,2},{0,3},{7,4},{6,5},{5,6},{4,7},{11,8},{10,9},{9,1... | collective-permute-start | bytes 159752 | tf_op jit(solution)/shard_map/ppermute | solution.py:28
  12.5 5.3 %collective-permute-start.2 = (f32[104,128]{1,0:T(8,128)S(1)}, f32[104,128]{1,0:T(8,128)S(1)}, u32[]{:S(2)}, u32[]{:S(2)}) collective-permute-start(f32[104,128]{1,0:T(8,128)S(1)} %get-tuple-element.31.refs_0_), channel_id=1, source_target_pairs={{2,0},{3,1},{0,2},{1,3},{6,4},{7,5},{4,6},{5,7},{10,8},{11,9},{8,1... | collective-permute-start | bytes 159752 | tf_op jit(solution)/shard_map/ppermute | solution.py:28
  12.5 5.3 %collective-permute-start.1 = (f32[104,128]{1,0:T(8,128)S(1)}, f32[104,128]{1,0:T(8,128)S(1)}, u32[]{:S(2)}, u32[]{:S(2)}) collective-permute-start(f32[104,128]{1,0:T(8,128)S(1)} %get-tuple-element.31.refs_0_), channel_id=1, source_target_pairs={{1,0},{0,1},{3,2},{2,3},{5,4},{4,5},{7,6},{6,7},{9,8},{8,9},{11,10... | collective-permute-start | bytes 159752 | tf_op jit(solution)/shard_map/ppermute | solution.py:28
  13.8 4.6 %collective-permute-start = (s32[2,32]{1,0:T(2,128)S(1)}, s32[2,32]{1,0:T(2,128)S(1)}, u32[]{:S(2)}, u32[]{:S(2)}) collective-permute-start(s32[2,32]{1,0:T(2,128)S(1)} %pad_add_fusion.1), channel_id=1, source_target_pairs={{4,0},{0,4},{5,1},{1,5},{6,2},{2,6},{7,3},{3,7},{12,8},{8,12},{13,... | collective-permute-start | bytes 776 | tf_op jit(solution)/shard_map/ppermute | solution.py:28
  15.1 4.0 %collective-permute-start.7 = (f32[128,128]{1,0:T(8,128)}, f32[128,128]{1,0:T(8,128)S(1)}, u32[]{:S(2)}, u32[]{:S(2)}) collective-permute-start(f32[128,128]{1,0:T(8,128)} %bitcast.16), channel_id=1, source_target_pairs={{4,0},{0,4},{5,1},{1,5},{6,2},{2,6},{7,3},{3,7},{12,8},{8,12},{13,... | collective-permute-start | bytes 196616 | tf_op jit(solution)/shard_map/ppermute | solution.py:28
  17.8 1.6 %collective-permute-start.4 = (f32[392,128]{1,0:T(8,128)S(1)}, f32[392,128]{1,0:T(8,128)S(1)}, u32[]{:S(2)}, u32[]{:S(2)}) collective-permute-start(f32[392,128]{1,0:T(8,128)S(1)} %shard_map.131.refs_1_.refs_6_.refs_5_), channel_id=1, source_target_pairs={{4,0},{0,4},{5,1},{1,5},{6,2},{2,6},{7,3},{3,7},{12,8},{8,12},{13,... | collective-permute-start | bytes 602120 | tf_op jit(solution)/shard_map/ppermute | solution.py:28
  24.1 3.7 %collective-permute-start.10 = (f32[16,128]{1,0:T(8,128)S(1)}, f32[16,128]{1,0:T(8,128)S(1)}, u32[]{:S(2)}, u32[]{:S(2)}) collective-permute-start(f32[16,128]{1,0:T(8,128)S(1)} %get-tuple-element.34.refs_2_), channel_id=1, source_target_pairs={{16,0},{24,8},{0,16},{8,24},{17,1},{25,9},{1,17},{9,25},{18,2},{26... | collective-permute-start | bytes 24584 | tf_op jit(solution)/shard_map/ppermute | solution.py:45
  25.7 4.5 %collective-permute-start.9 = (f32[16,128]{1,0:T(8,128)S(1)}, f32[16,128]{1,0:T(8,128)S(1)}, u32[]{:S(2)}, u32[]{:S(2)}) collective-permute-start(f32[16,128]{1,0:T(8,128)S(1)} %get-tuple-element.34.refs_2_), channel_id=1, source_target_pairs={{24,0},{16,8},{8,16},{0,24},{25,1},{17,9},{9,17},{1,25},{26,2},{18... | collective-permute-start | bytes 24584 | tf_op jit(solution)/shard_map/ppermute | solution.py:40
  27.1 3.7 %collective-permute-start.8 = (f32[16,128]{1,0:T(8,128)S(1)}, f32[16,128]{1,0:T(8,128)S(1)}, u32[]{:S(2)}, u32[]{:S(2)}) collective-permute-start(f32[16,128]{1,0:T(8,128)S(1)} %get-tuple-element.34.refs_2_), channel_id=1, source_target_pairs={{8,0},{0,8},{24,16},{16,24},{9,1},{1,9},{25,17},{17,25},{10,2},{2,... | collective-permute-start | bytes 24584 | tf_op jit(solution)/shard_map/ppermute | solution.py:40
  32.6 6.1 %collective-permute-start.13 = (f32[72,128]{1,0:T(8,128)S(1)}, f32[72,128]{1,0:T(8,128)S(1)}, u32[]{:S(2)}, u32[]{:S(2)}) collective-permute-start(f32[72,128]{1,0:T(8,128)S(1)} %get-tuple-element.37.refs_2_), channel_id=1, source_target_pairs={{3,0},{2,1},{1,2},{0,3},{7,4},{6,5},{5,6},{4,7},{11,8},{10,9},{9,1... | collective-permute-start | bytes 110600 | tf_op jit(solution)/shard_map/ppermute | solution.py:28
  34.9 4.9 %collective-permute-start.12 = (f32[72,128]{1,0:T(8,128)S(1)}, f32[72,128]{1,0:T(8,128)S(1)}, u32[]{:S(2)}, u32[]{:S(2)}) collective-permute-start(f32[72,128]{1,0:T(8,128)S(1)} %get-tuple-element.37.refs_2_), channel_id=1, source_target_pairs={{2,0},{3,1},{0,2},{1,3},{6,4},{7,5},{4,6},{5,7},{10,8},{11,9},{8,1... | collective-permute-start | bytes 110600 | tf_op jit(solution)/shard_map/ppermute | solution.py:28
  35.3 4.5 %collective-permute-start.11 = (f32[72,128]{1,0:T(8,128)S(1)}, f32[72,128]{1,0:T(8,128)S(1)}, u32[]{:S(2)}, u32[]{:S(2)}) collective-permute-start(f32[72,128]{1,0:T(8,128)S(1)} %get-tuple-element.37.refs_2_), channel_id=1, source_target_pairs={{1,0},{0,1},{3,2},{2,3},{5,4},{4,5},{7,6},{6,7},{9,8},{8,9},{11,10... | collective-permute-start | bytes 110600 | tf_op jit(solution)/shard_map/ppermute | solution.py:28
  42.3 4.6 %collective-permute-start.15 = (f32[8,128]{1,0:T(8,128)S(1)}, f32[8,128]{1,0:T(8,128)S(1)}, u32[]{:S(2)}, u32[]{:S(2)}) collective-permute-start(f32[8,128]{1,0:T(8,128)S(1)} %get-tuple-element.40.refs_3_), channel_id=1, source_target_pairs={{24,0},{16,8},{8,16},{0,24},{25,1},{17,9},{9,17},{1,25},{26,2},{18... | collective-permute-start | bytes 12296 | tf_op jit(solution)/shard_map/ppermute | solution.py:40
  43.8 3.6 %collective-permute-start.14 = (f32[8,128]{1,0:T(8,128)S(1)}, f32[8,128]{1,0:T(8,128)S(1)}, u32[]{:S(2)}, u32[]{:S(2)}) collective-permute-start(f32[8,128]{1,0:T(8,128)S(1)} %get-tuple-element.40.refs_3_), channel_id=1, source_target_pairs={{8,0},{0,8},{24,16},{16,24},{9,1},{1,9},{25,17},{17,25},{10,2},{2,... | collective-permute-start | bytes 12296 | tf_op jit(solution)/shard_map/ppermute | solution.py:40
  49.3 5.8 %collective-permute-start.18 = (f32[72,128]{1,0:T(8,128)S(1)}, f32[72,128]{1,0:T(8,128)S(1)}, u32[]{:S(2)}, u32[]{:S(2)}) collective-permute-start(f32[72,128]{1,0:T(8,128)S(1)} %get-tuple-element.43.refs_2_), channel_id=1, source_target_pairs={{3,0},{2,1},{1,2},{0,3},{7,4},{6,5},{5,6},{4,7},{11,8},{10,9},{9,1... | collective-permute-start | bytes 110600 | tf_op jit(solution)/shard_map/ppermute | solution.py:28
  51.2 5.3 %collective-permute-start.17 = (f32[72,128]{1,0:T(8,128)S(1)}, f32[72,128]{1,0:T(8,128)S(1)}, u32[]{:S(2)}, u32[]{:S(2)}) collective-permute-start(f32[72,128]{1,0:T(8,128)S(1)} %get-tuple-element.43.refs_2_), channel_id=1, source_target_pairs={{2,0},{3,1},{0,2},{1,3},{6,4},{7,5},{4,6},{5,7},{10,8},{11,9},{8,1... | collective-permute-start | bytes 110600 | tf_op jit(solution)/shard_map/ppermute | solution.py:28
  52.1 4.4 %collective-permute-start.16 = (f32[72,128]{1,0:T(8,128)S(1)}, f32[72,128]{1,0:T(8,128)S(1)}, u32[]{:S(2)}, u32[]{:S(2)}) collective-permute-start(f32[72,128]{1,0:T(8,128)S(1)} %get-tuple-element.43.refs_2_), channel_id=1, source_target_pairs={{1,0},{0,1},{3,2},{2,3},{5,4},{4,5},{7,6},{6,7},{9,8},{8,9},{11,10... | collective-permute-start | bytes 110600 | tf_op jit(solution)/shard_map/ppermute | solution.py:28
  59.1 3.7 %collective-permute-start.21 = (f32[8,128]{1,0:T(8,128)S(1)}, f32[8,128]{1,0:T(8,128)S(1)}, u32[]{:S(2)}, u32[]{:S(2)}) collective-permute-start(f32[8,128]{1,0:T(8,128)S(1)} %get-tuple-element.46.refs_3_), channel_id=1, source_target_pairs={{16,0},{24,8},{0,16},{8,24},{17,1},{25,9},{1,17},{9,25},{18,2},{26... | collective-permute-start | bytes 12296 | tf_op jit(solution)/shard_map/ppermute | solution.py:45
  60.1 4.5 %collective-permute-start.20 = (f32[8,128]{1,0:T(8,128)S(1)}, f32[8,128]{1,0:T(8,128)S(1)}, u32[]{:S(2)}, u32[]{:S(2)}) collective-permute-start(f32[8,128]{1,0:T(8,128)S(1)} %get-tuple-element.46.refs_3_), channel_id=1, source_target_pairs={{24,0},{16,8},{8,16},{0,24},{25,1},{17,9},{9,17},{1,25},{26,2},{18... | collective-permute-start | bytes 12296 | tf_op jit(solution)/shard_map/ppermute | solution.py:40
  62.1 3.6 %collective-permute-start.19 = (f32[8,128]{1,0:T(8,128)S(1)}, f32[8,128]{1,0:T(8,128)S(1)}, u32[]{:S(2)}, u32[]{:S(2)}) collective-permute-start(f32[8,128]{1,0:T(8,128)S(1)} %get-tuple-element.46.refs_3_), channel_id=1, source_target_pairs={{8,0},{0,8},{24,16},{16,24},{9,1},{1,9},{25,17},{17,25},{10,2},{2,... | collective-permute-start | bytes 12296 | tf_op jit(solution)/shard_map/ppermute | solution.py:40
  67.6 5.8 %collective-permute-start.24 = (f32[72,128]{1,0:T(8,128)S(1)}, f32[72,128]{1,0:T(8,128)S(1)}, u32[]{:S(2)}, u32[]{:S(2)}) collective-permute-start(f32[72,128]{1,0:T(8,128)S(1)} %get-tuple-element.49.refs_2_), channel_id=1, source_target_pairs={{3,0},{2,1},{1,2},{0,3},{7,4},{6,5},{5,6},{4,7},{11,8},{10,9},{9,1... | collective-permute-start | bytes 110600 | tf_op jit(solution)/shard_map/ppermute | solution.py:28
  69.8 4.9 %collective-permute-start.23 = (f32[72,128]{1,0:T(8,128)S(1)}, f32[72,128]{1,0:T(8,128)S(1)}, u32[]{:S(2)}, u32[]{:S(2)}) collective-permute-start(f32[72,128]{1,0:T(8,128)S(1)} %get-tuple-element.49.refs_2_), channel_id=1, source_target_pairs={{2,0},{3,1},{0,2},{1,3},{6,4},{7,5},{4,6},{5,7},{10,8},{11,9},{8,1... | collective-permute-start | bytes 110600 | tf_op jit(solution)/shard_map/ppermute | solution.py:28
  70.3 4.4 %collective-permute-start.22 = (f32[72,128]{1,0:T(8,128)S(1)}, f32[72,128]{1,0:T(8,128)S(1)}, u32[]{:S(2)}, u32[]{:S(2)}) collective-permute-start(f32[72,128]{1,0:T(8,128)S(1)} %get-tuple-element.49.refs_2_), channel_id=1, source_target_pairs={{1,0},{0,1},{3,2},{2,3},{5,4},{4,5},{7,6},{6,7},{9,8},{8,9},{11,10... | collective-permute-start | bytes 110600 | tf_op jit(solution)/shard_map/ppermute | solution.py:28
  77.2 4.6 %collective-permute-start.26 = (f32[8,128]{1,0:T(8,128)S(1)}, f32[8,128]{1,0:T(8,128)S(1)}, u32[]{:S(2)}, u32[]{:S(2)}) collective-permute-start(f32[8,128]{1,0:T(8,128)S(1)} %get-tuple-element.52.refs_3_), channel_id=1, source_target_pairs={{24,0},{16,8},{8,16},{0,24},{25,1},{17,9},{9,17},{1,25},{26,2},{18... | collective-permute-start | bytes 12296 | tf_op jit(solution)/shard_map/ppermute | solution.py:40
  78.2 3.6 %collective-permute-start.25 = (f32[8,128]{1,0:T(8,128)S(1)}, f32[8,128]{1,0:T(8,128)S(1)}, u32[]{:S(2)}, u32[]{:S(2)}) collective-permute-start(f32[8,128]{1,0:T(8,128)S(1)} %get-tuple-element.52.refs_3_), channel_id=1, source_target_pairs={{8,0},{0,8},{24,16},{16,24},{9,1},{1,9},{25,17},{17,25},{10,2},{2,... | collective-permute-start | bytes 12296 | tf_op jit(solution)/shard_map/ppermute | solution.py:40
  84.1 5.8 %collective-permute-start.29 = (f32[72,128]{1,0:T(8,128)S(1)}, f32[72,128]{1,0:T(8,128)S(1)}, u32[]{:S(2)}, u32[]{:S(2)}) collective-permute-start(f32[72,128]{1,0:T(8,128)S(1)} %get-tuple-element.55.refs_1_), channel_id=1, source_target_pairs={{3,0},{2,1},{1,2},{0,3},{7,4},{6,5},{5,6},{4,7},{11,8},{10,9},{9,1... | collective-permute-start | bytes 110600 | tf_op jit(solution)/shard_map/ppermute | solution.py:28
  86.0 5.3 %collective-permute-start.28 = (f32[72,128]{1,0:T(8,128)S(1)}, f32[72,128]{1,0:T(8,128)S(1)}, u32[]{:S(2)}, u32[]{:S(2)}) collective-permute-start(f32[72,128]{1,0:T(8,128)S(1)} %get-tuple-element.55.refs_1_), channel_id=1, source_target_pairs={{2,0},{3,1},{0,2},{1,3},{6,4},{7,5},{4,6},{5,7},{10,8},{11,9},{8,1... | collective-permute-start | bytes 110600 | tf_op jit(solution)/shard_map/ppermute | solution.py:28
  86.9 4.4 %collective-permute-start.27 = (f32[72,128]{1,0:T(8,128)S(1)}, f32[72,128]{1,0:T(8,128)S(1)}, u32[]{:S(2)}, u32[]{:S(2)}) collective-permute-start(f32[72,128]{1,0:T(8,128)S(1)} %get-tuple-element.55.refs_1_), channel_id=1, source_target_pairs={{1,0},{0,1},{3,2},{2,3},{5,4},{4,5},{7,6},{6,7},{9,8},{8,9},{11,10... | collective-permute-start | bytes 110600 | tf_op jit(solution)/shard_map/ppermute | solution.py:28
  92.2 3.6 %collective-permute-start.32 = (f32[8,128]{1,0:T(8,128)S(1)}, f32[8,128]{1,0:T(8,128)S(1)}, u32[]{:S(2)}, u32[]{:S(2)}) collective-permute-start(f32[8,128]{1,0:T(8,128)S(1)} %get-tuple-element.58.refs_1_), channel_id=1, source_target_pairs={{16,0},{24,8},{0,16},{8,24},{17,1},{25,9},{1,17},{9,25},{18,2},{26... | collective-permute-start | bytes 12296 | tf_op jit(solution)/shard_map/ppermute | solution.py:45
  93.3 4.5 %collective-permute-start.31 = (f32[8,128]{1,0:T(8,128)S(1)}, f32[8,128]{1,0:T(8,128)S(1)}, u32[]{:S(2)}, u32[]{:S(2)}) collective-permute-start(f32[8,128]{1,0:T(8,128)S(1)} %get-tuple-element.58.refs_1_), channel_id=1, source_target_pairs={{24,0},{16,8},{8,16},{0,24},{25,1},{17,9},{9,17},{1,25},{26,2},{18... | collective-permute-start | bytes 12296 | tf_op jit(solution)/shard_map/ppermute | solution.py:40
  94.7 3.6 %collective-permute-start.30 = (f32[8,128]{1,0:T(8,128)S(1)}, f32[8,128]{1,0:T(8,128)S(1)}, u32[]{:S(2)}, u32[]{:S(2)}) collective-permute-start(f32[8,128]{1,0:T(8,128)S(1)} %get-tuple-element.58.refs_1_), channel_id=1, source_target_pairs={{8,0},{0,8},{24,16},{16,24},{9,1},{1,9},{25,17},{17,25},{10,2},{2,... | collective-permute-start | bytes 12296 | tf_op jit(solution)/shard_map/ppermute | solution.py:40
  (13 other events, 36.2 us)

commit v2 on v1

--- a/solution.py
+++ b/solution.py
@@ -12,6 +12,9 @@
 EPSILON = 1e-06
 F32 = jnp.float32
 BF16 = jnp.bfloat16
+FETCH = 51 << 20
+AWAY = 59 << 20
+FETCHES = 8
 
 
 def up(n, m):
@@ -52,15 +55,6 @@
         is_even = lax.rem(me, 2) == 0
         return jnp.where(is_even, first, second), jnp.where(is_even, second, first)
     return first, second
-
-
-def exact_dot(chosen, values):
-    head = values.astype(BF16)
-    rest = values - head.astype(F32)
-    middle = rest.astype(BF16)
-    tail = (rest - middle.astype(F32)).astype(BF16)
-    dot = functools.partial(jnp.dot, preferred_element_type=F32)
-    return dot(chosen, head) + (dot(chosen, middle) + dot(chosen, tail))
 
 
 def onehot(lists, first, count, height):
@@ -89,78 +83,148 @@
         self.group = tile // self.nt
         self.row_lists = -(-self.nc // self.group)
         self.setup = 3 * self.rows + up(self.row_lists + 2, 8)
+        self.link = 4 * col_share + 8
         self.limit = (self.nr * listed * tile * tile * 4 * 3) // 2 + (10 << 20)
 
 
-def prepare_kernel(z, dual, rhs, rkind, x, obj, ub, ckind, rlist, clist, zmsg, xmsg):
-    rs, cs = z.rs, z.cs
-    zmsg[0:rs, :] = dual[...]
-    zmsg[rs : 2 * rs, :] = rhs[...]
+def copies(pairs, sems):
+    started = [pltpu.make_async_copy(src, dst, sems.at[i]) for i, (src, dst) in enumerate(pairs)]
+    for copy in started:
+        copy.start()
+    for copy in started:
+        copy.wait()
+
+
+def dual_message_kernel(z, dual_at, rhs_at, rkind_at, obj_at, rlist_at, zmsg, rkind, obj, rlist, sems):
+    rs = z.rs
+    copies(
+        [
+            (dual_at, zmsg.at[0:rs, :]),
+            (rhs_at, zmsg.at[rs : 2 * rs, :]),
+            (rkind_at, rkind),
+            (obj_at, obj),
+            (rlist_at, rlist),
+        ],
+        sems,
+    )
+    rhs = zmsg[rs : 2 * rs, :]
     zmsg[2 * rs : 3 * rs, :] = jnp.where(rkind[...] == 0, 0.0, -jnp.inf)
     zmsg[3 * rs : 3 * rs + 8, :] = jnp.zeros((8, z.tile), F32)
-    zmsg[3 * rs : 3 * rs + 1, :] = rlist[...].astype(F32)
+    zmsg[3 * rs : 3 * rs + 1, 0 : z.nt] = rlist[...].astype(F32)
     ones = jnp.ones((1, z.tile), F32)
     zmsg[3 * rs + 1 : 3 * rs + 2, :] = total(obj[...] * obj[...]) * ones
-    zmsg[3 * rs + 2 : 3 * rs + 3, :] = total(rhs[...] * rhs[...]) * ones
+    zmsg[3 * rs + 2 : 3 * rs + 3, :] = total(rhs * rhs) * ones
+
+
+def primal_message_kernel(
+    z, x_at, obj_at, ub_at, ckind_at, clist_at, link_at, xmsg, ub, ckind, clist, sems
+):
+    cs = z.cs
+    copies(
+        [
+            (x_at, xmsg.at[0:cs, :]),
+            (obj_at, xmsg.at[cs : 2 * cs, :]),
+            (ub_at, ub),
+            (ckind_at, ckind),
+            (clist_at, clist),
+            (link_at, xmsg.at[z.link : z.link + z.tile, :]),
+        ],
+        sems,
+    )
     kind = ckind[...]
-    xmsg[0:cs, :] = x[...]
-    xmsg[cs : 2 * cs, :] = obj[...]
     xmsg[2 * cs : 3 * cs, :] = jnp.where(kind == 2, -jnp.inf, 0.0)
     xmsg[3 * cs : 4 * cs, :] = jnp.where(kind == 1, ub[...], jnp.inf)
-    xmsg[4 * cs : 4 * cs + 8, :] = jnp.broadcast_to(clist[...].astype(F32), (8, z.tile))
+    xmsg[4 * cs : 4 * cs + 8, :] = jnp.zeros((8, z.tile), F32)
+    xmsg[4 * cs : 4 * cs + 1, 0 : z.nt] = clist[...].astype(F32)
+
+
+def fetch_kernel(z, tiles_at, tiles, token, sems):
+    step = max(z.nt // FETCHES, 1)
+    cuts = range(0, z.nt, step)
+    copies([(tiles_at.at[i : i + step], tiles.at[i : i + step]) for i in cuts], sems)
+    token[...] = jnp.zeros_like(token)
+
+
+def put_list(z, lists, rows, i):
+    lane = lax.broadcasted_iota(jnp.int32, (8, z.tile), 1)
+    moved = pltpu.roll(rows, i * z.nt, 1) if i else rows
+    return jnp.where(lane // z.nt == i, moved, lists)
 
 
 def assemble_kernel(z, *refs):
-    slots, out = refs[:-1], refs[-1]
+    slots, out = refs[1:-1], refs[-1]
     me = lax.axis_index("col")
-    lane = lax.broadcasted_iota(jnp.int32, (1, z.tile), 1)
     base = 3 * z.rows
     out[base:, :] = jnp.zeros((z.setup - base, z.tile), F32)
     sums = jnp.zeros((2, z.tile), F32)
-    lists = [jnp.zeros((1, z.tile), F32) for _ in range(z.row_lists)]
+    lists = [jnp.zeros((8, z.tile), F32) for _ in range(z.row_lists)]
     for d, slot in enumerate(slots):
         at = peer(me, d, z.nc) * z.rs
         for part in range(3):
             spot = pl.ds(pl.multiple_of(part * z.rows + at, z.rs), z.rs)
             out[spot, :] = slot[part * z.rs : (part + 1) * z.rs, :]
-        mine = lane // z.nt == d % z.group
         q = d // z.group
-        lists[q] = jnp.where(mine, slot[3 * z.rs : 3 * z.rs + 1, :], lists[q])
+        lists[q] = put_list(z, lists[q], slot[3 * z.rs : 3 * z.rs + 8, :], d % z.group)
         sums = sums + slot[3 * z.rs + 1 : 3 * z.rs + 3, :]
     for q in range(z.row_lists):
-        out[base + q : base + q + 1, :] = lists[q]
+        out[base + q : base + q + 1, :] = lists[q][0:1, :]
     out[base + z.row_lists : base + z.row_lists + 2, :] = sums
 
 
-def transposed_products(z, y_at, rlists, tiles, links, picked):
+def three_parts(values):
+    head = values.astype(BF16)
+    rest = values - head.astype(F32)
+    middle = rest.astype(BF16)
+    return head, middle, (rest - middle.astype(F32)).astype(BF16)
+
+
+def exact_dot(chosen, values):
+    head, middle, tail = three_parts(values)
+    dot = functools.partial(jnp.dot, preferred_element_type=F32)
+    return dot(chosen, head) + (dot(chosen, middle) + dot(chosen, tail))
+
+
+def exact_turned_dot(left, right):
+    dot = lambda a, b: lax.dot_general(
+        a, b, (((0,), (0,)), ((), ())), preferred_element_type=F32
+    )
+    if left.dtype == BF16:
+        head, middle, tail = three_parts(right)
+        return dot(left, head) + (dot(left, middle) + dot(left, tail))
+    head, middle, tail = three_parts(left)
+    return dot(head, right) + (dot(middle, right) + dot(tail, right))
+
+
+def transposed_products(z, y_at, shared, tiles, links, products):
     me = lax.axis_index("col")
-    picked[...] = jnp.zeros_like(picked)
     for j in range(z.nr):
+        chosen = onehot(shared[j][3 * z.rows : 3 * z.rows + 1, :], 0, z.nt, z.rows)
+        columns = exact_turned_dot(y_at[j * z.rows : (j + 1) * z.rows, :], chosen)
+        first = y_at[pl.ds(j * z.rows + me * z.rs, 1), :]
+        coupled = jnp.broadcast_to(first, (8, z.tile)).T
         for n in range(z.nt):
             k = j * z.nt + n
-            picked[k : k + 1, :] = y_at[pl.ds(j * z.rows + rlists[j, n], 1), :]
+            column = columns[:, n : n + 1]
+            products[k : k + 1, :] = jnp.sum(tiles[j][n] * column, axis=0, keepdims=True)
         k = z.listed + j
-        picked[k : k + 1, :] = y_at[pl.ds(j * z.rows + me * z.rs, 1), :]
-    turned = [picked[b * z.tile : (b + 1) * z.tile, :].T for b in range(z.blocks)]
-    for k in range(z.products):
-        if k < z.listed:
-            tile = tiles[k // z.nt][k % z.nt]
-        else:
-            tile = links[k - z.listed][...]
-        column = turned[k // z.tile][:, k % z.tile : k % z.tile + 1]
-        picked[k : k + 1, :] = jnp.sum(tile * column, axis=0, keepdims=True)
-
-
-def gradient_part(z, products, clists, g, msg, sums):
+        link = links[j][z.link : z.link + z.tile, :]
+        products[k : k + 1, :] = jnp.sum(link * coupled[:, 0:1], axis=0, keepdims=True)
+
+
+def column_lists(z, halves, q):
+    lists = jnp.zeros((8, z.tile), F32)
+    for i in range(min(z.group, z.nr - q * z.group)):
+        at = 4 * z.cs
+        lists = put_list(z, lists, halves[q * z.group + i][at : at + 8, :], i)
+    return lists[0:1, :]
+
+
+def gradient_part(z, products, halves, g, msg, sums):
     row = lax.axis_index("row")
     full = jnp.zeros((z.cols, z.tile), F32)
     for q in range(-(-z.listed // z.tile)):
         count = min(z.tile, z.listed - q * z.tile)
-        lane = lax.broadcasted_iota(jnp.int32, (1, z.tile), 1)
-        lists = jnp.zeros((1, z.tile), F32)
-        for i in range(count // z.nt):
-            lists = jnp.where(lane // z.nt == i, clists[q * z.group + i][0:1, :], lists)
-        chosen = onehot(lists, 0, count, z.cols)
+        chosen = onehot(column_lists(z, halves, q), 0, count, z.cols)
         full = full + exact_dot(chosen, products[q * z.tile : q * z.tile + count, :])
     g[0 : z.cols, :] = full
     g[z.cols :, :] = jnp.zeros((z.ghosts, z.tile), F32)
@@ -176,12 +240,10 @@
 
 
 def first_kernel(z, *refs):
-    rlists, refs = refs[0], refs[1:]
     shared, refs = refs[: z.nr], refs[z.nr :]
     halves, refs = refs[: z.nr], refs[z.nr :]
     tiles, refs = refs[: z.nr], refs[z.nr :]
-    links, refs = refs[: z.nr], refs[z.nr :]
-    y, xs, g, msg, picked = refs
+    y, xs, g, msg, products = refs
     row = lax.axis_index("row")
     for j in range(z.nr):
         y[j * z.rows : (j + 1) * z.rows, :] = shared[j][0 : z.rows, :]
@@ -189,12 +251,10 @@
         for part in range(4):
             spot = pl.ds(pl.multiple_of(part * z.xrows + at, 8), z.cs)
             xs[spot, :] = halves[j][part * z.cs : (part + 1) * z.cs, :]
-    transposed_products(z, y, rlists, tiles, links, picked)
+    transposed_products(z, y, shared, tiles, halves, products)
     base = 3 * z.rows + z.row_lists
     sums = [sum(s[base + i : base + i + 1, :] for s in shared) for i in range(2)]
-    gradient_part(
-        z, picked, [h.at[4 * z.cs : 4 * z.cs + 8, :] for h in halves], g, msg, sums
-    )
+    gradient_part(z, products, halves, g, msg, sums)
     for part in range(4):
         xs[part * z.xrows + z.cols : (part + 1) * z.xrows, :] = jnp.zeros((z.ghosts, z.tile), F32)
         for j in range(z.nr):
@@ -228,15 +288,14 @@
 
 
 def dual_kernel(z, ends, *refs):
-    rlists, w, refs = refs[0], refs[1], refs[2:]
+    w, refs = refs[0], refs[1:]
     slots, refs = refs[: z.nc], refs[z.nc :]
     shared, refs = refs[: z.nr], refs[z.nr :]
     halves, refs = refs[: z.nr], refs[z.nr :]
     tiles, refs = refs[: z.nr], refs[z.nr :]
-    links, refs = refs[: z.nr], refs[z.nr :]
     y_old = refs[0]
     y_begin = refs[1] if ends else None
-    y_out, g, msg, picked = refs[-4:]
+    y_out, g, msg, products = refs[-4:]
     dual_part(z, w, slots, shared, y_old, y_out)
     sums = []
     if ends:
@@ -244,10 +303,8 @@
         y_out[...] = mean
         moved = sum(s[z.products : z.products + 1, :] for s in slots)
         sums = [moved, move * jnp.ones((1, z.tile), F32)]
-    transposed_products(z, y_out, rlists, tiles, links, picked)
-    gradient_part(
-        z, picked, [h.at[4 * z.cs : 4 * z.cs + 8, :] for h in halves], g, msg, sums
-    )
+    transposed_products(z, y_out, shared, tiles, halves, products)
+    gradient_part(z, products, halves, g, msg, sums)
 
 
 def last_kernel(z, *refs):
@@ -270,11 +327,10 @@
     dx = sum(m[0:1, :] for m in msgs)
     dy = sum(m[1:2, :] for m in msgs)
     new = jnp.sqrt(w[0:1, :] * jnp.sqrt((dx + EPSILON) / (dy + EPSILON)))
-    out[...] = jnp.broadcast_to(new, out.shape)
+    out[0] = new[0, 0]
 
 
 def primal_kernel(z, starts, first, ends, last, *refs):
-    clists, refs = refs[0], refs[1:]
     w_old, refs = (None, refs) if first else (refs[0], refs[1:])
     g, own, refs = refs[0], refs[1], refs[2:]
     count = (z.np - 1) if starts else 2
@@ -282,12 +338,12 @@
     xs, refs = refs[0], refs[1:]
     x_old, refs = (None, refs) if first else (refs[0], refs[1:])
     x_begin, refs = (refs[0], refs[1:]) if ends else (None, refs)
+    halves, refs = refs[: z.nr], refs[z.nr :]
     tiles, refs = refs[: z.nr], refs[z.nr :]
-    links, refs = refs[: z.nr], refs[z.nr :]
     x_out, zmsg, refs = refs[0], refs[1], refs[2:]
     w_out, refs = (refs[0], refs[1:]) if starts else (None, refs)
     xs_out, refs = (refs[0], refs[1:]) if first else (None, refs)
-    work, v = refs
+    work, v, vectors = refs
     period, row = lax.axis_index("period"), lax.axis_index("row")
 
     if starts:
@@ -344,15 +400,19 @@
     else:
         x_out[...] = x_new
 
+    for q in range(-(-z.listed // z.tile)):
+        count = min(z.tile, z.listed - q * z.tile)
+        chosen = onehot(column_lists(z, halves, q), 0, count, z.cols)
+        vectors[q * z.tile : q * z.tile + count, :] = exact_turned_dot(chosen, v[0 : z.cols, :])
     lane = lax.broadcasted_iota(jnp.int32, (z.tile, z.tile), 1)
     for b in range(z.blocks):
         columns = jnp.zeros((z.tile, z.tile), F32)
         for k in range(b * z.tile, min((b + 1) * z.tile, z.products)):
             if k < z.listed:
                 tile = tiles[k // z.nt][k % z.nt]
-                vector = v[pl.ds(clists[k // z.nt, k % z.nt], 1), :]
+                vector = vectors[k : k + 1, :]
             else:
-                tile = links[k - z.listed][...]
+                tile = halves[k - z.listed][z.link : z.link + z.tile, :]
                 vector = v[z.cols + k - z.listed : z.cols + k - z.listed + 1, :]
             column = jnp.sum(tile * vector, axis=1, keepdims=True)
             columns = jnp.where(lane == k % z.tile, column, columns)
@@ -362,15 +422,19 @@
         zmsg[z.products : z.products + 1, :] = move * jnp.ones((1, z.tile), F32)
 
 
-def call(z, kernel, operands, shapes, scratch=(), smem=0):
-    spaces = [pltpu.SMEM] * smem + [pltpu.VMEM] * (len(operands) - smem)
+def call(z, kernel, operands, shapes, scratch=(), away=0, sems=0, scalar=False, limit=None):
+    spaces = [pl.ANY] * away + [pltpu.VMEM] * (len(operands) - away)
+    kinds = [s if isinstance(s, tuple) and isinstance(s[0], tuple) else (s, F32) for s in scratch]
     return pl.pallas_call(
         kernel,
         out_shape=[jax.ShapeDtypeStruct(s, F32) for s in shapes],
         in_specs=[pl.BlockSpec(memory_space=s) for s in spaces],
-        out_specs=[pl.BlockSpec(memory_space=pltpu.VMEM) for _ in shapes],
-        scratch_shapes=[pltpu.VMEM(s, F32) for s in scratch],
-        compiler_params=pltpu.CompilerParams(vmem_limit_bytes=z.limit),
+        out_specs=[
+            pl.BlockSpec(memory_space=pltpu.SMEM if scalar else pltpu.VMEM) for _ in shapes
+        ],
+        scratch_shapes=[pltpu.VMEM(s, kind) for s, kind in kinds]
+        + ([pltpu.SemaphoreType.DMA((sems,))] if sems else []),
+        compiler_params=pltpu.CompilerParams(vmem_limit_bytes=limit or z.limit),
     )(*operands)
 
 
@@ -402,42 +466,56 @@
     line = lambda rows: (rows, tile)
     row_list = tile_rows.reshape(1, listed)
     col_list = tile_cols.reshape(1, listed)
-    tiles = exchange(tile_values.reshape(listed, tile, tile), "row")
-    links = exchange(coupling.reshape(tile, tile), "row")
-    both = jnp.concatenate([row_list, col_list], axis=0)
-    lists = exchange(both, "row")
-    rlists = jnp.concatenate([b[0:1] for b in lists], axis=0)
-    clists = jnp.concatenate([b[1:2] for b in lists], axis=0)
-
-    zmsg, xmsg = call(
+    tiles_away = tile_values.reshape(listed, tile, tile)
+    tiles = exchange(tiles_away, "row")
+    (zmsg,) = call(
         z,
-        part(prepare_kernel, z),
+        part(dual_message_kernel, z),
+        (dual_start, right_side, row_kind, objective, row_list),
+        [line(3 * z.rs + 8)],
+        [(line(z.rs), jnp.int32), line(z.cs), ((1, listed), jnp.int32)],
+        away=5,
+        sems=5,
+        limit=AWAY,
+    )
+    (xmsg,) = call(
+        z,
+        part(primal_message_kernel, z),
         (
-            dual_start,
-            right_side,
-            row_kind,
             primal_start,
             objective,
             upper_bound,
             column_kind,
-            jnp.tile(row_list, (1, z.group)),
-            jnp.tile(col_list, (1, z.group)),
+            col_list,
+            coupling.reshape(tile, tile),
         ),
-        [line(3 * z.rs + 8), line(4 * z.cs + 8)],
+        [line(z.link + tile)],
+        [line(z.cs), (line(z.cs), jnp.int32), ((1, listed), jnp.int32)],
+        away=6,
+        sems=6,
+        limit=AWAY,
+    )
+    tiles[0], token = call(
+        z,
+        part(fetch_kernel, z),
+        (tiles_away,),
+        [(listed, tile, tile), line(8)],
+        away=1,
+        sems=FETCHES,
+        limit=FETCH,
     )
     slots = exchange(zmsg, "col")
     halves = exchange(xmsg, "row")
-    (gathered,) = call(z, part(assemble_kernel, z), slots, [line(z.setup)])
+    (gathered,) = call(z, part(assemble_kernel, z), [token] + slots, [line(z.setup)])
     shared = exchange(gathered, "row")
 
-    picked = line(z.blocks * tile)
+    products = line(up(z.products, 8))
     y, xs, g, msg = call(
         z,
         part(first_kernel, z),
-        (rlists, *shared, *halves, *tiles, *links),
+        (*shared, *halves, *tiles),
         [line(z.nr * z.rows), line(4 * z.xrows), line(z.xrows), line(z.hop_first)],
-        [picked],
-        smem=1,
+        [products],
     )
     x = None
     weight = None
@@ -447,8 +525,8 @@
         ends = step % INNER == INNER - 1
         first, last = step == 0, step == ROUNDS * INNER - 1
         got = period_exchange(msg, starts)
-        operands = [clists] + ([] if first else [weight]) + [g, msg, *got, xs]
-        operands += ([] if first else [x]) + ([x_begin] if ends else []) + [*tiles, *links]
+        operands = ([] if first else [weight]) + [g, msg, *got, xs]
+        operands += ([] if first else [x]) + ([x_begin] if ends else []) + [*halves, *tiles]
         shapes = [line(z.cs if last else z.xrows), line(z.zrows)]
         shapes += ([line(8)] if starts else []) + ([line(4 * z.xrows)] if first else [])
         outs = call(
@@ -456,8 +534,7 @@
             part(primal_kernel, z, starts, first, ends, last),
             operands,
             shapes,
-            [line(z.xrows), line(z.xrows)],
-            smem=1,
+            [line(z.xrows), line(z.xrows), line(up(z.listed, 8))],
         )
         x_next, zmsg = outs[:2]
         if starts:
@@ -471,14 +548,13 @@
         slots = exchange(zmsg, "col")
         if last:
             break
-        operands = [rlists, weight, *slots, *shared, *halves, *tiles, *links, y]
+        operands = [weight, *slots, *shared, *halves, *tiles, y]
         y_next, g, msg = call(
             z,
             part(dual_kernel, z, ends),
             operands + ([y_begin] if ends else []),
             [line(z.nr * z.rows), line(z.xrows), line(z.hop)],
-            [picked],
-            smem=1,
+            [products],
         )
         y = y_next
         if ends:
@@ -494,9 +570,10 @@
         z,
         part(weight_kernel, z),
         (weight, sums, *period_exchange(sums, True)),
-        [line(8)],
-    )
-    return (x, dual, final[0, 0])
+        [(1,)],
+        scalar=True,
+    )
+    return (x, dual, final.reshape(()))
 
 
 def solution(mesh):

time: 99.5 us -> 89 us (0.89)
  local copies, waits for them, and re-layouts: 9.64 us -> 0.01 us
  Pallas kernels: 18.8 us -> 21.2 us
  other arithmetic: 1.36 us -> 0 us
  waiting for transfers between devices: 28.6 us -> 27.4 us
    unnamed x24 -> x4, local copies, waits for them, and re-layouts: 7.62 us -> 0.01 us
    pallas_call x12 -> x14, Pallas kernels: 18.8 us -> 21.2 us  [call(): pl.pallas_call(kernel, out_shape=[jax.ShapeDtypeStruct(s, F32) for s in s...]
    another operation x4 -> x0, local copies, waits for them, and re-layouts: 1.48 us -> none  [the longest x2 0.74 us: per_device(): jnp.tile(row_list, (1, z.group))]
    concatenate x3 -> x0, other arithmetic: 1.36 us -> none  [the longest x1 0.68 us: per_device(): both = jnp.concatenate([row_list, col_list], axis=0)]
    ppermute x20 -> x18, waiting for transfers between devices: 15.1 us -> 13.9 us  [from_peer(): return lax.ppermute(x, axis, pairs)]
    ppermute x20 -> x18, starting transfers between devices: 24.1 us -> 23.7 us  [from_peer(): return lax.ppermute(x, axis, pairs)]
  transfers between devices with their start and end apart: 33 -> 31, of which waited for: 24 -> 23; matrix products, arithmetic and copies ran while one was open for 3% -> 0% of each run, Pallas kernels for 0% -> 6%
where the time goes in v2:
time: 89 us; the launch traced here: 88.7 us
  starting transfers between devices  39.4 us (44%)
  waiting for transfers between devices  27.4 us (31%)
  Pallas kernels  21.2 us (24%)
    ppermute x18, starting transfers between devices, from_peer(): return lax.ppermute(x, axis, pairs)  23.7 us
    pallas_call x14, Pallas kernels, call(): pl.pallas_call(kernel, out_shape=[jax.ShapeDtypeStruct(s, F32) for s in s...  21.2 us
    ppermute x18, waiting for transfers between devices, from_peer(): return lax.ppermute(x, axis, pairs)  13.9 us
    ppermute x10, waiting for transfers between devices, period_exchange(): lax.ppermute(x, 'period', [(m[i], i) for i in range(n)])  13.1 us
    ppermute x10, starting transfers between devices, period_exchange(): lax.ppermute(x, 'period', [(m[i], i) for i in range(n)])  12 us
    ppermute x3, starting transfers between devices, period_exchange(): lax.ppermute(x, 'period', [((i + s) % n, i) for i in range(n)])  3.68 us
  transfers between devices with their start and end apart: 31, of which 23 were waited for; matrix products, arithmetic and copies ran while one was open for 0% of the time, Pallas kernels for 6%

profile of v2, /device:TPU:0, one launch (start us, length us, event | category | flops | bytes accessed | tf_op | source)
XLA Modules:
  0.0 88.7 jit_solution(584792031410799076)
XLA Ops:
  1.1 1.6 %shard_map.131.refs_1_ = f32[104,128]{1,0:T(8,128)} custom-call(f32[32,128]{1,0:T(8,128)} %dual_at.1, f32[32,128]{1,0:T(8,128)} %rhs_at.1, s32[32,128]{1,0:T(8,128)} %rkind_at.1, f32[64,128]{1,0:T(8,128)} %obj_at.3, s32[1,32]{1,0:T(1,128)} %bitcast.8), custom_call_target="tpu_custom_call" | custom-call | tf_op jit(solution)/shard_map/pallas_call | solution.py:428
  2.7 4.7 %collective-permute-start.2 = (f32[104,128]{1,0:T(8,128)}, f32[104,128]{1,0:T(8,128)S(1)}, u32[]{:S(2)}, u32[]{:S(2)}) collective-permute-start(f32[104,128]{1,0:T(8,128)} %shard_map.131.refs_1_), channel_id=1, source_target_pairs={{3,0},{2,1},{1,2},{0,3},{7,4},{6,5},{5,6},{4,7},{11,8},{10,9},{9,1... | collective-permute-start | bytes 159752 | tf_op jit(solution)/shard_map/ppermute | solution.py:31
  8.0 1.7 %shard_map.133.refs_2_.refs_6_.refs_7_.refs_8_ = f32[392,128]{1,0:T(8,128)} custom-call(f32[64,128]{1,0:T(8,128)} %x_at.1, f32[64,128]{1,0:T(8,128)} %obj_at.3, f32[64,128]{1,0:T(8,128)} %ub_at.1, s32[64,128]{1,0:T(8,128)} %ckind_at.1, s32[1,32]{1,0:T(1,128)} %bitcast.9, f32[128,128]{1,0:T(8,128)} %bitcast.7), custom_call_target="tpu_custom_call" | custom-call | tf_op jit(solution)/shard_map/pallas_call | solution.py:428
  9.8 1.6 %shard_map.130 = (f32[32,128,128]{2,1,0:T(8,128)S(1)}, f32[8,128]{1,0:T(8,128)S(1)}) custom-call(f32[32,128,128]{2,1,0:T(8,128)} %bitcast.6), custom_call_target="tpu_custom_call" | custom-call | tf_op jit(solution)/shard_map/pallas_call | solution.py:428
  11.4 1.4 %collective-permute-done.1.refs_3_ = f32[104,128]{1,0:T(8,128)S(1)} collective-permute-done((f32[104,128]{1,0:T(8,128)}, f32[104,128]{1,0:T(8,128)S(1)}, u32[]{:S(2)}, u32[]{:S(2)}) %collective-permute-start.1) | collective-permute-done | bytes 53280 | tf_op jit(solution)/shard_map/ppermute | solution.py:31
  14.5 1.8 %shard_map.134 = (f32[256,128]{1,0:T(8,128)S(1)}, f32[544,128]{1,0:T(8,128)S(1)}, f32[136,128]{1,0:T(8,128)S(1)}, f32[16,128]{1,0:T(8,128)S(1)}) custom-call(f32[392,128]{1,0:T(8,128)S(1)} %shard_map.132.refs_0_.refs_5_, f32[392,128]{1,0:T(8,128)S(1)} %collective-permute-done.3.refs_1_.refs_6_, f32[392,128]{1,0:T(8,128)S(1)} %copy-done, ...), custom_call_target="tpu_custom_call" | custom-call | tf_op jit(solution)/shard_map/pallas_call | solution.py:428
  16.2 1.6 %collective-permute-start.8 = (f32[16,128]{1,0:T(8,128)S(1)}, f32[16,128]{1,0:T(8,128)S(1)}, u32[]{:S(2)}, u32[]{:S(2)}) collective-permute-start(f32[16,128]{1,0:T(8,128)S(1)} %get-tuple-element.34.refs_1_), channel_id=1, source_target_pairs={{16,0},{24,8},{0,16},{8,24},{17,1},{25,9},{1,17},{9,25},{18,2},{26... | collective-permute-start | bytes 24584 | tf_op jit(solution)/shard_map/ppermute | solution.py:48
  20.0 2.4 %collective-permute-done.7.refs_3_ = f32[16,128]{1,0:T(8,128)S(1)} collective-permute-done((f32[16,128]{1,0:T(8,128)S(1)}, f32[16,128]{1,0:T(8,128)S(1)}, u32[]{:S(2)}, u32[]{:S(2)}) %collective-permute-start.7) | collective-permute-done | bytes 8224 | tf_op jit(solution)/shard_map/ppermute | solution.py:43
  22.9 1.5 %shard_map.135 = (f32[136,128]{1,0:T(8,128)S(1)}, f32[72,128]{1,0:T(8,128)S(1)}, f32[8,128]{1,0:T(8,128)S(1)}, f32[544,128]{1,0:T(8,128)S(1)}) custom-call(f32[136,128]{1,0:T(8,128)S(1)} %get-tuple-element.33.refs_0_, f32[16,128]{1,0:T(8,128)S(1)} %get-tuple-element.34.refs_1_, f32[16,128]{1,0:T(8,128)S(1)} %collective-permute-done.6.refs_2_, ...), custom_call_target="tpu_custom_call" | custom-call | tf_op jit(solution)/shard_map/pallas_call | solution.py:428
  24.4 2.5 %collective-permute-start.11 = (f32[72,128]{1,0:T(8,128)S(1)}, f32[72,128]{1,0:T(8,128)S(1)}, u32[]{:S(2)}, u32[]{:S(2)}) collective-permute-start(f32[72,128]{1,0:T(8,128)S(1)} %get-tuple-element.37.refs_1_), channel_id=1, source_target_pairs={{3,0},{2,1},{1,2},{0,3},{7,4},{6,5},{5,6},{4,7},{11,8},{10,9},{9,1... | collective-permute-start | bytes 110600 | tf_op jit(solution)/shard_map/ppermute | solution.py:31
  27.3 1.6 %collective-permute-start.9 = (f32[72,128]{1,0:T(8,128)S(1)}, f32[72,128]{1,0:T(8,128)S(1)}, u32[]{:S(2)}, u32[]{:S(2)}) collective-permute-start(f32[72,128]{1,0:T(8,128)S(1)} %get-tuple-element.37.refs_1_), channel_id=1, source_target_pairs={{1,0},{0,1},{3,2},{2,3},{5,4},{4,5},{7,6},{6,7},{9,8},{8,9},{11,10... | collective-permute-start | bytes 110600 | tf_op jit(solution)/shard_map/ppermute | solution.py:31
  28.9 1.7 %collective-permute-done.11.refs_4_ = f32[72,128]{1,0:T(8,128)S(1)} collective-permute-done((f32[72,128]{1,0:T(8,128)S(1)}, f32[72,128]{1,0:T(8,128)S(1)}, u32[]{:S(2)}, u32[]{:S(2)}) %collective-permute-start.11) | collective-permute-done | bytes 36896 | tf_op jit(solution)/shard_map/ppermute | solution.py:31
  31.8 2.1 %shard_map.136 = (f32[256,128]{1,0:T(8,128)S(1)}, f32[136,128]{1,0:T(8,128)S(1)}, f32[8,128]{1,0:T(8,128)S(1)}) custom-call(f32[8,128]{1,0:T(8,128)S(1)} %get-tuple-element.36.refs_0_, f32[72,128]{1,0:T(8,128)S(1)} %get-tuple-element.37.refs_1_, f32[72,128]{1,0:T(8,128)S(1)} %collective-permute-done.9.refs_2_, ...), custom_call_target="tpu_custom_call" | custom-call | tf_op jit(solution)/shard_map/pallas_call | solution.py:428
  33.9 1.6 %collective-permute-start.13 = (f32[8,128]{1,0:T(8,128)S(1)}, f32[8,128]{1,0:T(8,128)S(1)}, u32[]{:S(2)}, u32[]{:S(2)}) collective-permute-start(f32[8,128]{1,0:T(8,128)S(1)} %get-tuple-element.40.refs_2_), channel_id=1, source_target_pairs={{24,0},{16,8},{8,16},{0,24},{25,1},{17,9},{9,17},{1,25},{26,2},{18... | collective-permute-start | bytes 12296 | tf_op jit(solution)/shard_map/ppermute | solution.py:43
  35.5 1.5 %collective-permute-start.12 = (f32[8,128]{1,0:T(8,128)S(1)}, f32[8,128]{1,0:T(8,128)S(1)}, u32[]{:S(2)}, u32[]{:S(2)}) collective-permute-start(f32[8,128]{1,0:T(8,128)S(1)} %get-tuple-element.40.refs_2_), channel_id=1, source_target_pairs={{8,0},{0,8},{24,16},{16,24},{9,1},{1,9},{25,17},{17,25},{10,2},{2,... | collective-permute-start | bytes 12296 | tf_op jit(solution)/shard_map/ppermute | solution.py:43
  37.0 1.5 %collective-permute-done.13.refs_4_ = f32[8,128]{1,0:T(8,128)S(1)} collective-permute-done((f32[8,128]{1,0:T(8,128)S(1)}, f32[8,128]{1,0:T(8,128)S(1)}, u32[]{:S(2)}, u32[]{:S(2)}) %collective-permute-start.13) | collective-permute-done | bytes 4128 | tf_op jit(solution)/shard_map/ppermute | solution.py:43
  39.1 1.5 %shard_map.137 = (f32[136,128]{1,0:T(8,128)S(1)}, f32[72,128]{1,0:T(8,128)S(1)}) custom-call(f32[8,128]{1,0:T(8,128)S(1)} %get-tuple-element.36.refs_0_, f32[136,128]{1,0:T(8,128)S(1)} %get-tuple-element.39.refs_1_, f32[8,128]{1,0:T(8,128)S(1)} %get-tuple-element.40.refs_2_, f32[8,128]{1,0:T(8,128)S(1)} %collective-permute-done.12.refs_3_, ...), custom_call_target="tpu_custom_call" | custom-call | tf_op jit(solution)/shard_map/pallas_call | solution.py:428
  40.6 1.9 %collective-permute-start.16 = (f32[72,128]{1,0:T(8,128)S(1)}, f32[72,128]{1,0:T(8,128)S(1)}, u32[]{:S(2)}, u32[]{:S(2)}) collective-permute-start(f32[72,128]{1,0:T(8,128)S(1)} %get-tuple-element.43.refs_1_), channel_id=1, source_target_pairs={{3,0},{2,1},{1,2},{0,3},{7,4},{6,5},{5,6},{4,7},{11,8},{10,9},{9,1... | collective-permute-start | bytes 110600 | tf_op jit(solution)/shard_map/ppermute | solution.py:31
  43.2 1.9 %collective-permute-start.14 = (f32[72,128]{1,0:T(8,128)S(1)}, f32[72,128]{1,0:T(8,128)S(1)}, u32[]{:S(2)}, u32[]{:S(2)}) collective-permute-start(f32[72,128]{1,0:T(8,128)S(1)} %get-tuple-element.43.refs_1_), channel_id=1, source_target_pairs={{1,0},{0,1},{3,2},{2,3},{5,4},{4,5},{7,6},{6,7},{9,8},{8,9},{11,10... | collective-permute-start | bytes 110600 | tf_op jit(solution)/shard_map/ppermute | solution.py:31
  47.8 2.1 %shard_map.138 = (f32[256,128]{1,0:T(8,128)S(1)}, f32[136,128]{1,0:T(8,128)S(1)}, f32[8,128]{1,0:T(8,128)S(1)}) custom-call(f32[8,128]{1,0:T(8,128)S(1)} %get-tuple-element.36.refs_0_, f32[72,128]{1,0:T(8,128)S(1)} %get-tuple-element.43.refs_1_, f32[72,128]{1,0:T(8,128)S(1)} %collective-permute-done.14.refs_2_, ...), custom_call_target="tpu_custom_call" | custom-call | tf_op jit(solution)/shard_map/pallas_call | solution.py:428
  50.9 2.0 %collective-permute-start.18 = (f32[8,128]{1,0:T(8,128)S(1)}, f32[8,128]{1,0:T(8,128)S(1)}, u32[]{:S(2)}, u32[]{:S(2)}) collective-permute-start(f32[8,128]{1,0:T(8,128)S(1)} %get-tuple-element.46.refs_2_), channel_id=1, source_target_pairs={{24,0},{16,8},{8,16},{0,24},{25,1},{17,9},{9,17},{1,25},{26,2},{18... | collective-permute-start | bytes 12296 | tf_op jit(solution)/shard_map/ppermute | solution.py:43
  53.6 1.8 %collective-permute-done.18.refs_4_ = f32[8,128]{1,0:T(8,128)S(1)} collective-permute-done((f32[8,128]{1,0:T(8,128)S(1)}, f32[8,128]{1,0:T(8,128)S(1)}, u32[]{:S(2)}, u32[]{:S(2)}) %collective-permute-start.18) | collective-permute-done | bytes 4128 | tf_op jit(solution)/shard_map/ppermute | solution.py:43
  56.6 1.5 %shard_map.139 = (f32[136,128]{1,0:T(8,128)S(1)}, f32[72,128]{1,0:T(8,128)S(1)}, f32[8,128]{1,0:T(8,128)S(1)}) custom-call(f32[8,128]{1,0:T(8,128)S(1)} %get-tuple-element.36.refs_0_, f32[136,128]{1,0:T(8,128)S(1)} %get-tuple-element.45.refs_1_, f32[8,128]{1,0:T(8,128)S(1)} %get-tuple-element.46.refs_2_, f32[8,128]{1,0:T(8,128)S(1)} %collective-permute-done.17.refs_3_, ...), custom_call_target="tpu_custom_call" | custom-call | tf_op jit(solution)/shard_map/pallas_call | solution.py:428
  58.1 2.0 %collective-permute-start.22 = (f32[72,128]{1,0:T(8,128)S(1)}, f32[72,128]{1,0:T(8,128)S(1)}, u32[]{:S(2)}, u32[]{:S(2)}) collective-permute-start(f32[72,128]{1,0:T(8,128)S(1)} %get-tuple-element.49.refs_1_), channel_id=1, source_target_pairs={{3,0},{2,1},{1,2},{0,3},{7,4},{6,5},{5,6},{4,7},{11,8},{10,9},{9,1... | collective-permute-start | bytes 110600 | tf_op jit(solution)/shard_map/ppermute | solution.py:31
  60.8 1.7 %collective-permute-start.20 = (f32[72,128]{1,0:T(8,128)S(1)}, f32[72,128]{1,0:T(8,128)S(1)}, u32[]{:S(2)}, u32[]{:S(2)}) collective-permute-start(f32[72,128]{1,0:T(8,128)S(1)} %get-tuple-element.49.refs_1_), channel_id=1, source_target_pairs={{1,0},{0,1},{3,2},{2,3},{5,4},{4,5},{7,6},{6,7},{9,8},{8,9},{11,10... | collective-permute-start | bytes 110600 | tf_op jit(solution)/shard_map/ppermute | solution.py:31
  65.2 2.1 %shard_map.140 = (f32[256,128]{1,0:T(8,128)S(1)}, f32[136,128]{1,0:T(8,128)S(1)}, f32[8,128]{1,0:T(8,128)S(1)}) custom-call(f32[8,128]{1,0:T(8,128)S(1)} %get-tuple-element.48.refs_0_, f32[72,128]{1,0:T(8,128)S(1)} %get-tuple-element.49.refs_1_, f32[72,128]{1,0:T(8,128)S(1)} %collective-permute-done.20.refs_2_, ...), custom_call_target="tpu_custom_call" | custom-call | tf_op jit(solution)/shard_map/pallas_call | solution.py:428
  69.4 2.5 %collective-permute-done.24.refs_4_ = f32[8,128]{1,0:T(8,128)S(1)} collective-permute-done((f32[8,128]{1,0:T(8,128)S(1)}, f32[8,128]{1,0:T(8,128)S(1)}, u32[]{:S(2)}, u32[]{:S(2)}) %collective-permute-start.24) | collective-permute-done | bytes 4128 | tf_op jit(solution)/shard_map/ppermute | solution.py:43
  71.9 2.1 %shard_map.141 = (f32[64,128]{1,0:T(8,128)}, f32[72,128]{1,0:T(8,128)S(1)}) custom-call(f32[8,128]{1,0:T(8,128)S(1)} %get-tuple-element.48.refs_0_, f32[136,128]{1,0:T(8,128)S(1)} %get-tuple-element.51.refs_1_, f32[8,128]{1,0:T(8,128)S(1)} %get-tuple-element.52.refs_2_, f32[8,128]{1,0:T(8,128)S(1)} %collective-permute-done.23.refs_3_, ...), custom_call_target="tpu_custom_call" | custom-call | tf_op jit(solution)/shard_map/pallas_call | solution.py:428
  74.0 1.9 %collective-permute-start.27 = (f32[72,128]{1,0:T(8,128)S(1)}, f32[72,128]{1,0:T(8,128)S(1)}, u32[]{:S(2)}, u32[]{:S(2)}) collective-permute-start(f32[72,128]{1,0:T(8,128)S(1)} %get-tuple-element.55.refs_1_), channel_id=1, source_target_pairs={{3,0},{2,1},{1,2},{0,3},{7,4},{6,5},{5,6},{4,7},{11,8},{10,9},{9,1... | collective-permute-start | bytes 110600 | tf_op jit(solution)/shard_map/ppermute | solution.py:31
  76.7 1.6 %collective-permute-start.25 = (f32[72,128]{1,0:T(8,128)S(1)}, f32[72,128]{1,0:T(8,128)S(1)}, u32[]{:S(2)}, u32[]{:S(2)}) collective-permute-start(f32[72,128]{1,0:T(8,128)S(1)} %get-tuple-element.55.refs_1_), channel_id=1, source_target_pairs={{1,0},{0,1},{3,2},{2,3},{5,4},{4,5},{7,6},{6,7},{9,8},{8,9},{11,10... | collective-permute-start | bytes 110600 | tf_op jit(solution)/shard_map/ppermute | solution.py:31
  83.1 1.4 %collective-permute-start.29 = (f32[8,128]{1,0:T(8,128)S(1)}, f32[8,128]{1,0:T(8,128)S(1)}, u32[]{:S(2)}, u32[]{:S(2)}) collective-permute-start(f32[8,128]{1,0:T(8,128)S(1)} %get-tuple-element.58.refs_1_), channel_id=1, source_target_pairs={{24,0},{16,8},{8,16},{0,24},{25,1},{17,9},{9,17},{1,25},{26,2},{18... | collective-permute-start | bytes 12296 | tf_op jit(solution)/shard_map/ppermute | solution.py:43
  85.6 2.0 %collective-permute-done.29.refs_3_ = f32[8,128]{1,0:T(8,128)S(1)} collective-permute-done((f32[8,128]{1,0:T(8,128)S(1)}, f32[8,128]{1,0:T(8,128)S(1)}, u32[]{:S(2)}, u32[]{:S(2)}) %collective-permute-start.29) | collective-permute-done | bytes 4128 | tf_op jit(solution)/shard_map/ppermute | solution.py:43
  (49 shorter events, 27.0 us)
Async XLA Ops:
  0.6 13.8 %collective-permute-start.5 = (f32[32,128,128]{2,1,0:T(8,128)}, f32[32,128,128]{2,1,0:T(8,128)S(1)}, u32[]{:S(2)}, u32[]{:S(2)}) collective-permute-start(f32[32,128,128]{2,1,0:T(8,128)} %bitcast.5), channel_id=1, source_target_pairs={{4,0},{0,4},{5,1},{1,5},{6,2},{2,6},{7,3},{3,7},{12,8},{8,12},{13,... | collective-permute-start | bytes 6291464 | tf_op jit(solution)/shard_map/ppermute | solution.py:31
  2.7 10.2 %copy-start.1 = (f32[104,128]{1,0:T(8,128)S(1)}, f32[104,128]{1,0:T(8,128)}, u32[]{:S(2)}) copy-start(f32[104,128]{1,0:T(8,128)} %shard_map.131.refs_1_) | copy-start | bytes 159748
  2.7 8.7 %collective-permute-start.2 = (f32[104,128]{1,0:T(8,128)}, f32[104,128]{1,0:T(8,128)S(1)}, u32[]{:S(2)}, u32[]{:S(2)}) collective-permute-start(f32[104,128]{1,0:T(8,128)} %shard_map.131.refs_1_), channel_id=1, source_target_pairs={{3,0},{2,1},{1,2},{0,3},{7,4},{6,5},{5,6},{4,7},{11,8},{10,9},{9,1... | collective-permute-start | bytes 159752 | tf_op jit(solution)/shard_map/ppermute | solution.py:31
  7.4 5.5 %collective-permute-start.1 = (f32[104,128]{1,0:T(8,128)}, f32[104,128]{1,0:T(8,128)S(1)}, u32[]{:S(2)}, u32[]{:S(2)}) collective-permute-start(f32[104,128]{1,0:T(8,128)} %shard_map.131.refs_1_), channel_id=1, source_target_pairs={{2,0},{3,1},{0,2},{1,3},{6,4},{7,5},{4,6},{5,7},{10,8},{11,9},{8,1... | collective-permute-start | bytes 159752 | tf_op jit(solution)/shard_map/ppermute | solution.py:31
  7.4 5.5 %collective-permute-start = (f32[104,128]{1,0:T(8,128)}, f32[104,128]{1,0:T(8,128)S(1)}, u32[]{:S(2)}, u32[]{:S(2)}) collective-permute-start(f32[104,128]{1,0:T(8,128)} %shard_map.131.refs_1_), channel_id=1, source_target_pairs={{1,0},{0,1},{3,2},{2,3},{5,4},{4,5},{7,6},{6,7},{9,8},{8,9},{11,10... | collective-permute-start | bytes 159752 | tf_op jit(solution)/shard_map/ppermute | solution.py:31
  9.7 3.3 %collective-permute-start.4 = (f32[392,128]{1,0:T(8,128)}, f32[392,128]{1,0:T(8,128)S(1)}, u32[]{:S(2)}, u32[]{:S(2)}) collective-permute-start(f32[392,128]{1,0:T(8,128)} %shard_map.133.refs_2_.refs_6_.refs_7_.refs_8_), channel_id=1, source_target_pairs={{4,0},{0,4},{5,1},{1,5},{6,2},{2,6},{7,3},{3,7},{12,8},{8,12},{13,... | collective-permute-start | bytes 602120 | tf_op jit(solution)/shard_map/ppermute | solution.py:31
  13.0 1.5 %collective-permute-start.3 = (f32[392,128]{1,0:T(8,128)S(1)}, f32[392,128]{1,0:T(8,128)S(1)}, u32[]{:S(2)}, u32[]{:S(2)}) collective-permute-start(f32[392,128]{1,0:T(8,128)S(1)} %shard_map.132.refs_0_.refs_5_), channel_id=1, source_target_pairs={{4,0},{0,4},{5,1},{1,5},{6,2},{2,6},{7,3},{3,7},{12,8},{8,12},{13,... | collective-permute-start | bytes 602120 | tf_op jit(solution)/shard_map/ppermute | solution.py:31
  16.2 3.7 %collective-permute-start.8 = (f32[16,128]{1,0:T(8,128)S(1)}, f32[16,128]{1,0:T(8,128)S(1)}, u32[]{:S(2)}, u32[]{:S(2)}) collective-permute-start(f32[16,128]{1,0:T(8,128)S(1)} %get-tuple-element.34.refs_1_), channel_id=1, source_target_pairs={{16,0},{24,8},{0,16},{8,24},{17,1},{25,9},{1,17},{9,25},{18,2},{26... | collective-permute-start | bytes 24584 | tf_op jit(solution)/shard_map/ppermute | solution.py:48
  17.8 4.5 %collective-permute-start.7 = (f32[16,128]{1,0:T(8,128)S(1)}, f32[16,128]{1,0:T(8,128)S(1)}, u32[]{:S(2)}, u32[]{:S(2)}) collective-permute-start(f32[16,128]{1,0:T(8,128)S(1)} %get-tuple-element.34.refs_1_), channel_id=1, source_target_pairs={{24,0},{16,8},{8,16},{0,24},{25,1},{17,9},{9,17},{1,25},{26,2},{18... | collective-permute-start | bytes 24584 | tf_op jit(solution)/shard_map/ppermute | solution.py:43
  19.3 3.7 %collective-permute-start.6 = (f32[16,128]{1,0:T(8,128)S(1)}, f32[16,128]{1,0:T(8,128)S(1)}, u32[]{:S(2)}, u32[]{:S(2)}) collective-permute-start(f32[16,128]{1,0:T(8,128)S(1)} %get-tuple-element.34.refs_1_), channel_id=1, source_target_pairs={{8,0},{0,8},{24,16},{16,24},{9,1},{1,9},{25,17},{17,25},{10,2},{2,... | collective-permute-start | bytes 24584 | tf_op jit(solution)/shard_map/ppermute | solution.py:43
  24.4 6.1 %collective-permute-start.11 = (f32[72,128]{1,0:T(8,128)S(1)}, f32[72,128]{1,0:T(8,128)S(1)}, u32[]{:S(2)}, u32[]{:S(2)}) collective-permute-start(f32[72,128]{1,0:T(8,128)S(1)} %get-tuple-element.37.refs_1_), channel_id=1, source_target_pairs={{3,0},{2,1},{1,2},{0,3},{7,4},{6,5},{5,6},{4,7},{11,8},{10,9},{9,1... | collective-permute-start | bytes 110600 | tf_op jit(solution)/shard_map/ppermute | solution.py:31
  26.9 4.9 %collective-permute-start.10 = (f32[72,128]{1,0:T(8,128)S(1)}, f32[72,128]{1,0:T(8,128)S(1)}, u32[]{:S(2)}, u32[]{:S(2)}) collective-permute-start(f32[72,128]{1,0:T(8,128)S(1)} %get-tuple-element.37.refs_1_), channel_id=1, source_target_pairs={{2,0},{3,1},{0,2},{1,3},{6,4},{7,5},{4,6},{5,7},{10,8},{11,9},{8,1... | collective-permute-start | bytes 110600 | tf_op jit(solution)/shard_map/ppermute | solution.py:31
  27.3 4.5 %collective-permute-start.9 = (f32[72,128]{1,0:T(8,128)S(1)}, f32[72,128]{1,0:T(8,128)S(1)}, u32[]{:S(2)}, u32[]{:S(2)}) collective-permute-start(f32[72,128]{1,0:T(8,128)S(1)} %get-tuple-element.37.refs_1_), channel_id=1, source_target_pairs={{1,0},{0,1},{3,2},{2,3},{5,4},{4,5},{7,6},{6,7},{9,8},{8,9},{11,10... | collective-permute-start | bytes 110600 | tf_op jit(solution)/shard_map/ppermute | solution.py:31
  33.9 4.6 %collective-permute-start.13 = (f32[8,128]{1,0:T(8,128)S(1)}, f32[8,128]{1,0:T(8,128)S(1)}, u32[]{:S(2)}, u32[]{:S(2)}) collective-permute-start(f32[8,128]{1,0:T(8,128)S(1)} %get-tuple-element.40.refs_2_), channel_id=1, source_target_pairs={{24,0},{16,8},{8,16},{0,24},{25,1},{17,9},{9,17},{1,25},{26,2},{18... | collective-permute-start | bytes 12296 | tf_op jit(solution)/shard_map/ppermute | solution.py:43
  35.5 3.6 %collective-permute-start.12 = (f32[8,128]{1,0:T(8,128)S(1)}, f32[8,128]{1,0:T(8,128)S(1)}, u32[]{:S(2)}, u32[]{:S(2)}) collective-permute-start(f32[8,128]{1,0:T(8,128)S(1)} %get-tuple-element.40.refs_2_), channel_id=1, source_target_pairs={{8,0},{0,8},{24,16},{16,24},{9,1},{1,9},{25,17},{17,25},{10,2},{2,... | collective-permute-start | bytes 12296 | tf_op jit(solution)/shard_map/ppermute | solution.py:43
  40.6 5.8 %collective-permute-start.16 = (f32[72,128]{1,0:T(8,128)S(1)}, f32[72,128]{1,0:T(8,128)S(1)}, u32[]{:S(2)}, u32[]{:S(2)}) collective-permute-start(f32[72,128]{1,0:T(8,128)S(1)} %get-tuple-element.43.refs_1_), channel_id=1, source_target_pairs={{3,0},{2,1},{1,2},{0,3},{7,4},{6,5},{5,6},{4,7},{11,8},{10,9},{9,1... | collective-permute-start | bytes 110600 | tf_op jit(solution)/shard_map/ppermute | solution.py:31
  42.5 5.3 %collective-permute-start.15 = (f32[72,128]{1,0:T(8,128)S(1)}, f32[72,128]{1,0:T(8,128)S(1)}, u32[]{:S(2)}, u32[]{:S(2)}) collective-permute-start(f32[72,128]{1,0:T(8,128)S(1)} %get-tuple-element.43.refs_1_), channel_id=1, source_target_pairs={{2,0},{3,1},{0,2},{1,3},{6,4},{7,5},{4,6},{5,7},{10,8},{11,9},{8,1... | collective-permute-start | bytes 110600 | tf_op jit(solution)/shard_map/ppermute | solution.py:31
  43.2 4.6 %collective-permute-start.14 = (f32[72,128]{1,0:T(8,128)S(1)}, f32[72,128]{1,0:T(8,128)S(1)}, u32[]{:S(2)}, u32[]{:S(2)}) collective-permute-start(f32[72,128]{1,0:T(8,128)S(1)} %get-tuple-element.43.refs_1_), channel_id=1, source_target_pairs={{1,0},{0,1},{3,2},{2,3},{5,4},{4,5},{7,6},{6,7},{9,8},{8,9},{11,10... | collective-permute-start | bytes 110600 | tf_op jit(solution)/shard_map/ppermute | solution.py:31
  49.9 3.7 %collective-permute-start.19 = (f32[8,128]{1,0:T(8,128)S(1)}, f32[8,128]{1,0:T(8,128)S(1)}, u32[]{:S(2)}, u32[]{:S(2)}) collective-permute-start(f32[8,128]{1,0:T(8,128)S(1)} %get-tuple-element.46.refs_2_), channel_id=1, source_target_pairs={{16,0},{24,8},{0,16},{8,24},{17,1},{25,9},{1,17},{9,25},{18,2},{26... | collective-permute-start | bytes 12296 | tf_op jit(solution)/shard_map/ppermute | solution.py:48
  50.9 4.5 %collective-permute-start.18 = (f32[8,128]{1,0:T(8,128)S(1)}, f32[8,128]{1,0:T(8,128)S(1)}, u32[]{:S(2)}, u32[]{:S(2)}) collective-permute-start(f32[8,128]{1,0:T(8,128)S(1)} %get-tuple-element.46.refs_2_), channel_id=1, source_target_pairs={{24,0},{16,8},{8,16},{0,24},{25,1},{17,9},{9,17},{1,25},{26,2},{18... | collective-permute-start | bytes 12296 | tf_op jit(solution)/shard_map/ppermute | solution.py:43
  53.0 3.6 %collective-permute-start.17 = (f32[8,128]{1,0:T(8,128)S(1)}, f32[8,128]{1,0:T(8,128)S(1)}, u32[]{:S(2)}, u32[]{:S(2)}) collective-permute-start(f32[8,128]{1,0:T(8,128)S(1)} %get-tuple-element.46.refs_2_), channel_id=1, source_target_pairs={{8,0},{0,8},{24,16},{16,24},{9,1},{1,9},{25,17},{17,25},{10,2},{2,... | collective-permute-start | bytes 12296 | tf_op jit(solution)/shard_map/ppermute | solution.py:43
  58.1 5.8 %collective-permute-start.22 = (f32[72,128]{1,0:T(8,128)S(1)}, f32[72,128]{1,0:T(8,128)S(1)}, u32[]{:S(2)}, u32[]{:S(2)}) collective-permute-start(f32[72,128]{1,0:T(8,128)S(1)} %get-tuple-element.49.refs_1_), channel_id=1, source_target_pairs={{3,0},{2,1},{1,2},{0,3},{7,4},{6,5},{5,6},{4,7},{11,8},{10,9},{9,1... | collective-permute-start | bytes 110600 | tf_op jit(solution)/shard_map/ppermute | solution.py:31
  60.1 5.0 %collective-permute-start.21 = (f32[72,128]{1,0:T(8,128)S(1)}, f32[72,128]{1,0:T(8,128)S(1)}, u32[]{:S(2)}, u32[]{:S(2)}) collective-permute-start(f32[72,128]{1,0:T(8,128)S(1)} %get-tuple-element.49.refs_1_), channel_id=1, source_target_pairs={{2,0},{3,1},{0,2},{1,3},{6,4},{7,5},{4,6},{5,7},{10,8},{11,9},{8,1... | collective-permute-start | bytes 110600 | tf_op jit(solution)/shard_map/ppermute | solution.py:31
  60.8 4.4 %collective-permute-start.20 = (f32[72,128]{1,0:T(8,128)S(1)}, f32[72,128]{1,0:T(8,128)S(1)}, u32[]{:S(2)}, u32[]{:S(2)}) collective-permute-start(f32[72,128]{1,0:T(8,128)S(1)} %get-tuple-element.49.refs_1_), channel_id=1, source_target_pairs={{1,0},{0,1},{3,2},{2,3},{5,4},{4,5},{7,6},{6,7},{9,8},{8,9},{11,10... | collective-permute-start | bytes 110600 | tf_op jit(solution)/shard_map/ppermute | solution.py:31
  67.3 4.6 %collective-permute-start.24 = (f32[8,128]{1,0:T(8,128)S(1)}, f32[8,128]{1,0:T(8,128)S(1)}, u32[]{:S(2)}, u32[]{:S(2)}) collective-permute-start(f32[8,128]{1,0:T(8,128)S(1)} %get-tuple-element.52.refs_2_), channel_id=1, source_target_pairs={{24,0},{16,8},{8,16},{0,24},{25,1},{17,9},{9,17},{1,25},{26,2},{18... | collective-permute-start | bytes 12296 | tf_op jit(solution)/shard_map/ppermute | solution.py:43
  68.3 3.6 %collective-permute-start.23 = (f32[8,128]{1,0:T(8,128)S(1)}, f32[8,128]{1,0:T(8,128)S(1)}, u32[]{:S(2)}, u32[]{:S(2)}) collective-permute-start(f32[8,128]{1,0:T(8,128)S(1)} %get-tuple-element.52.refs_2_), channel_id=1, source_target_pairs={{8,0},{0,8},{24,16},{16,24},{9,1},{1,9},{25,17},{17,25},{10,2},{2,... | collective-permute-start | bytes 12296 | tf_op jit(solution)/shard_map/ppermute | solution.py:43
  74.0 5.8 %collective-permute-start.27 = (f32[72,128]{1,0:T(8,128)S(1)}, f32[72,128]{1,0:T(8,128)S(1)}, u32[]{:S(2)}, u32[]{:S(2)}) collective-permute-start(f32[72,128]{1,0:T(8,128)S(1)} %get-tuple-element.55.refs_1_), channel_id=1, source_target_pairs={{3,0},{2,1},{1,2},{0,3},{7,4},{6,5},{5,6},{4,7},{11,8},{10,9},{9,1... | collective-permute-start | bytes 110600 | tf_op jit(solution)/shard_map/ppermute | solution.py:31
  75.8 5.2 %collective-permute-start.26 = (f32[72,128]{1,0:T(8,128)S(1)}, f32[72,128]{1,0:T(8,128)S(1)}, u32[]{:S(2)}, u32[]{:S(2)}) collective-permute-start(f32[72,128]{1,0:T(8,128)S(1)} %get-tuple-element.55.refs_1_), channel_id=1, source_target_pairs={{2,0},{3,1},{0,2},{1,3},{6,4},{7,5},{4,6},{5,7},{10,8},{11,9},{8,1... | collective-permute-start | bytes 110600 | tf_op jit(solution)/shard_map/ppermute | solution.py:31
  76.7 4.4 %collective-permute-start.25 = (f32[72,128]{1,0:T(8,128)S(1)}, f32[72,128]{1,0:T(8,128)S(1)}, u32[]{:S(2)}, u32[]{:S(2)}) collective-permute-start(f32[72,128]{1,0:T(8,128)S(1)} %get-tuple-element.55.refs_1_), channel_id=1, source_target_pairs={{1,0},{0,1},{3,2},{2,3},{5,4},{4,5},{7,6},{6,7},{9,8},{8,9},{11,10... | collective-permute-start | bytes 110600 | tf_op jit(solution)/shard_map/ppermute | solution.py:31
  82.0 3.6 %collective-permute-start.30 = (f32[8,128]{1,0:T(8,128)S(1)}, f32[8,128]{1,0:T(8,128)S(1)}, u32[]{:S(2)}, u32[]{:S(2)}) collective-permute-start(f32[8,128]{1,0:T(8,128)S(1)} %get-tuple-element.58.refs_1_), channel_id=1, source_target_pairs={{16,0},{24,8},{0,16},{8,24},{17,1},{25,9},{1,17},{9,25},{18,2},{26... | collective-permute-start | bytes 12296 | tf_op jit(solution)/shard_map/ppermute | solution.py:48
  83.1 4.5 %collective-permute-start.29 = (f32[8,128]{1,0:T(8,128)S(1)}, f32[8,128]{1,0:T(8,128)S(1)}, u32[]{:S(2)}, u32[]{:S(2)}) collective-permute-start(f32[8,128]{1,0:T(8,128)S(1)} %get-tuple-element.58.refs_1_), channel_id=1, source_target_pairs={{24,0},{16,8},{8,16},{0,24},{25,1},{17,9},{9,17},{1,25},{26,2},{18... | collective-permute-start | bytes 12296 | tf_op jit(solution)/shard_map/ppermute | solution.py:43
  84.5 3.6 %collective-permute-start.28 = (f32[8,128]{1,0:T(8,128)S(1)}, f32[8,128]{1,0:T(8,128)S(1)}, u32[]{:S(2)}, u32[]{:S(2)}) collective-permute-start(f32[8,128]{1,0:T(8,128)S(1)} %get-tuple-element.58.refs_1_), channel_id=1, source_target_pairs={{8,0},{0,8},{24,16},{16,24},{9,1},{1,9},{25,17},{17,25},{10,2},{2,... | collective-permute-start | bytes 12296 | tf_op jit(solution)/shard_map/ppermute | solution.py:43
  (1 other events, 4.7 us)

commit v3 on v2

--- a/solution.py
+++ b/solution.py
@@ -12,7 +12,7 @@
 EPSILON = 1e-06
 F32 = jnp.float32
 BF16 = jnp.bfloat16
-FETCH = 51 << 20
+FETCH = 49 << 20
 AWAY = 59 << 20
 FETCHES = 8
 
@@ -138,11 +138,44 @@
     xmsg[4 * cs : 4 * cs + 1, 0 : z.nt] = clist[...].astype(F32)
 
 
-def fetch_kernel(z, tiles_at, tiles, token, sems):
+def two_parts(values):
+    head = values.astype(BF16)
+    return head, (values - head.astype(F32)).astype(BF16)
+
+
+def fetch_kernel(z, tiles_at, tiles, heads, rests, token, sems):
     step = max(z.nt // FETCHES, 1)
     cuts = range(0, z.nt, step)
-    copies([(tiles_at.at[i : i + step], tiles.at[i : i + step]) for i in cuts], sems)
+    started = [
+        pltpu.make_async_copy(tiles_at.at[i : i + step], tiles.at[i : i + step], sems.at[c])
+        for c, i in enumerate(cuts)
+    ]
+    for copy in started:
+        copy.start()
     token[...] = jnp.zeros_like(token)
+    for i, copy in zip(cuts, started):
+        copy.wait()
+        for n in range(i, i + step):
+            heads[n], rests[n] = two_parts(tiles[n])
+
+
+def turn_kernel(z, when, tiles, heads, rests):
+    for n in range(z.nt):
+        heads[n], rests[n] = two_parts(tiles[n].T)
+
+
+def part_rows(values, pairs):
+    head, rest = two_parts(values)
+    count = values.shape[0]
+    pairs[pl.ds(0, count, stride=2), :] = head.astype(F32)
+    pairs[pl.ds(1, count, stride=2), :] = rest.astype(F32)
+
+
+def row_times_tile(pairs, n, heads, rests):
+    row = pairs[2 * n : 2 * n + 2, :].astype(BF16)
+    main = jnp.dot(row, heads[n], preferred_element_type=F32)
+    small = jnp.dot(row, rests[n], preferred_element_type=F32)
+    return main[0:1] + (main[1:2] + small[0:1])
 
 
 def put_list(z, lists, rows, i):
@@ -195,17 +228,26 @@
     return dot(head, right) + (dot(middle, right) + dot(tail, right))
 
 
-def transposed_products(z, y_at, shared, tiles, links, products):
+def transposed_products(z, y_at, shared, tiles, parts, links, products, pairs):
     me = lax.axis_index("col")
+    columns = []
     for j in range(z.nr):
         chosen = onehot(shared[j][3 * z.rows : 3 * z.rows + 1, :], 0, z.nt, z.rows)
-        columns = exact_turned_dot(y_at[j * z.rows : (j + 1) * z.rows, :], chosen)
+        block = y_at[j * z.rows : (j + 1) * z.rows, :]
+        if j == 0:
+            part_rows(exact_turned_dot(chosen, block), pairs)
+            columns.append(None)
+        else:
+            columns.append(exact_turned_dot(block, chosen))
+    for n in range(z.nt):
+        products[n : n + 1, :] = row_times_tile(pairs, n, *parts)
+        for j in range(1, z.nr):
+            k = j * z.nt + n
+            column = columns[j][:, n : n + 1]
+            products[k : k + 1, :] = jnp.sum(tiles[j][n] * column, axis=0, keepdims=True)
+    for j in range(z.nr):
         first = y_at[pl.ds(j * z.rows + me * z.rs, 1), :]
         coupled = jnp.broadcast_to(first, (8, z.tile)).T
-        for n in range(z.nt):
-            k = j * z.nt + n
-            column = columns[:, n : n + 1]
-            products[k : k + 1, :] = jnp.sum(tiles[j][n] * column, axis=0, keepdims=True)
         k = z.listed + j
         link = links[j][z.link : z.link + z.tile, :]
         products[k : k + 1, :] = jnp.sum(link * coupled[:, 0:1], axis=0, keepdims=True)
@@ -242,8 +284,9 @@
 def first_kernel(z, *refs):
     shared, refs = refs[: z.nr], refs[z.nr :]
     halves, refs = refs[: z.nr], refs[z.nr :]
-    tiles, refs = refs[: z.nr], refs[z.nr :]
-    y, xs, g, msg, products = refs
+    tiles, refs = (None, *refs[: z.nr - 1]), refs[z.nr - 1 :]
+    parts, refs = refs[:2], refs[2:]
+    y, xs, g, msg, products, pairs = refs
     row = lax.axis_index("row")
     for j in range(z.nr):
         y[j * z.rows : (j + 1) * z.rows, :] = shared[j][0 : z.rows, :]
@@ -251,7 +294,7 @@
         for part in range(4):
             spot = pl.ds(pl.multiple_of(part * z.xrows + at, 8), z.cs)
             xs[spot, :] = halves[j][part * z.cs : (part + 1) * z.cs, :]
-    transposed_products(z, y, shared, tiles, halves, products)
+    transposed_products(z, y, shared, tiles, parts, halves, products, pairs)
     base = 3 * z.rows + z.row_lists
     sums = [sum(s[base + i : base + i + 1, :] for s in shared) for i in range(2)]
     gradient_part(z, products, halves, g, msg, sums)
@@ -292,10 +335,11 @@
     slots, refs = refs[: z.nc], refs[z.nc :]
     shared, refs = refs[: z.nr], refs[z.nr :]
     halves, refs = refs[: z.nr], refs[z.nr :]
-    tiles, refs = refs[: z.nr], refs[z.nr :]
+    tiles, refs = (None, *refs[: z.nr - 1]), refs[z.nr - 1 :]
+    parts, refs = refs[:2], refs[2:]
     y_old = refs[0]
     y_begin = refs[1] if ends else None
-    y_out, g, msg, products = refs[-4:]
+    y_out, g, msg, products, pairs = refs[-5:]
     dual_part(z, w, slots, shared, y_old, y_out)
     sums = []
     if ends:
@@ -303,7 +347,7 @@
         y_out[...] = mean
         moved = sum(s[z.products : z.products + 1, :] for s in slots)
         sums = [moved, move * jnp.ones((1, z.tile), F32)]
-    transposed_products(z, y_out, shared, tiles, halves, products)
+    transposed_products(z, y_out, shared, tiles, parts, halves, products, pairs)
     gradient_part(z, products, halves, g, msg, sums)
 
 
@@ -339,11 +383,12 @@
     x_old, refs = (None, refs) if first else (refs[0], refs[1:])
     x_begin, refs = (refs[0], refs[1:]) if ends else (None, refs)
     halves, refs = refs[: z.nr], refs[z.nr :]
-    tiles, refs = refs[: z.nr], refs[z.nr :]
+    tiles, refs = (None, *refs[: z.nr - 1]), refs[z.nr - 1 :]
+    parts, refs = refs[:2], refs[2:]
     x_out, zmsg, refs = refs[0], refs[1], refs[2:]
     w_out, refs = (refs[0], refs[1:]) if starts else (None, refs)
     xs_out, refs = (refs[0], refs[1:]) if first else (None, refs)
-    work, v, vectors = refs
+    work, v, vectors, pairs = refs
     period, row = lax.axis_index("period"), lax.axis_index("row")
 
     if starts:
@@ -404,10 +449,16 @@
         count = min(z.tile, z.listed - q * z.tile)
         chosen = onehot(column_lists(z, halves, q), 0, count, z.cols)
         vectors[q * z.tile : q * z.tile + count, :] = exact_turned_dot(chosen, v[0 : z.cols, :])
+    part_rows(vectors[0 : z.nt, :], pairs)
     lane = lax.broadcasted_iota(jnp.int32, (z.tile, z.tile), 1)
+    rows = []
     for b in range(z.blocks):
         columns = jnp.zeros((z.tile, z.tile), F32)
         for k in range(b * z.tile, min((b + 1) * z.tile, z.products)):
+            if k < z.nt:
+                continue
+            if k < 2 * z.nt:
+                rows.append(row_times_tile(pairs, k - z.nt, *parts))
             if k < z.listed:
                 tile = tiles[k // z.nt][k % z.nt]
                 vector = vectors[k : k + 1, :]
@@ -416,23 +467,28 @@
                 vector = v[z.cols + k - z.listed : z.cols + k - z.listed + 1, :]
             column = jnp.sum(tile * vector, axis=1, keepdims=True)
             columns = jnp.where(lane == k % z.tile, column, columns)
-        rows = min(z.zrows - b * z.tile, z.tile)
-        zmsg[b * z.tile : b * z.tile + rows, :] = columns.T[0:rows, :]
+        count = min(z.zrows - b * z.tile, z.tile)
+        zmsg[b * z.tile : b * z.tile + count, :] = columns.T[0:count, :]
+    for n, row_n in enumerate(rows):
+        zmsg[n : n + 1, :] = row_n
     if ends:
         zmsg[z.products : z.products + 1, :] = move * jnp.ones((1, z.tile), F32)
 
 
+def typed(shapes):
+    return [s if isinstance(s[0], tuple) else (s, F32) for s in shapes]
+
+
 def call(z, kernel, operands, shapes, scratch=(), away=0, sems=0, scalar=False, limit=None):
     spaces = [pl.ANY] * away + [pltpu.VMEM] * (len(operands) - away)
-    kinds = [s if isinstance(s, tuple) and isinstance(s[0], tuple) else (s, F32) for s in scratch]
     return pl.pallas_call(
         kernel,
-        out_shape=[jax.ShapeDtypeStruct(s, F32) for s in shapes],
+        out_shape=[jax.ShapeDtypeStruct(s, kind) for s, kind in typed(shapes)],
         in_specs=[pl.BlockSpec(memory_space=s) for s in spaces],
         out_specs=[
             pl.BlockSpec(memory_space=pltpu.SMEM if scalar else pltpu.VMEM) for _ in shapes
         ],
-        scratch_shapes=[pltpu.VMEM(s, kind) for s, kind in kinds]
+        scratch_shapes=[pltpu.VMEM(s, kind) for s, kind in typed(scratch)]
         + ([pltpu.SemaphoreType.DMA((sems,))] if sems else []),
         compiler_params=pltpu.CompilerParams(vmem_limit_bytes=limit or z.limit),
     )(*operands)
@@ -495,11 +551,12 @@
         sems=6,
         limit=AWAY,
     )
-    tiles[0], token = call(
+    block = (listed, tile, tile)
+    own_tiles, heads, rests, token = call(
         z,
         part(fetch_kernel, z),
         (tiles_away,),
-        [(listed, tile, tile), line(8)],
+        [block, (block, BF16), (block, BF16), line(8)],
         away=1,
         sems=FETCHES,
         limit=FETCH,
@@ -513,10 +570,11 @@
     y, xs, g, msg = call(
         z,
         part(first_kernel, z),
-        (*shared, *halves, *tiles),
+        (*shared, *halves, *tiles[1:], heads, rests),
         [line(z.nr * z.rows), line(4 * z.xrows), line(z.xrows), line(z.hop_first)],
-        [products],
-    )
+        [products, line(2 * listed)],
+    )
+    turned = call(z, part(turn_kernel, z), (g, own_tiles), [(block, BF16), (block, BF16)])
     x = None
     weight = None
     y_begin, x_begin = y, None
@@ -526,7 +584,7 @@
         first, last = step == 0, step == ROUNDS * INNER - 1
         got = period_exchange(msg, starts)
         operands = ([] if first else [weight]) + [g, msg, *got, xs]
-        operands += ([] if first else [x]) + ([x_begin] if ends else []) + [*halves, *tiles]
+        operands += ([] if first else [x]) + ([x_begin] if ends else []) + [*halves, *tiles[1:], *turned]
         shapes = [line(z.cs if last else z.xrows), line(z.zrows)]
         shapes += ([line(8)] if starts else []) + ([line(4 * z.xrows)] if first else [])
         outs = call(
@@ -534,7 +592,7 @@
             part(primal_kernel, z, starts, first, ends, last),
             operands,
             shapes,
-            [line(z.xrows), line(z.xrows), line(up(z.listed, 8))],
+            [line(z.xrows), line(z.xrows), line(up(z.listed, 8)), line(2 * listed)],
         )
         x_next, zmsg = outs[:2]
         if starts:
@@ -548,13 +606,13 @@
         slots = exchange(zmsg, "col")
         if last:
             break
-        operands = [weight, *slots, *shared, *halves, *tiles, y]
+        operands = [weight, *slots, *shared, *halves, *tiles[1:], heads, rests, y]
         y_next, g, msg = call(
             z,
             part(dual_kernel, z, ends),
             operands + ([y_begin] if ends else []),
             [line(z.nr * z.rows), line(z.xrows), line(z.hop)],
-            [products],
+            [products, line(2 * listed)],
         )
         y = y_next
         if ends:

time: 89 us -> 84.7 us (0.952)
  Pallas kernels: 21.2 us -> 17.5 us
    pallas_call x14 -> x15, Pallas kernels: 21.2 us -> 17.5 us  [call(): pl.pallas_call(kernel, out_shape=[jax.ShapeDtypeStruct(s, kind) for s, ki...]
  transfers between devices with their start and end apart: 31 -> 31, of which waited for: 23 -> 22; matrix products, arithmetic and copies ran while one was open for 0% -> 0% of each run, Pallas kernels for 6% -> 7%
where the time goes in v3:
time: 84.7 us; the launch traced here: 84.5 us
  starting transfers between devices  39.4 us (47%)
  waiting for transfers between devices  26.7 us (32%)
  Pallas kernels  17.5 us (21%)
    ppermute x18, starting transfers between devices, from_peer(): return lax.ppermute(x, axis, pairs)  23.7 us
    pallas_call x15, Pallas kernels, call(): pl.pallas_call(kernel, out_shape=[jax.ShapeDtypeStruct(s, kind) for s, ki...  17.5 us
    ppermute x18, waiting for transfers between devices, from_peer(): return lax.ppermute(x, axis, pairs)  13.9 us
    ppermute x10, waiting for transfers between devices, period_exchange(): lax.ppermute(x, 'period', [(m[i], i) for i in range(n)])  12.6 us
    ppermute x10, starting transfers between devices, period_exchange(): lax.ppermute(x, 'period', [(m[i], i) for i in range(n)])  12 us
    ppermute x3, starting transfers between devices, period_exchange(): lax.ppermute(x, 'period', [((i + s) % n, i) for i in range(n)])  3.67 us
  transfers between devices with their start and end apart: 31, of which 22 were waited for; matrix products, arithmetic and copies ran while one was open for 0% of the time, Pallas kernels for 7%

profile of v3, /device:TPU:0, one launch (start us, length us, event | category | flops | bytes accessed | tf_op | source)
XLA Modules:
  0.0 84.5 jit_solution(17721716948013222253)
XLA Ops:
  1.1 1.6 %shard_map.131.refs_1_ = f32[104,128]{1,0:T(8,128)} custom-call(f32[32,128]{1,0:T(8,128)} %dual_at.1, f32[32,128]{1,0:T(8,128)} %rhs_at.1, s32[32,128]{1,0:T(8,128)} %rkind_at.1, f32[64,128]{1,0:T(8,128)} %obj_at.3, s32[1,32]{1,0:T(1,128)} %bitcast.8), custom_call_target="tpu_custom_call" | custom-call | tf_op jit(solution)/shard_map/pallas_call | solution.py:484
  2.7 4.7 %collective-permute-start.2 = (f32[104,128]{1,0:T(8,128)}, f32[104,128]{1,0:T(8,128)S(1)}, u32[]{:S(2)}, u32[]{:S(2)}) collective-permute-start(f32[104,128]{1,0:T(8,128)} %shard_map.131.refs_1_), channel_id=1, source_target_pairs={{3,0},{2,1},{1,2},{0,3},{7,4},{6,5},{5,6},{4,7},{11,8},{10,9},{9,1... | collective-permute-start | bytes 159752 | tf_op jit(solution)/shard_map/ppermute | solution.py:31
  8.1 1.7 %shard_map.133.refs_2_.refs_6_.refs_7_.refs_8_ = f32[392,128]{1,0:T(8,128)} custom-call(f32[64,128]{1,0:T(8,128)} %x_at.1, f32[64,128]{1,0:T(8,128)} %obj_at.3, f32[64,128]{1,0:T(8,128)} %ub_at.1, s32[64,128]{1,0:T(8,128)} %ckind_at.1, s32[1,32]{1,0:T(1,128)} %bitcast.9, f32[128,128]{1,0:T(8,128)} %bitcast.7), custom_call_target="tpu_custom_call" | custom-call | tf_op jit(solution)/shard_map/pallas_call | solution.py:484
  9.8 1.6 %shard_map.130 = (f32[32,128,128]{2,1,0:T(8,128)S(1)}, bf16[32,128,128]{2,1,0:T(8,128)(2,1)S(1)}, bf16[32,128,128]{2,1,0:T(8,128)(2,1)S(1)}, f32[8,128]{1,0:T(8,128)S(1)}) custom-call(f32[32,128,128]{2,1,0:T(8,128)} %bitcast.6), custom_call_target="tpu_custom_call" | custom-call | tf_op jit(solution)/shard_map/pallas_call | solution.py:484
  11.5 1.4 %collective-permute-done.1.refs_3_ = f32[104,128]{1,0:T(8,128)S(1)} collective-permute-done((f32[104,128]{1,0:T(8,128)}, f32[104,128]{1,0:T(8,128)S(1)}, u32[]{:S(2)}, u32[]{:S(2)}) %collective-permute-start.1) | collective-permute-done | bytes 53280 | tf_op jit(solution)/shard_map/ppermute | solution.py:31
  13.0 1.4 %collective-permute-done.3.refs_1_.refs_6_ = f32[392,128]{1,0:T(8,128)S(1)} collective-permute-done((f32[392,128]{1,0:T(8,128)S(1)}, f32[392,128]{1,0:T(8,128)S(1)}, u32[]{:S(2)}, u32[]{:S(2)}) %collective-permute-start.3) | collective-permute-done | bytes 200736 | tf_op jit(solution)/shard_map/ppermute | solution.py:31
  15.7 1.6 %collective-permute-start.8 = (f32[16,128]{1,0:T(8,128)S(1)}, f32[16,128]{1,0:T(8,128)S(1)}, u32[]{:S(2)}, u32[]{:S(2)}) collective-permute-start(f32[16,128]{1,0:T(8,128)S(1)} %get-tuple-element.39.refs_1_), channel_id=1, source_target_pairs={{16,0},{24,8},{0,16},{8,24},{17,1},{25,9},{1,17},{9,25},{18,2},{26... | collective-permute-start | bytes 24584 | tf_op jit(solution)/shard_map/ppermute | solution.py:48
  17.3 1.4 %collective-permute-start.7 = (f32[16,128]{1,0:T(8,128)S(1)}, f32[16,128]{1,0:T(8,128)S(1)}, u32[]{:S(2)}, u32[]{:S(2)}) collective-permute-start(f32[16,128]{1,0:T(8,128)S(1)} %get-tuple-element.39.refs_1_), channel_id=1, source_target_pairs={{24,0},{16,8},{8,16},{0,24},{25,1},{17,9},{9,17},{1,25},{26,2},{18... | collective-permute-start | bytes 24584 | tf_op jit(solution)/shard_map/ppermute | solution.py:43
  19.9 2.0 %collective-permute-done.7.refs_3_ = f32[16,128]{1,0:T(8,128)S(1)} collective-permute-done((f32[16,128]{1,0:T(8,128)S(1)}, f32[16,128]{1,0:T(8,128)S(1)}, u32[]{:S(2)}, u32[]{:S(2)}) %collective-permute-start.7) | collective-permute-done | bytes 8224 | tf_op jit(solution)/shard_map/ppermute | solution.py:43
  23.4 2.5 %collective-permute-start.11 = (f32[72,128]{1,0:T(8,128)S(1)}, f32[72,128]{1,0:T(8,128)S(1)}, u32[]{:S(2)}, u32[]{:S(2)}) collective-permute-start(f32[72,128]{1,0:T(8,128)S(1)} %get-tuple-element.45.refs_1_), channel_id=1, source_target_pairs={{3,0},{2,1},{1,2},{0,3},{7,4},{6,5},{5,6},{4,7},{11,8},{10,9},{9,1... | collective-permute-start | bytes 110600 | tf_op jit(solution)/shard_map/ppermute | solution.py:31
  26.2 1.6 %collective-permute-start.9 = (f32[72,128]{1,0:T(8,128)S(1)}, f32[72,128]{1,0:T(8,128)S(1)}, u32[]{:S(2)}, u32[]{:S(2)}) collective-permute-start(f32[72,128]{1,0:T(8,128)S(1)} %get-tuple-element.45.refs_1_), channel_id=1, source_target_pairs={{1,0},{0,1},{3,2},{2,3},{5,4},{4,5},{7,6},{6,7},{9,8},{8,9},{11,10... | collective-permute-start | bytes 110600 | tf_op jit(solution)/shard_map/ppermute | solution.py:31
  27.8 1.6 %collective-permute-done.11.refs_4_ = f32[72,128]{1,0:T(8,128)S(1)} collective-permute-done((f32[72,128]{1,0:T(8,128)S(1)}, f32[72,128]{1,0:T(8,128)S(1)}, u32[]{:S(2)}, u32[]{:S(2)}) %collective-permute-start.11) | collective-permute-done | bytes 36896 | tf_op jit(solution)/shard_map/ppermute | solution.py:31
  30.8 1.6 %shard_map.137 = (f32[256,128]{1,0:T(8,128)S(1)}, f32[136,128]{1,0:T(8,128)S(1)}, f32[8,128]{1,0:T(8,128)S(1)}) custom-call(f32[8,128]{1,0:T(8,128)S(1)} %get-tuple-element.44.refs_0_, f32[72,128]{1,0:T(8,128)S(1)} %get-tuple-element.45.refs_1_, f32[72,128]{1,0:T(8,128)S(1)} %collective-permute-done.9.refs_2_, ...), custom_call_target="tpu_custom_call" | custom-call | tf_op jit(solution)/shard_map/pallas_call | solution.py:484
  32.3 1.6 %collective-permute-start.13 = (f32[8,128]{1,0:T(8,128)S(1)}, f32[8,128]{1,0:T(8,128)S(1)}, u32[]{:S(2)}, u32[]{:S(2)}) collective-permute-start(f32[8,128]{1,0:T(8,128)S(1)} %get-tuple-element.48.refs_2_), channel_id=1, source_target_pairs={{24,0},{16,8},{8,16},{0,24},{25,1},{17,9},{9,17},{1,25},{26,2},{18... | collective-permute-start | bytes 12296 | tf_op jit(solution)/shard_map/ppermute | solution.py:43
  33.9 1.5 %collective-permute-start.12 = (f32[8,128]{1,0:T(8,128)S(1)}, f32[8,128]{1,0:T(8,128)S(1)}, u32[]{:S(2)}, u32[]{:S(2)}) collective-permute-start(f32[8,128]{1,0:T(8,128)S(1)} %get-tuple-element.48.refs_2_), channel_id=1, source_target_pairs={{8,0},{0,8},{24,16},{16,24},{9,1},{1,9},{25,17},{17,25},{10,2},{2,... | collective-permute-start | bytes 12296 | tf_op jit(solution)/shard_map/ppermute | solution.py:43
  35.4 1.5 %collective-permute-done.13.refs_4_ = f32[8,128]{1,0:T(8,128)S(1)} collective-permute-done((f32[8,128]{1,0:T(8,128)S(1)}, f32[8,128]{1,0:T(8,128)S(1)}, u32[]{:S(2)}, u32[]{:S(2)}) %collective-permute-start.13) | collective-permute-done | bytes 4128 | tf_op jit(solution)/shard_map/ppermute | solution.py:43
  38.5 1.9 %collective-permute-start.16 = (f32[72,128]{1,0:T(8,128)S(1)}, f32[72,128]{1,0:T(8,128)S(1)}, u32[]{:S(2)}, u32[]{:S(2)}) collective-permute-start(f32[72,128]{1,0:T(8,128)S(1)} %get-tuple-element.51.refs_1_), channel_id=1, source_target_pairs={{3,0},{2,1},{1,2},{0,3},{7,4},{6,5},{5,6},{4,7},{11,8},{10,9},{9,1... | collective-permute-start | bytes 110600 | tf_op jit(solution)/shard_map/ppermute | solution.py:31
  41.1 1.9 %collective-permute-start.14 = (f32[72,128]{1,0:T(8,128)S(1)}, f32[72,128]{1,0:T(8,128)S(1)}, u32[]{:S(2)}, u32[]{:S(2)}) collective-permute-start(f32[72,128]{1,0:T(8,128)S(1)} %get-tuple-element.51.refs_1_), channel_id=1, source_target_pairs={{1,0},{0,1},{3,2},{2,3},{5,4},{4,5},{7,6},{6,7},{9,8},{8,9},{11,10... | collective-permute-start | bytes 110600 | tf_op jit(solution)/shard_map/ppermute | solution.py:31
  43.0 1.4 %collective-permute-done.16.refs_4_ = f32[72,128]{1,0:T(8,128)S(1)} collective-permute-done((f32[72,128]{1,0:T(8,128)S(1)}, f32[72,128]{1,0:T(8,128)S(1)}, u32[]{:S(2)}, u32[]{:S(2)}) %collective-permute-start.16) | collective-permute-done | bytes 36896 | tf_op jit(solution)/shard_map/ppermute | solution.py:31
  45.7 1.6 %shard_map.139 = (f32[256,128]{1,0:T(8,128)S(1)}, f32[136,128]{1,0:T(8,128)S(1)}, f32[8,128]{1,0:T(8,128)S(1)}) custom-call(f32[8,128]{1,0:T(8,128)S(1)} %get-tuple-element.44.refs_0_, f32[72,128]{1,0:T(8,128)S(1)} %get-tuple-element.51.refs_1_, f32[72,128]{1,0:T(8,128)S(1)} %collective-permute-done.14.refs_2_, ...), custom_call_target="tpu_custom_call" | custom-call | tf_op jit(solution)/shard_map/pallas_call | solution.py:484
  48.3 2.0 %collective-permute-start.18 = (f32[8,128]{1,0:T(8,128)S(1)}, f32[8,128]{1,0:T(8,128)S(1)}, u32[]{:S(2)}, u32[]{:S(2)}) collective-permute-start(f32[8,128]{1,0:T(8,128)S(1)} %get-tuple-element.54.refs_2_), channel_id=1, source_target_pairs={{24,0},{16,8},{8,16},{0,24},{25,1},{17,9},{9,17},{1,25},{26,2},{18... | collective-permute-start | bytes 12296 | tf_op jit(solution)/shard_map/ppermute | solution.py:43
  50.9 1.8 %collective-permute-done.18.refs_4_ = f32[8,128]{1,0:T(8,128)S(1)} collective-permute-done((f32[8,128]{1,0:T(8,128)S(1)}, f32[8,128]{1,0:T(8,128)S(1)}, u32[]{:S(2)}, u32[]{:S(2)}) %collective-permute-start.18) | collective-permute-done | bytes 4128 | tf_op jit(solution)/shard_map/ppermute | solution.py:43
  54.9 2.0 %collective-permute-start.22 = (f32[72,128]{1,0:T(8,128)S(1)}, f32[72,128]{1,0:T(8,128)S(1)}, u32[]{:S(2)}, u32[]{:S(2)}) collective-permute-start(f32[72,128]{1,0:T(8,128)S(1)} %get-tuple-element.57.refs_1_), channel_id=1, source_target_pairs={{3,0},{2,1},{1,2},{0,3},{7,4},{6,5},{5,6},{4,7},{11,8},{10,9},{9,1... | collective-permute-start | bytes 110600 | tf_op jit(solution)/shard_map/ppermute | solution.py:31
  57.7 1.7 %collective-permute-start.20 = (f32[72,128]{1,0:T(8,128)S(1)}, f32[72,128]{1,0:T(8,128)S(1)}, u32[]{:S(2)}, u32[]{:S(2)}) collective-permute-start(f32[72,128]{1,0:T(8,128)S(1)} %get-tuple-element.57.refs_1_), channel_id=1, source_target_pairs={{1,0},{0,1},{3,2},{2,3},{5,4},{4,5},{7,6},{6,7},{9,8},{8,9},{11,10... | collective-permute-start | bytes 110600 | tf_op jit(solution)/shard_map/ppermute | solution.py:31
  59.4 1.4 %collective-permute-done.22.refs_4_ = f32[72,128]{1,0:T(8,128)S(1)} collective-permute-done((f32[72,128]{1,0:T(8,128)S(1)}, f32[72,128]{1,0:T(8,128)S(1)}, u32[]{:S(2)}, u32[]{:S(2)}) %collective-permute-start.22) | collective-permute-done | bytes 36896 | tf_op jit(solution)/shard_map/ppermute | solution.py:31
  62.0 1.6 %shard_map.141 = (f32[256,128]{1,0:T(8,128)S(1)}, f32[136,128]{1,0:T(8,128)S(1)}, f32[8,128]{1,0:T(8,128)S(1)}) custom-call(f32[8,128]{1,0:T(8,128)S(1)} %get-tuple-element.56.refs_0_, f32[72,128]{1,0:T(8,128)S(1)} %get-tuple-element.57.refs_1_, f32[72,128]{1,0:T(8,128)S(1)} %collective-permute-done.20.refs_2_, ...), custom_call_target="tpu_custom_call" | custom-call | tf_op jit(solution)/shard_map/pallas_call | solution.py:484
  65.6 2.5 %collective-permute-done.24.refs_4_ = f32[8,128]{1,0:T(8,128)S(1)} collective-permute-done((f32[8,128]{1,0:T(8,128)S(1)}, f32[8,128]{1,0:T(8,128)S(1)}, u32[]{:S(2)}, u32[]{:S(2)}) %collective-permute-start.24) | collective-permute-done | bytes 4128 | tf_op jit(solution)/shard_map/ppermute | solution.py:43
  68.2 1.5 %shard_map.142 = (f32[64,128]{1,0:T(8,128)}, f32[72,128]{1,0:T(8,128)S(1)}) custom-call(f32[8,128]{1,0:T(8,128)S(1)} %get-tuple-element.56.refs_0_, f32[136,128]{1,0:T(8,128)S(1)} %get-tuple-element.59.refs_1_, f32[8,128]{1,0:T(8,128)S(1)} %get-tuple-element.60.refs_2_, f32[8,128]{1,0:T(8,128)S(1)} %collective-permute-done.23.refs_3_, ...), custom_call_target="tpu_custom_call" | custom-call | tf_op jit(solution)/shard_map/pallas_call | solution.py:484
  69.7 1.9 %collective-permute-start.27 = (f32[72,128]{1,0:T(8,128)S(1)}, f32[72,128]{1,0:T(8,128)S(1)}, u32[]{:S(2)}, u32[]{:S(2)}) collective-permute-start(f32[72,128]{1,0:T(8,128)S(1)} %get-tuple-element.63.refs_1_), channel_id=1, source_target_pairs={{3,0},{2,1},{1,2},{0,3},{7,4},{6,5},{5,6},{4,7},{11,8},{10,9},{9,1... | collective-permute-start | bytes 110600 | tf_op jit(solution)/shard_map/ppermute | solution.py:31
  72.5 1.6 %collective-permute-start.25 = (f32[72,128]{1,0:T(8,128)S(1)}, f32[72,128]{1,0:T(8,128)S(1)}, u32[]{:S(2)}, u32[]{:S(2)}) collective-permute-start(f32[72,128]{1,0:T(8,128)S(1)} %get-tuple-element.63.refs_1_), channel_id=1, source_target_pairs={{1,0},{0,1},{3,2},{2,3},{5,4},{4,5},{7,6},{6,7},{9,8},{8,9},{11,10... | collective-permute-start | bytes 110600 | tf_op jit(solution)/shard_map/ppermute | solution.py:31
  78.8 1.4 %collective-permute-start.29 = (f32[8,128]{1,0:T(8,128)S(1)}, f32[8,128]{1,0:T(8,128)S(1)}, u32[]{:S(2)}, u32[]{:S(2)}) collective-permute-start(f32[8,128]{1,0:T(8,128)S(1)} %get-tuple-element.66.refs_1_), channel_id=1, source_target_pairs={{24,0},{16,8},{8,16},{0,24},{25,1},{17,9},{9,17},{1,25},{26,2},{18... | collective-permute-start | bytes 12296 | tf_op jit(solution)/shard_map/ppermute | solution.py:43
  81.3 2.0 %collective-permute-done.29.refs_3_ = f32[8,128]{1,0:T(8,128)S(1)} collective-permute-done((f32[8,128]{1,0:T(8,128)S(1)}, f32[8,128]{1,0:T(8,128)S(1)}, u32[]{:S(2)}, u32[]{:S(2)}) %collective-permute-start.29) | collective-permute-done | bytes 4128 | tf_op jit(solution)/shard_map/ppermute | solution.py:43
  (50 shorter events, 26.1 us)
Async XLA Ops:
  0.6 13.8 %collective-permute-start.5 = (f32[32,128,128]{2,1,0:T(8,128)}, f32[32,128,128]{2,1,0:T(8,128)S(1)}, u32[]{:S(2)}, u32[]{:S(2)}) collective-permute-start(f32[32,128,128]{2,1,0:T(8,128)} %bitcast.5), channel_id=1, source_target_pairs={{4,0},{0,4},{5,1},{1,5},{6,2},{2,6},{7,3},{3,7},{12,8},{8,12},{13,... | collective-permute-start | bytes 6291464 | tf_op jit(solution)/shard_map/ppermute | solution.py:31
  2.7 10.2 %copy-start.1 = (f32[104,128]{1,0:T(8,128)S(1)}, f32[104,128]{1,0:T(8,128)}, u32[]{:S(2)}) copy-start(f32[104,128]{1,0:T(8,128)} %shard_map.131.refs_1_) | copy-start | bytes 159748
  2.7 8.7 %collective-permute-start.2 = (f32[104,128]{1,0:T(8,128)}, f32[104,128]{1,0:T(8,128)S(1)}, u32[]{:S(2)}, u32[]{:S(2)}) collective-permute-start(f32[104,128]{1,0:T(8,128)} %shard_map.131.refs_1_), channel_id=1, source_target_pairs={{3,0},{2,1},{1,2},{0,3},{7,4},{6,5},{5,6},{4,7},{11,8},{10,9},{9,1... | collective-permute-start | bytes 159752 | tf_op jit(solution)/shard_map/ppermute | solution.py:31
  7.4 5.5 %collective-permute-start.1 = (f32[104,128]{1,0:T(8,128)}, f32[104,128]{1,0:T(8,128)S(1)}, u32[]{:S(2)}, u32[]{:S(2)}) collective-permute-start(f32[104,128]{1,0:T(8,128)} %shard_map.131.refs_1_), channel_id=1, source_target_pairs={{2,0},{3,1},{0,2},{1,3},{6,4},{7,5},{4,6},{5,7},{10,8},{11,9},{8,1... | collective-permute-start | bytes 159752 | tf_op jit(solution)/shard_map/ppermute | solution.py:31
  7.4 5.5 %collective-permute-start = (f32[104,128]{1,0:T(8,128)}, f32[104,128]{1,0:T(8,128)S(1)}, u32[]{:S(2)}, u32[]{:S(2)}) collective-permute-start(f32[104,128]{1,0:T(8,128)} %shard_map.131.refs_1_), channel_id=1, source_target_pairs={{1,0},{0,1},{3,2},{2,3},{5,4},{4,5},{7,6},{6,7},{9,8},{8,9},{11,10... | collective-permute-start | bytes 159752 | tf_op jit(solution)/shard_map/ppermute | solution.py:31
  9.8 3.3 %collective-permute-start.4 = (f32[392,128]{1,0:T(8,128)}, f32[392,128]{1,0:T(8,128)S(1)}, u32[]{:S(2)}, u32[]{:S(2)}) collective-permute-start(f32[392,128]{1,0:T(8,128)} %shard_map.133.refs_2_.refs_6_.refs_7_.refs_8_), channel_id=1, source_target_pairs={{4,0},{0,4},{5,1},{1,5},{6,2},{2,6},{7,3},{3,7},{12,8},{8,12},{13,... | collective-permute-start | bytes 602120 | tf_op jit(solution)/shard_map/ppermute | solution.py:31
  13.0 1.5 %collective-permute-start.3 = (f32[392,128]{1,0:T(8,128)S(1)}, f32[392,128]{1,0:T(8,128)S(1)}, u32[]{:S(2)}, u32[]{:S(2)}) collective-permute-start(f32[392,128]{1,0:T(8,128)S(1)} %shard_map.132.refs_0_.refs_5_), channel_id=1, source_target_pairs={{4,0},{0,4},{5,1},{1,5},{6,2},{2,6},{7,3},{3,7},{12,8},{8,12},{13,... | collective-permute-start | bytes 602120 | tf_op jit(solution)/shard_map/ppermute | solution.py:31
  15.7 4.2 %collective-permute-start.8 = (f32[16,128]{1,0:T(8,128)S(1)}, f32[16,128]{1,0:T(8,128)S(1)}, u32[]{:S(2)}, u32[]{:S(2)}) collective-permute-start(f32[16,128]{1,0:T(8,128)S(1)} %get-tuple-element.39.refs_1_), channel_id=1, source_target_pairs={{16,0},{24,8},{0,16},{8,24},{17,1},{25,9},{1,17},{9,25},{18,2},{26... | collective-permute-start | bytes 24584 | tf_op jit(solution)/shard_map/ppermute | solution.py:48
  17.3 4.5 %collective-permute-start.7 = (f32[16,128]{1,0:T(8,128)S(1)}, f32[16,128]{1,0:T(8,128)S(1)}, u32[]{:S(2)}, u32[]{:S(2)}) collective-permute-start(f32[16,128]{1,0:T(8,128)S(1)} %get-tuple-element.39.refs_1_), channel_id=1, source_target_pairs={{24,0},{16,8},{8,16},{0,24},{25,1},{17,9},{9,17},{1,25},{26,2},{18... | collective-permute-start | bytes 24584 | tf_op jit(solution)/shard_map/ppermute | solution.py:43
  18.7 3.7 %collective-permute-start.6 = (f32[16,128]{1,0:T(8,128)S(1)}, f32[16,128]{1,0:T(8,128)S(1)}, u32[]{:S(2)}, u32[]{:S(2)}) collective-permute-start(f32[16,128]{1,0:T(8,128)S(1)} %get-tuple-element.39.refs_1_), channel_id=1, source_target_pairs={{8,0},{0,8},{24,16},{16,24},{9,1},{1,9},{25,17},{17,25},{10,2},{2,... | collective-permute-start | bytes 24584 | tf_op jit(solution)/shard_map/ppermute | solution.py:43
  23.4 6.1 %collective-permute-start.11 = (f32[72,128]{1,0:T(8,128)S(1)}, f32[72,128]{1,0:T(8,128)S(1)}, u32[]{:S(2)}, u32[]{:S(2)}) collective-permute-start(f32[72,128]{1,0:T(8,128)S(1)} %get-tuple-element.45.refs_1_), channel_id=1, source_target_pairs={{3,0},{2,1},{1,2},{0,3},{7,4},{6,5},{5,6},{4,7},{11,8},{10,9},{9,1... | collective-permute-start | bytes 110600 | tf_op jit(solution)/shard_map/ppermute | solution.py:31
  25.9 4.9 %collective-permute-start.10 = (f32[72,128]{1,0:T(8,128)S(1)}, f32[72,128]{1,0:T(8,128)S(1)}, u32[]{:S(2)}, u32[]{:S(2)}) collective-permute-start(f32[72,128]{1,0:T(8,128)S(1)} %get-tuple-element.45.refs_1_), channel_id=1, source_target_pairs={{2,0},{3,1},{0,2},{1,3},{6,4},{7,5},{4,6},{5,7},{10,8},{11,9},{8,1... | collective-permute-start | bytes 110600 | tf_op jit(solution)/shard_map/ppermute | solution.py:31
  26.2 4.6 %collective-permute-start.9 = (f32[72,128]{1,0:T(8,128)S(1)}, f32[72,128]{1,0:T(8,128)S(1)}, u32[]{:S(2)}, u32[]{:S(2)}) collective-permute-start(f32[72,128]{1,0:T(8,128)S(1)} %get-tuple-element.45.refs_1_), channel_id=1, source_target_pairs={{1,0},{0,1},{3,2},{2,3},{5,4},{4,5},{7,6},{6,7},{9,8},{8,9},{11,10... | collective-permute-start | bytes 110600 | tf_op jit(solution)/shard_map/ppermute | solution.py:31
  32.3 4.6 %collective-permute-start.13 = (f32[8,128]{1,0:T(8,128)S(1)}, f32[8,128]{1,0:T(8,128)S(1)}, u32[]{:S(2)}, u32[]{:S(2)}) collective-permute-start(f32[8,128]{1,0:T(8,128)S(1)} %get-tuple-element.48.refs_2_), channel_id=1, source_target_pairs={{24,0},{16,8},{8,16},{0,24},{25,1},{17,9},{9,17},{1,25},{26,2},{18... | collective-permute-start | bytes 12296 | tf_op jit(solution)/shard_map/ppermute | solution.py:43
  33.9 3.6 %collective-permute-start.12 = (f32[8,128]{1,0:T(8,128)S(1)}, f32[8,128]{1,0:T(8,128)S(1)}, u32[]{:S(2)}, u32[]{:S(2)}) collective-permute-start(f32[8,128]{1,0:T(8,128)S(1)} %get-tuple-element.48.refs_2_), channel_id=1, source_target_pairs={{8,0},{0,8},{24,16},{16,24},{9,1},{1,9},{25,17},{17,25},{10,2},{2,... | collective-permute-start | bytes 12296 | tf_op jit(solution)/shard_map/ppermute | solution.py:43
  38.5 5.8 %collective-permute-start.16 = (f32[72,128]{1,0:T(8,128)S(1)}, f32[72,128]{1,0:T(8,128)S(1)}, u32[]{:S(2)}, u32[]{:S(2)}) collective-permute-start(f32[72,128]{1,0:T(8,128)S(1)} %get-tuple-element.51.refs_1_), channel_id=1, source_target_pairs={{3,0},{2,1},{1,2},{0,3},{7,4},{6,5},{5,6},{4,7},{11,8},{10,9},{9,1... | collective-permute-start | bytes 110600 | tf_op jit(solution)/shard_map/ppermute | solution.py:31
  40.4 5.3 %collective-permute-start.15 = (f32[72,128]{1,0:T(8,128)S(1)}, f32[72,128]{1,0:T(8,128)S(1)}, u32[]{:S(2)}, u32[]{:S(2)}) collective-permute-start(f32[72,128]{1,0:T(8,128)S(1)} %get-tuple-element.51.refs_1_), channel_id=1, source_target_pairs={{2,0},{3,1},{0,2},{1,3},{6,4},{7,5},{4,6},{5,7},{10,8},{11,9},{8,1... | collective-permute-start | bytes 110600 | tf_op jit(solution)/shard_map/ppermute | solution.py:31
  41.1 4.6 %collective-permute-start.14 = (f32[72,128]{1,0:T(8,128)S(1)}, f32[72,128]{1,0:T(8,128)S(1)}, u32[]{:S(2)}, u32[]{:S(2)}) collective-permute-start(f32[72,128]{1,0:T(8,128)S(1)} %get-tuple-element.51.refs_1_), channel_id=1, source_target_pairs={{1,0},{0,1},{3,2},{2,3},{5,4},{4,5},{7,6},{6,7},{9,8},{8,9},{11,10... | collective-permute-start | bytes 110600 | tf_op jit(solution)/shard_map/ppermute | solution.py:31
  47.3 3.7 %collective-permute-start.19 = (f32[8,128]{1,0:T(8,128)S(1)}, f32[8,128]{1,0:T(8,128)S(1)}, u32[]{:S(2)}, u32[]{:S(2)}) collective-permute-start(f32[8,128]{1,0:T(8,128)S(1)} %get-tuple-element.54.refs_2_), channel_id=1, source_target_pairs={{16,0},{24,8},{0,16},{8,24},{17,1},{25,9},{1,17},{9,25},{18,2},{26... | collective-permute-start | bytes 12296 | tf_op jit(solution)/shard_map/ppermute | solution.py:48
  48.3 4.5 %collective-permute-start.18 = (f32[8,128]{1,0:T(8,128)S(1)}, f32[8,128]{1,0:T(8,128)S(1)}, u32[]{:S(2)}, u32[]{:S(2)}) collective-permute-start(f32[8,128]{1,0:T(8,128)S(1)} %get-tuple-element.54.refs_2_), channel_id=1, source_target_pairs={{24,0},{16,8},{8,16},{0,24},{25,1},{17,9},{9,17},{1,25},{26,2},{18... | collective-permute-start | bytes 12296 | tf_op jit(solution)/shard_map/ppermute | solution.py:43
  50.3 3.6 %collective-permute-start.17 = (f32[8,128]{1,0:T(8,128)S(1)}, f32[8,128]{1,0:T(8,128)S(1)}, u32[]{:S(2)}, u32[]{:S(2)}) collective-permute-start(f32[8,128]{1,0:T(8,128)S(1)} %get-tuple-element.54.refs_2_), channel_id=1, source_target_pairs={{8,0},{0,8},{24,16},{16,24},{9,1},{1,9},{25,17},{17,25},{10,2},{2,... | collective-permute-start | bytes 12296 | tf_op jit(solution)/shard_map/ppermute | solution.py:43
  54.9 5.8 %collective-permute-start.22 = (f32[72,128]{1,0:T(8,128)S(1)}, f32[72,128]{1,0:T(8,128)S(1)}, u32[]{:S(2)}, u32[]{:S(2)}) collective-permute-start(f32[72,128]{1,0:T(8,128)S(1)} %get-tuple-element.57.refs_1_), channel_id=1, source_target_pairs={{3,0},{2,1},{1,2},{0,3},{7,4},{6,5},{5,6},{4,7},{11,8},{10,9},{9,1... | collective-permute-start | bytes 110600 | tf_op jit(solution)/shard_map/ppermute | solution.py:31
  56.9 5.0 %collective-permute-start.21 = (f32[72,128]{1,0:T(8,128)S(1)}, f32[72,128]{1,0:T(8,128)S(1)}, u32[]{:S(2)}, u32[]{:S(2)}) collective-permute-start(f32[72,128]{1,0:T(8,128)S(1)} %get-tuple-element.57.refs_1_), channel_id=1, source_target_pairs={{2,0},{3,1},{0,2},{1,3},{6,4},{7,5},{4,6},{5,7},{10,8},{11,9},{8,1... | collective-permute-start | bytes 110600 | tf_op jit(solution)/shard_map/ppermute | solution.py:31
  57.7 4.4 %collective-permute-start.20 = (f32[72,128]{1,0:T(8,128)S(1)}, f32[72,128]{1,0:T(8,128)S(1)}, u32[]{:S(2)}, u32[]{:S(2)}) collective-permute-start(f32[72,128]{1,0:T(8,128)S(1)} %get-tuple-element.57.refs_1_), channel_id=1, source_target_pairs={{1,0},{0,1},{3,2},{2,3},{5,4},{4,5},{7,6},{6,7},{9,8},{8,9},{11,10... | collective-permute-start | bytes 110600 | tf_op jit(solution)/shard_map/ppermute | solution.py:31
  63.6 4.6 %collective-permute-start.24 = (f32[8,128]{1,0:T(8,128)S(1)}, f32[8,128]{1,0:T(8,128)S(1)}, u32[]{:S(2)}, u32[]{:S(2)}) collective-permute-start(f32[8,128]{1,0:T(8,128)S(1)} %get-tuple-element.60.refs_2_), channel_id=1, source_target_pairs={{24,0},{16,8},{8,16},{0,24},{25,1},{17,9},{9,17},{1,25},{26,2},{18... | collective-permute-start | bytes 12296 | tf_op jit(solution)/shard_map/ppermute | solution.py:43
  64.6 3.6 %collective-permute-start.23 = (f32[8,128]{1,0:T(8,128)S(1)}, f32[8,128]{1,0:T(8,128)S(1)}, u32[]{:S(2)}, u32[]{:S(2)}) collective-permute-start(f32[8,128]{1,0:T(8,128)S(1)} %get-tuple-element.60.refs_2_), channel_id=1, source_target_pairs={{8,0},{0,8},{24,16},{16,24},{9,1},{1,9},{25,17},{17,25},{10,2},{2,... | collective-permute-start | bytes 12296 | tf_op jit(solution)/shard_map/ppermute | solution.py:43
  69.7 5.8 %collective-permute-start.27 = (f32[72,128]{1,0:T(8,128)S(1)}, f32[72,128]{1,0:T(8,128)S(1)}, u32[]{:S(2)}, u32[]{:S(2)}) collective-permute-start(f32[72,128]{1,0:T(8,128)S(1)} %get-tuple-element.63.refs_1_), channel_id=1, source_target_pairs={{3,0},{2,1},{1,2},{0,3},{7,4},{6,5},{5,6},{4,7},{11,8},{10,9},{9,1... | collective-permute-start | bytes 110600 | tf_op jit(solution)/shard_map/ppermute | solution.py:31
  71.6 5.2 %collective-permute-start.26 = (f32[72,128]{1,0:T(8,128)S(1)}, f32[72,128]{1,0:T(8,128)S(1)}, u32[]{:S(2)}, u32[]{:S(2)}) collective-permute-start(f32[72,128]{1,0:T(8,128)S(1)} %get-tuple-element.63.refs_1_), channel_id=1, source_target_pairs={{2,0},{3,1},{0,2},{1,3},{6,4},{7,5},{4,6},{5,7},{10,8},{11,9},{8,1... | collective-permute-start | bytes 110600 | tf_op jit(solution)/shard_map/ppermute | solution.py:31
  72.5 4.4 %collective-permute-start.25 = (f32[72,128]{1,0:T(8,128)S(1)}, f32[72,128]{1,0:T(8,128)S(1)}, u32[]{:S(2)}, u32[]{:S(2)}) collective-permute-start(f32[72,128]{1,0:T(8,128)S(1)} %get-tuple-element.63.refs_1_), channel_id=1, source_target_pairs={{1,0},{0,1},{3,2},{2,3},{5,4},{4,5},{7,6},{6,7},{9,8},{8,9},{11,10... | collective-permute-start | bytes 110600 | tf_op jit(solution)/shard_map/ppermute | solution.py:31
  77.7 3.6 %collective-permute-start.30 = (f32[8,128]{1,0:T(8,128)S(1)}, f32[8,128]{1,0:T(8,128)S(1)}, u32[]{:S(2)}, u32[]{:S(2)}) collective-permute-start(f32[8,128]{1,0:T(8,128)S(1)} %get-tuple-element.66.refs_1_), channel_id=1, source_target_pairs={{16,0},{24,8},{0,16},{8,24},{17,1},{25,9},{1,17},{9,25},{18,2},{26... | collective-permute-start | bytes 12296 | tf_op jit(solution)/shard_map/ppermute | solution.py:48
  78.8 4.5 %collective-permute-start.29 = (f32[8,128]{1,0:T(8,128)S(1)}, f32[8,128]{1,0:T(8,128)S(1)}, u32[]{:S(2)}, u32[]{:S(2)}) collective-permute-start(f32[8,128]{1,0:T(8,128)S(1)} %get-tuple-element.66.refs_1_), channel_id=1, source_target_pairs={{24,0},{16,8},{8,16},{0,24},{25,1},{17,9},{9,17},{1,25},{26,2},{18... | collective-permute-start | bytes 12296 | tf_op jit(solution)/shard_map/ppermute | solution.py:43
  80.3 3.6 %collective-permute-start.28 = (f32[8,128]{1,0:T(8,128)S(1)}, f32[8,128]{1,0:T(8,128)S(1)}, u32[]{:S(2)}, u32[]{:S(2)}) collective-permute-start(f32[8,128]{1,0:T(8,128)S(1)} %get-tuple-element.66.refs_1_), channel_id=1, source_target_pairs={{8,0},{0,8},{24,16},{16,24},{9,1},{1,9},{25,17},{17,25},{10,2},{2,... | collective-permute-start | bytes 12296 | tf_op jit(solution)/shard_map/ppermute | solution.py:43
  (1 other events, 4.7 us)

commit v4 on v3

--- a/solution.py
+++ b/solution.py
@@ -143,7 +143,12 @@
     return head, (values - head.astype(F32)).astype(BF16)
 
 
-def fetch_kernel(z, tiles_at, tiles, heads, rests, token, sems):
+def put_parts(wide, values):
+    tile = values.shape[-1]
+    wide[:, 0:tile], wide[:, tile : 2 * tile] = two_parts(values)
+
+
+def fetch_kernel(z, tiles_at, tiles, wide, token, sems):
     step = max(z.nt // FETCHES, 1)
     cuts = range(0, z.nt, step)
     started = [
@@ -156,26 +161,35 @@
     for i, copy in zip(cuts, started):
         copy.wait()
         for n in range(i, i + step):
-            heads[n], rests[n] = two_parts(tiles[n])
-
-
-def turn_kernel(z, when, tiles, heads, rests):
+            put_parts(wide.at[n], tiles[n])
+
+
+def turn_kernel(z, when, tiles, sibling, turned, sibling_wide, sibling_turned):
     for n in range(z.nt):
-        heads[n], rests[n] = two_parts(tiles[n].T)
-
-
-def part_rows(values, pairs):
+        put_parts(turned.at[n], tiles[n].T)
+    for n in range(z.nt // 2):
+        put_parts(sibling_wide.at[n], sibling[n])
+        put_parts(sibling_turned.at[n], sibling[n].T)
+
+
+def part_rows(values, pairs, first):
     head, rest = two_parts(values)
     count = values.shape[0]
-    pairs[pl.ds(0, count, stride=2), :] = head.astype(F32)
-    pairs[pl.ds(1, count, stride=2), :] = rest.astype(F32)
-
-
-def row_times_tile(pairs, n, heads, rests):
-    row = pairs[2 * n : 2 * n + 2, :].astype(BF16)
-    main = jnp.dot(row, heads[n], preferred_element_type=F32)
-    small = jnp.dot(row, rests[n], preferred_element_type=F32)
-    return main[0:1] + (main[1:2] + small[0:1])
+    pairs[pl.ds(2 * first, count, stride=2), :] = head.astype(F32)
+    pairs[pl.ds(2 * first + 1, count, stride=2), :] = rest.astype(F32)
+
+
+def row_times_tile(z, pairs, k, wide):
+    row = pairs[2 * k : 2 * k + 2, :].astype(BF16)
+    product = jnp.dot(row, wide[k // z.nt][k % z.nt], preferred_element_type=F32)
+    head, rest = product[:, 0 : z.tile], product[:, z.tile : 2 * z.tile]
+    return head[0:1] + (head[1:2] + rest[0:1])
+
+
+def two_units(matrix, vector):
+    jobs = [((i + 0.5) / len(matrix), 0, k) for i, k in enumerate(matrix)]
+    jobs += [((i + 0.5) / len(vector), 1, k) for i, k in enumerate(vector)]
+    return [(kind == 0, k) for _, kind, k in sorted(jobs)]
 
 
 def put_list(z, lists, rows, i):
@@ -185,7 +199,7 @@
 
 
 def assemble_kernel(z, *refs):
-    slots, out = refs[1:-1], refs[-1]
+    slots, out = refs[-2:0:-1], refs[-1]
     me = lax.axis_index("col")
     base = 3 * z.rows
     out[base:, :] = jnp.zeros((z.setup - base, z.tile), F32)
@@ -228,22 +242,29 @@
     return dot(head, right) + (dot(middle, right) + dot(tail, right))
 
 
-def transposed_products(z, y_at, shared, tiles, parts, links, products, pairs):
+def transposed_products(z, y_at, shared, tiles, wide, links, products, pairs):
     me = lax.axis_index("col")
-    columns = []
+    columns, on_matrix, on_vector = [], [], []
     for j in range(z.nr):
-        chosen = onehot(shared[j][3 * z.rows : 3 * z.rows + 1, :], 0, z.nt, z.rows)
+        lists = shared[j][3 * z.rows : 3 * z.rows + 1, :]
         block = y_at[j * z.rows : (j + 1) * z.rows, :]
-        if j == 0:
-            part_rows(exact_turned_dot(chosen, block), pairs)
-            columns.append(None)
+        wides = wide[j].shape[0] if j < len(wide) else 0
+        columns.append((None, wides))
+        if wides:
+            chosen = onehot(lists, 0, wides, z.rows)
+            part_rows(exact_turned_dot(chosen, block), pairs, j * z.nt)
+        if wides < z.nt:
+            chosen = onehot(lists, wides, z.nt - wides, z.rows)
+            columns[j] = (exact_turned_dot(block, chosen), wides)
+        on_matrix += range(j * z.nt, j * z.nt + wides)
+        on_vector += range(j * z.nt + wides, (j + 1) * z.nt)
+    for matrix, k in two_units(on_matrix, on_vector):
+        j, n = k // z.nt, k % z.nt
+        if matrix:
+            products[k : k + 1, :] = row_times_tile(z, pairs, k, wide)
         else:
-            columns.append(exact_turned_dot(block, chosen))
-    for n in range(z.nt):
-        products[n : n + 1, :] = row_times_tile(pairs, n, *parts)
-        for j in range(1, z.nr):
-            k = j * z.nt + n
-            column = columns[j][:, n : n + 1]
+            block, skip = columns[j]
+            column = block[:, n - skip : n - skip + 1]
             products[k : k + 1, :] = jnp.sum(tiles[j][n] * column, axis=0, keepdims=True)
     for j in range(z.nr):
         first = y_at[pl.ds(j * z.rows + me * z.rs, 1), :]
@@ -285,7 +306,7 @@
     shared, refs = refs[: z.nr], refs[z.nr :]
     halves, refs = refs[: z.nr], refs[z.nr :]
     tiles, refs = (None, *refs[: z.nr - 1]), refs[z.nr - 1 :]
-    parts, refs = refs[:2], refs[2:]
+    wide, refs = refs[:1], refs[1:]
     y, xs, g, msg, products, pairs = refs
     row = lax.axis_index("row")
     for j in range(z.nr):
@@ -294,7 +315,7 @@
         for part in range(4):
             spot = pl.ds(pl.multiple_of(part * z.xrows + at, 8), z.cs)
             xs[spot, :] = halves[j][part * z.cs : (part + 1) * z.cs, :]
-    transposed_products(z, y, shared, tiles, parts, halves, products, pairs)
+    transposed_products(z, y, shared, tiles, wide, halves, products, pairs)
     base = 3 * z.rows + z.row_lists
     sums = [sum(s[base + i : base + i + 1, :] for s in shared) for i in range(2)]
     gradient_part(z, products, halves, g, msg, sums)
@@ -308,6 +329,7 @@
 def dual_part(z, w, slots, shared, y_old, y_out):
     me = lax.axis_index("col")
     sigma = STEP_SCALE * w[0:1, :]
+    spots = lax.broadcasted_iota(jnp.int32, (z.rows, z.tile), 0)
     for j in range(z.nr):
         summed = jnp.zeros((z.rows, z.tile), F32)
         for q in range(z.row_lists):
@@ -316,12 +338,11 @@
             chosen = onehot(lists, 0, len(ds) * z.nt, z.rows)
             parts = [slots[d][j * z.nt : (j + 1) * z.nt, :] for d in ds]
             summed = summed + exact_dot(chosen, jnp.concatenate(parts, axis=0))
+        for d in range(z.nc):
+            inflow = slots[d][z.listed + j : z.listed + j + 1, :]
+            summed = summed + jnp.where(spots == peer(me, d, z.nc) * z.rs, inflow, 0.0)
         spot = slice(j * z.rows, (j + 1) * z.rows)
-        y_out[spot, :] = summed
-        for d in range(z.nc):
-            at = pl.ds(j * z.rows + peer(me, d, z.nc) * z.rs, 1)
-            y_out[at, :] = y_out[at, :] + slots[d][z.listed + j : z.listed + j + 1, :]
-        moved = y_old[spot, :] + sigma * (shared[j][z.rows : 2 * z.rows, :] - y_out[spot, :])
+        moved = y_old[spot, :] + sigma * (shared[j][z.rows : 2 * z.rows, :] - summed)
         y_out[spot, :] = jnp.maximum(moved, shared[j][2 * z.rows : 3 * z.rows, :])
 
 
@@ -330,13 +351,13 @@
     return mean, total((mean - begin) * (mean - begin))
 
 
-def dual_kernel(z, ends, *refs):
+def dual_kernel(z, ends, order, *refs):
     w, refs = refs[0], refs[1:]
-    slots, refs = refs[: z.nc], refs[z.nc :]
+    slots, refs = [refs[order.index(d)] for d in range(z.nc)], refs[z.nc :]
     shared, refs = refs[: z.nr], refs[z.nr :]
     halves, refs = refs[: z.nr], refs[z.nr :]
     tiles, refs = (None, *refs[: z.nr - 1]), refs[z.nr - 1 :]
-    parts, refs = refs[:2], refs[2:]
+    wide, refs = refs[:2], refs[2:]
     y_old = refs[0]
     y_begin = refs[1] if ends else None
     y_out, g, msg, products, pairs = refs[-5:]
@@ -347,44 +368,49 @@
         y_out[...] = mean
         moved = sum(s[z.products : z.products + 1, :] for s in slots)
         sums = [moved, move * jnp.ones((1, z.tile), F32)]
-    transposed_products(z, y_out, shared, tiles, parts, halves, products, pairs)
+    transposed_products(z, y_out, shared, tiles, wide, halves, products, pairs)
     gradient_part(z, products, halves, g, msg, sums)
 
 
 def last_kernel(z, *refs):
     w, refs = refs[0], refs[1:]
-    slots, refs = refs[: z.nc], refs[z.nc :]
+    slots, refs = refs[: z.nc][::-1], refs[z.nc :]
     shared, refs = refs[: z.nr], refs[z.nr :]
-    y_old, y_begin, out, msg, y_new = refs
+    y_old, y_begin, y_mean, msg, y_new = refs
     dual_part(z, w, slots, shared, y_old, y_new)
     mean, move = mean_and_move(y_new[...], y_old[...], y_begin[...])
-    y_new[...] = mean
-    me = lax.axis_index("col")
-    out[...] = y_new[pl.ds(pl.multiple_of(me * z.rs, z.rs), z.rs), :]
+    y_mean[...] = mean
     msg[...] = jnp.zeros_like(msg)
     msg[0:1, :] = sum(s[z.products : z.products + 1, :] for s in slots)
     msg[1:2, :] = move * jnp.ones((1, z.tile), F32)
 
 
+def output_kernel(z, x, y, x_out, y_out, token):
+    row, col = lax.axis_index("row"), lax.axis_index("col")
+    x_out[...] = x[pl.ds(pl.multiple_of(row * z.cs, z.cs), z.cs), :]
+    y_out[...] = y[pl.ds(pl.multiple_of(col * z.rs, z.rs), z.rs), :]
+    token[...] = jnp.zeros_like(token)
+
+
 def weight_kernel(z, *refs):
-    w, msgs, out = refs[0], refs[1:-1], refs[-1]
+    w, msgs, out = refs[1], refs[2:-1], refs[-1]
     dx = sum(m[0:1, :] for m in msgs)
     dy = sum(m[1:2, :] for m in msgs)
     new = jnp.sqrt(w[0:1, :] * jnp.sqrt((dx + EPSILON) / (dy + EPSILON)))
     out[0] = new[0, 0]
 
 
-def primal_kernel(z, starts, first, ends, last, *refs):
+def primal_kernel(z, starts, first, ends, *refs):
     w_old, refs = (None, refs) if first else (refs[0], refs[1:])
     g, own, refs = refs[0], refs[1], refs[2:]
     count = (z.np - 1) if starts else 2
-    got, refs = refs[:count], refs[count:]
+    got, refs = refs[:count][::-1], refs[count:]
     xs, refs = refs[0], refs[1:]
     x_old, refs = (None, refs) if first else (refs[0], refs[1:])
     x_begin, refs = (refs[0], refs[1:]) if ends else (None, refs)
     halves, refs = refs[: z.nr], refs[z.nr :]
     tiles, refs = (None, *refs[: z.nr - 1]), refs[z.nr - 1 :]
-    parts, refs = refs[:2], refs[2:]
+    wide, refs = refs[:2], refs[2:]
     x_out, zmsg, refs = refs[0], refs[1], refs[2:]
     w_out, refs = (refs[0], refs[1:]) if starts else (None, refs)
     xs_out, refs = (refs[0], refs[1:]) if first else (None, refs)
@@ -437,11 +463,7 @@
         mean = (x_new + x_now) * (1.0 / INNER)
         moved = mean[0 : z.cols, :] - x_begin[0 : z.cols, :]
         move = total(moved * moved)
-        if last:
-            work[...] = mean
-            x_out[...] = work[pl.ds(pl.multiple_of(row * z.cs, z.cs), z.cs), :]
-        else:
-            x_out[...] = mean
+        x_out[...] = mean
     else:
         x_out[...] = x_new
 
@@ -449,28 +471,28 @@
         count = min(z.tile, z.listed - q * z.tile)
         chosen = onehot(column_lists(z, halves, q), 0, count, z.cols)
         vectors[q * z.tile : q * z.tile + count, :] = exact_turned_dot(chosen, v[0 : z.cols, :])
-    part_rows(vectors[0 : z.nt, :], pairs)
+    wides = sum(w.shape[0] for w in wide)
+    part_rows(vectors[0:wides, :], pairs, 0)
     lane = lax.broadcasted_iota(jnp.int32, (z.tile, z.tile), 1)
-    rows = []
+    columns = [jnp.zeros((z.tile, z.tile), F32) for _ in range(z.blocks)]
+    rows = {}
+    for matrix, k in two_units(range(wides), range(wides, z.products)):
+        if matrix:
+            rows[k] = row_times_tile(z, pairs, k, wide)
+            continue
+        if k < z.listed:
+            tile = tiles[k // z.nt][k % z.nt]
+            vector = vectors[k : k + 1, :]
+        else:
+            tile = halves[k - z.listed][z.link : z.link + z.tile, :]
+            vector = v[z.cols + k - z.listed : z.cols + k - z.listed + 1, :]
+        column = jnp.sum(tile * vector, axis=1, keepdims=True)
+        columns[k // z.tile] = jnp.where(lane == k % z.tile, column, columns[k // z.tile])
     for b in range(z.blocks):
-        columns = jnp.zeros((z.tile, z.tile), F32)
-        for k in range(b * z.tile, min((b + 1) * z.tile, z.products)):
-            if k < z.nt:
-                continue
-            if k < 2 * z.nt:
-                rows.append(row_times_tile(pairs, k - z.nt, *parts))
-            if k < z.listed:
-                tile = tiles[k // z.nt][k % z.nt]
-                vector = vectors[k : k + 1, :]
-            else:
-                tile = halves[k - z.listed][z.link : z.link + z.tile, :]
-                vector = v[z.cols + k - z.listed : z.cols + k - z.listed + 1, :]
-            column = jnp.sum(tile * vector, axis=1, keepdims=True)
-            columns = jnp.where(lane == k % z.tile, column, columns)
         count = min(z.zrows - b * z.tile, z.tile)
-        zmsg[b * z.tile : b * z.tile + count, :] = columns.T[0:count, :]
-    for n, row_n in enumerate(rows):
-        zmsg[n : n + 1, :] = row_n
+        zmsg[b * z.tile : b * z.tile + count, :] = columns[b].T[0:count, :]
+    for k, row_k in rows.items():
+        zmsg[k : k + 1, :] = row_k
     if ends:
         zmsg[z.products : z.products + 1, :] = move * jnp.ones((1, z.tile), F32)
 
@@ -552,29 +574,36 @@
         limit=AWAY,
     )
     block = (listed, tile, tile)
-    own_tiles, heads, rests, token = call(
+    wide_block = (listed, tile, 2 * tile)
+    half_block = (listed // 2, tile, 2 * tile)
+    own_tiles, wide, token = call(
         z,
         part(fetch_kernel, z),
         (tiles_away,),
-        [block, (block, BF16), (block, BF16), line(8)],
+        [block, (wide_block, BF16), line(8)],
         away=1,
         sems=FETCHES,
         limit=FETCH,
     )
     slots = exchange(zmsg, "col")
     halves = exchange(xmsg, "row")
-    (gathered,) = call(z, part(assemble_kernel, z), [token] + slots, [line(z.setup)])
+    (gathered,) = call(z, part(assemble_kernel, z), [token] + slots[::-1], [line(z.setup)])
     shared = exchange(gathered, "row")
 
     products = line(up(z.products, 8))
     y, xs, g, msg = call(
         z,
         part(first_kernel, z),
-        (*shared, *halves, *tiles[1:], heads, rests),
+        (*shared, *halves, *tiles[1:], wide),
         [line(z.nr * z.rows), line(4 * z.xrows), line(z.xrows), line(z.hop_first)],
-        [products, line(2 * listed)],
-    )
-    turned = call(z, part(turn_kernel, z), (g, own_tiles), [(block, BF16), (block, BF16)])
+        [products, line(up(3 * listed, 8))],
+    )
+    turned, sibling_wide, sibling_turned = call(
+        z,
+        part(turn_kernel, z),
+        (g, own_tiles, tiles[1]),
+        [(wide_block, BF16), (half_block, BF16), (half_block, BF16)],
+    )
     x = None
     weight = None
     y_begin, x_begin = y, None
@@ -583,16 +612,16 @@
         ends = step % INNER == INNER - 1
         first, last = step == 0, step == ROUNDS * INNER - 1
         got = period_exchange(msg, starts)
-        operands = ([] if first else [weight]) + [g, msg, *got, xs]
-        operands += ([] if first else [x]) + ([x_begin] if ends else []) + [*halves, *tiles[1:], *turned]
-        shapes = [line(z.cs if last else z.xrows), line(z.zrows)]
+        operands = ([] if first else [weight]) + [g, msg, *got[::-1], xs]
+        operands += ([] if first else [x]) + ([x_begin] if ends else []) + [*halves, *tiles[1:], turned, sibling_turned]
+        shapes = [line(z.xrows), line(z.zrows)]
         shapes += ([line(8)] if starts else []) + ([line(4 * z.xrows)] if first else [])
         outs = call(
             z,
-            part(primal_kernel, z, starts, first, ends, last),
+            part(primal_kernel, z, starts, first, ends),
             operands,
             shapes,
-            [line(z.xrows), line(z.xrows), line(up(z.listed, 8)), line(2 * listed)],
+            [line(z.xrows), line(z.xrows), line(up(z.listed, 8)), line(up(3 * listed, 8))],
         )
         x_next, zmsg = outs[:2]
         if starts:
@@ -606,32 +635,39 @@
         slots = exchange(zmsg, "col")
         if last:
             break
-        operands = [weight, *slots, *shared, *halves, *tiles[1:], heads, rests, y]
+        order = list(range(z.nc))[::-1]
+        if first:
+            order = order[-2:-1] + order[:-2] + order[-1:]
+        operands = [weight, *[slots[d] for d in order], *shared, *halves, *tiles[1:], wide, sibling_wide, y]
         y_next, g, msg = call(
             z,
-            part(dual_kernel, z, ends),
+            part(dual_kernel, z, ends, order),
             operands + ([y_begin] if ends else []),
             [line(z.nr * z.rows), line(z.xrows), line(z.hop)],
-            [products, line(2 * listed)],
+            [products, line(up(3 * listed, 8))],
         )
         y = y_next
         if ends:
             y_begin = y
-    dual, sums = call(
+    y, sums = call(
         z,
         part(last_kernel, z),
-        (weight, *slots, *shared, y, y_begin),
-        [line(z.rs), line(8)],
+        (weight, *slots[::-1], *shared, y, y_begin),
+        [line(z.nr * z.rows), line(8)],
         [line(z.nr * z.rows)],
+    )
+    got = period_exchange(sums, True)
+    primal, dual, token = call(
+        z, part(output_kernel, z), (x, y), [line(z.cs), line(z.rs), line(8)]
     )
     (final,) = call(
         z,
         part(weight_kernel, z),
-        (weight, sums, *period_exchange(sums, True)),
+        (token, weight, sums, *got[::-1]),
         [(1,)],
         scalar=True,
     )
-    return (x, dual, final.reshape(()))
+    return (primal, dual, final.reshape(()))
 
 
 def solution(mesh):

time: 84.7 us -> 82 us (0.968)
  Pallas kernels: 17.5 us -> 15.8 us
  waiting for transfers between devices: 26.7 us -> 25.7 us
    pallas_call x15 -> x16, Pallas kernels: 17.5 us -> 15.8 us  [call(): pl.pallas_call(kernel, out_shape=[jax.ShapeDtypeStruct(s, kind) for s, ki...]
    ppermute x10, waiting for transfers between devices: 12.6 us -> 11.7 us  [period_exchange(): lax.ppermute(x, 'period', [(m[i], i) for i in range(n)])]
  transfers between devices with their start and end apart: 31 -> 31, of which waited for: 22 -> 21; matrix products, arithmetic and copies ran while one was open for 0% -> 0% of each run, Pallas kernels for 7% -> 8%
where the time goes in v4:
time: 82 us; the launch traced here: 81.7 us
  starting transfers between devices  39.4 us (48%)
  waiting for transfers between devices  25.7 us (31%)
  Pallas kernels  15.8 us (19%)
    ppermute x18, starting transfers between devices, from_peer(): return lax.ppermute(x, axis, pairs)  23.7 us
    pallas_call x16, Pallas kernels, call(): pl.pallas_call(kernel, out_shape=[jax.ShapeDtypeStruct(s, kind) for s, ki...  15.8 us
    ppermute x18, waiting for transfers between devices, from_peer(): return lax.ppermute(x, axis, pairs)  13.9 us
    ppermute x10, starting transfers between devices, period_exchange(): lax.ppermute(x, 'period', [(m[i], i) for i in range(n)])  12 us
    ppermute x10, waiting for transfers between devices, period_exchange(): lax.ppermute(x, 'period', [(m[i], i) for i in range(n)])  11.7 us
    ppermute x3, starting transfers between devices, period_exchange(): lax.ppermute(x, 'period', [((i + s) % n, i) for i in range(n)])  3.67 us
  transfers between devices with their start and end apart: 31, of which 21 were waited for; matrix products, arithmetic and copies ran while one was open for 0% of the time, Pallas kernels for 8%

profile of v4, /device:TPU:0, one launch (start us, length us, event | category | flops | bytes accessed | tf_op | source)
XLA Modules:
  0.0 81.7 jit_solution(7143440340365781706)
XLA Ops:
  1.1 1.6 %shard_map.131.refs_4_ = f32[104,128]{1,0:T(8,128)} custom-call(f32[32,128]{1,0:T(8,128)} %dual_at.1, f32[32,128]{1,0:T(8,128)} %rhs_at.1, s32[32,128]{1,0:T(8,128)} %rkind_at.1, f32[64,128]{1,0:T(8,128)} %obj_at.3, s32[1,32]{1,0:T(1,128)} %bitcast.8), custom_call_target="tpu_custom_call" | custom-call | tf_op jit(solution)/shard_map/pallas_call | solution.py:506
  2.7 4.7 %collective-permute-start = (f32[104,128]{1,0:T(8,128)}, f32[104,128]{1,0:T(8,128)S(1)}, u32[]{:S(2)}, u32[]{:S(2)}) collective-permute-start(f32[104,128]{1,0:T(8,128)} %shard_map.131.refs_4_), channel_id=1, source_target_pairs={{3,0},{2,1},{1,2},{0,3},{7,4},{6,5},{5,6},{4,7},{11,8},{10,9},{9,1... | collective-permute-start | bytes 159752 | tf_op jit(solution)/shard_map/ppermute | solution.py:31
  8.0 1.7 %shard_map.133.refs_2_.refs_6_.refs_7_.refs_8_ = f32[392,128]{1,0:T(8,128)} custom-call(f32[64,128]{1,0:T(8,128)} %x_at.1, f32[64,128]{1,0:T(8,128)} %obj_at.3, f32[64,128]{1,0:T(8,128)} %ub_at.1, s32[64,128]{1,0:T(8,128)} %ckind_at.1, s32[1,32]{1,0:T(1,128)} %bitcast.9, f32[128,128]{1,0:T(8,128)} %bitcast.7), custom_call_target="tpu_custom_call" | custom-call | tf_op jit(solution)/shard_map/pallas_call | solution.py:506
  9.8 1.6 %shard_map.130 = (f32[32,128,128]{2,1,0:T(8,128)S(1)}, bf16[32,128,256]{2,1,0:T(8,128)(2,1)S(1)}, f32[8,128]{1,0:T(8,128)S(1)}) custom-call(f32[32,128,128]{2,1,0:T(8,128)} %bitcast.6), custom_call_target="tpu_custom_call" | custom-call | tf_op jit(solution)/shard_map/pallas_call | solution.py:506
  11.5 1.4 %collective-permute-done.1.refs_2_ = f32[104,128]{1,0:T(8,128)S(1)} collective-permute-done((f32[104,128]{1,0:T(8,128)}, f32[104,128]{1,0:T(8,128)S(1)}, u32[]{:S(2)}, u32[]{:S(2)}) %collective-permute-start.1) | collective-permute-done | bytes 53280 | tf_op jit(solution)/shard_map/ppermute | solution.py:31
  13.0 1.4 %collective-permute-done.3.refs_1_.refs_6_ = f32[392,128]{1,0:T(8,128)S(1)} collective-permute-done((f32[392,128]{1,0:T(8,128)S(1)}, f32[392,128]{1,0:T(8,128)S(1)}, u32[]{:S(2)}, u32[]{:S(2)}) %collective-permute-start.3) | collective-permute-done | bytes 200736 | tf_op jit(solution)/shard_map/ppermute | solution.py:31
  15.7 1.6 %collective-permute-start.6 = (f32[16,128]{1,0:T(8,128)S(1)}, f32[16,128]{1,0:T(8,128)S(1)}, u32[]{:S(2)}, u32[]{:S(2)}) collective-permute-start(f32[16,128]{1,0:T(8,128)S(1)} %get-tuple-element.41.refs_1_), channel_id=1, source_target_pairs={{16,0},{24,8},{0,16},{8,24},{17,1},{25,9},{1,17},{9,25},{18,2},{26... | collective-permute-start | bytes 24584 | tf_op jit(solution)/shard_map/ppermute | solution.py:48
  17.3 1.4 %collective-permute-start.7 = (f32[16,128]{1,0:T(8,128)S(1)}, f32[16,128]{1,0:T(8,128)S(1)}, u32[]{:S(2)}, u32[]{:S(2)}) collective-permute-start(f32[16,128]{1,0:T(8,128)S(1)} %get-tuple-element.41.refs_1_), channel_id=1, source_target_pairs={{24,0},{16,8},{8,16},{0,24},{25,1},{17,9},{9,17},{1,25},{26,2},{18... | collective-permute-start | bytes 24584 | tf_op jit(solution)/shard_map/ppermute | solution.py:43
  20.3 1.5 %collective-permute-done.7.refs_3_ = f32[16,128]{1,0:T(8,128)S(1)} collective-permute-done((f32[16,128]{1,0:T(8,128)S(1)}, f32[16,128]{1,0:T(8,128)S(1)}, u32[]{:S(2)}, u32[]{:S(2)}) %collective-permute-start.7) | collective-permute-done | bytes 8224 | tf_op jit(solution)/shard_map/ppermute | solution.py:43
  23.2 2.5 %collective-permute-start.10 = (f32[72,128]{1,0:T(8,128)S(1)}, f32[72,128]{1,0:T(8,128)S(1)}, u32[]{:S(2)}, u32[]{:S(2)}) collective-permute-start(f32[72,128]{1,0:T(8,128)S(1)} %get-tuple-element.47.refs_4_), channel_id=1, source_target_pairs={{3,0},{2,1},{1,2},{0,3},{7,4},{6,5},{5,6},{4,7},{11,8},{10,9},{9,1... | collective-permute-start | bytes 110600 | tf_op jit(solution)/shard_map/ppermute | solution.py:31
  26.0 1.6 %collective-permute-start.9 = (f32[72,128]{1,0:T(8,128)S(1)}, f32[72,128]{1,0:T(8,128)S(1)}, u32[]{:S(2)}, u32[]{:S(2)}) collective-permute-start(f32[72,128]{1,0:T(8,128)S(1)} %get-tuple-element.47.refs_4_), channel_id=1, source_target_pairs={{1,0},{0,1},{3,2},{2,3},{5,4},{4,5},{7,6},{6,7},{9,8},{8,9},{11,10... | collective-permute-start | bytes 110600 | tf_op jit(solution)/shard_map/ppermute | solution.py:31
  27.6 1.6 %collective-permute-done.10.refs_2_ = f32[72,128]{1,0:T(8,128)S(1)} collective-permute-done((f32[72,128]{1,0:T(8,128)S(1)}, f32[72,128]{1,0:T(8,128)S(1)}, u32[]{:S(2)}, u32[]{:S(2)}) %collective-permute-start.10) | collective-permute-done | bytes 36896 | tf_op jit(solution)/shard_map/ppermute | solution.py:31
  29.2 1.3 %collective-permute-done.11.refs_3_ = f32[72,128]{1,0:T(8,128)S(1)} collective-permute-done((f32[72,128]{1,0:T(8,128)S(1)}, f32[72,128]{1,0:T(8,128)S(1)}, u32[]{:S(2)}, u32[]{:S(2)}) %collective-permute-start.11) | collective-permute-done | bytes 36896 | tf_op jit(solution)/shard_map/ppermute | solution.py:31
  31.8 1.6 %collective-permute-start.12 = (f32[8,128]{1,0:T(8,128)S(1)}, f32[8,128]{1,0:T(8,128)S(1)}, u32[]{:S(2)}, u32[]{:S(2)}) collective-permute-start(f32[8,128]{1,0:T(8,128)S(1)} %get-tuple-element.51.refs_2_), channel_id=1, source_target_pairs={{24,0},{16,8},{8,16},{0,24},{25,1},{17,9},{9,17},{1,25},{26,2},{18... | collective-permute-start | bytes 12296 | tf_op jit(solution)/shard_map/ppermute | solution.py:43
  33.3 1.5 %collective-permute-start.13 = (f32[8,128]{1,0:T(8,128)S(1)}, f32[8,128]{1,0:T(8,128)S(1)}, u32[]{:S(2)}, u32[]{:S(2)}) collective-permute-start(f32[8,128]{1,0:T(8,128)S(1)} %get-tuple-element.51.refs_2_), channel_id=1, source_target_pairs={{8,0},{0,8},{24,16},{16,24},{9,1},{1,9},{25,17},{17,25},{10,2},{2,... | collective-permute-start | bytes 12296 | tf_op jit(solution)/shard_map/ppermute | solution.py:43
  34.8 1.5 %collective-permute-done.12.refs_3_ = f32[8,128]{1,0:T(8,128)S(1)} collective-permute-done((f32[8,128]{1,0:T(8,128)S(1)}, f32[8,128]{1,0:T(8,128)S(1)}, u32[]{:S(2)}, u32[]{:S(2)}) %collective-permute-start.12) | collective-permute-done | bytes 4128 | tf_op jit(solution)/shard_map/ppermute | solution.py:43
  37.8 1.9 %collective-permute-start.14 = (f32[72,128]{1,0:T(8,128)S(1)}, f32[72,128]{1,0:T(8,128)S(1)}, u32[]{:S(2)}, u32[]{:S(2)}) collective-permute-start(f32[72,128]{1,0:T(8,128)S(1)} %get-tuple-element.54.refs_4_), channel_id=1, source_target_pairs={{3,0},{2,1},{1,2},{0,3},{7,4},{6,5},{5,6},{4,7},{11,8},{10,9},{9,1... | collective-permute-start | bytes 110600 | tf_op jit(solution)/shard_map/ppermute | solution.py:31
  40.3 1.9 %collective-permute-start.16 = (f32[72,128]{1,0:T(8,128)S(1)}, f32[72,128]{1,0:T(8,128)S(1)}, u32[]{:S(2)}, u32[]{:S(2)}) collective-permute-start(f32[72,128]{1,0:T(8,128)S(1)} %get-tuple-element.54.refs_4_), channel_id=1, source_target_pairs={{1,0},{0,1},{3,2},{2,3},{5,4},{4,5},{7,6},{6,7},{9,8},{8,9},{11,10... | collective-permute-start | bytes 110600 | tf_op jit(solution)/shard_map/ppermute | solution.py:31
  42.2 1.4 %collective-permute-done.14.refs_1_ = f32[72,128]{1,0:T(8,128)S(1)} collective-permute-done((f32[72,128]{1,0:T(8,128)S(1)}, f32[72,128]{1,0:T(8,128)S(1)}, u32[]{:S(2)}, u32[]{:S(2)}) %collective-permute-start.14) | collective-permute-done | bytes 36896 | tf_op jit(solution)/shard_map/ppermute | solution.py:31
  43.6 1.3 %collective-permute-done.15.refs_2_ = f32[72,128]{1,0:T(8,128)S(1)} collective-permute-done((f32[72,128]{1,0:T(8,128)S(1)}, f32[72,128]{1,0:T(8,128)S(1)}, u32[]{:S(2)}, u32[]{:S(2)}) %collective-permute-start.15) | collective-permute-done | bytes 36896 | tf_op jit(solution)/shard_map/ppermute | solution.py:31
  47.2 2.0 %collective-permute-start.18 = (f32[8,128]{1,0:T(8,128)S(1)}, f32[8,128]{1,0:T(8,128)S(1)}, u32[]{:S(2)}, u32[]{:S(2)}) collective-permute-start(f32[8,128]{1,0:T(8,128)S(1)} %get-tuple-element.57.refs_2_), channel_id=1, source_target_pairs={{24,0},{16,8},{8,16},{0,24},{25,1},{17,9},{9,17},{1,25},{26,2},{18... | collective-permute-start | bytes 12296 | tf_op jit(solution)/shard_map/ppermute | solution.py:43
  49.9 1.8 %collective-permute-done.18.refs_4_ = f32[8,128]{1,0:T(8,128)S(1)} collective-permute-done((f32[8,128]{1,0:T(8,128)S(1)}, f32[8,128]{1,0:T(8,128)S(1)}, u32[]{:S(2)}, u32[]{:S(2)}) %collective-permute-start.18) | collective-permute-done | bytes 4128 | tf_op jit(solution)/shard_map/ppermute | solution.py:43
  53.7 2.0 %collective-permute-start.20 = (f32[72,128]{1,0:T(8,128)S(1)}, f32[72,128]{1,0:T(8,128)S(1)}, u32[]{:S(2)}, u32[]{:S(2)}) collective-permute-start(f32[72,128]{1,0:T(8,128)S(1)} %get-tuple-element.60.refs_4_), channel_id=1, source_target_pairs={{3,0},{2,1},{1,2},{0,3},{7,4},{6,5},{5,6},{4,7},{11,8},{10,9},{9,1... | collective-permute-start | bytes 110600 | tf_op jit(solution)/shard_map/ppermute | solution.py:31
  56.4 1.7 %collective-permute-start.22 = (f32[72,128]{1,0:T(8,128)S(1)}, f32[72,128]{1,0:T(8,128)S(1)}, u32[]{:S(2)}, u32[]{:S(2)}) collective-permute-start(f32[72,128]{1,0:T(8,128)S(1)} %get-tuple-element.60.refs_4_), channel_id=1, source_target_pairs={{1,0},{0,1},{3,2},{2,3},{5,4},{4,5},{7,6},{6,7},{9,8},{8,9},{11,10... | collective-permute-start | bytes 110600 | tf_op jit(solution)/shard_map/ppermute | solution.py:31
  58.1 1.4 %collective-permute-done.20.refs_1_ = f32[72,128]{1,0:T(8,128)S(1)} collective-permute-done((f32[72,128]{1,0:T(8,128)S(1)}, f32[72,128]{1,0:T(8,128)S(1)}, u32[]{:S(2)}, u32[]{:S(2)}) %collective-permute-start.20) | collective-permute-done | bytes 36896 | tf_op jit(solution)/shard_map/ppermute | solution.py:31
  64.0 2.5 %collective-permute-done.23.refs_3_ = f32[8,128]{1,0:T(8,128)S(1)} collective-permute-done((f32[8,128]{1,0:T(8,128)S(1)}, f32[8,128]{1,0:T(8,128)S(1)}, u32[]{:S(2)}, u32[]{:S(2)}) %collective-permute-start.23) | collective-permute-done | bytes 4128 | tf_op jit(solution)/shard_map/ppermute | solution.py:43
  67.4 1.9 %collective-permute-start.25 = (f32[72,128]{1,0:T(8,128)S(1)}, f32[72,128]{1,0:T(8,128)S(1)}, u32[]{:S(2)}, u32[]{:S(2)}) collective-permute-start(f32[72,128]{1,0:T(8,128)S(1)} %get-tuple-element.66.refs_4_), channel_id=1, source_target_pairs={{3,0},{2,1},{1,2},{0,3},{7,4},{6,5},{5,6},{4,7},{11,8},{10,9},{9,1... | collective-permute-start | bytes 110600 | tf_op jit(solution)/shard_map/ppermute | solution.py:31
  70.3 1.5 %collective-permute-start.27 = (f32[72,128]{1,0:T(8,128)S(1)}, f32[72,128]{1,0:T(8,128)S(1)}, u32[]{:S(2)}, u32[]{:S(2)}) collective-permute-start(f32[72,128]{1,0:T(8,128)S(1)} %get-tuple-element.66.refs_4_), channel_id=1, source_target_pairs={{1,0},{0,1},{3,2},{2,3},{5,4},{4,5},{7,6},{6,7},{9,8},{8,9},{11,10... | collective-permute-start | bytes 110600 | tf_op jit(solution)/shard_map/ppermute | solution.py:31
  71.9 1.4 %collective-permute-done.25.refs_1_ = f32[72,128]{1,0:T(8,128)S(1)} collective-permute-done((f32[72,128]{1,0:T(8,128)S(1)}, f32[72,128]{1,0:T(8,128)S(1)}, u32[]{:S(2)}, u32[]{:S(2)}) %collective-permute-start.25) | collective-permute-done | bytes 36896 | tf_op jit(solution)/shard_map/ppermute | solution.py:31
  73.2 1.4 %collective-permute-done.26.refs_2_ = f32[72,128]{1,0:T(8,128)S(1)} collective-permute-done((f32[72,128]{1,0:T(8,128)S(1)}, f32[72,128]{1,0:T(8,128)S(1)}, u32[]{:S(2)}, u32[]{:S(2)}) %collective-permute-start.26) | collective-permute-done | bytes 36896 | tf_op jit(solution)/shard_map/ppermute | solution.py:31
  76.0 1.4 %collective-permute-start.29 = (f32[8,128]{1,0:T(8,128)S(1)}, f32[8,128]{1,0:T(8,128)S(1)}, u32[]{:S(2)}, u32[]{:S(2)}) collective-permute-start(f32[8,128]{1,0:T(8,128)S(1)} %get-tuple-element.72.refs_2_), channel_id=1, source_target_pairs={{24,0},{16,8},{8,16},{0,24},{25,1},{17,9},{9,17},{1,25},{26,2},{18... | collective-permute-start | bytes 12296 | tf_op jit(solution)/shard_map/ppermute | solution.py:43
  79.1 1.5 %collective-permute-done.29.refs_4_ = f32[8,128]{1,0:T(8,128)S(1)} collective-permute-done((f32[8,128]{1,0:T(8,128)S(1)}, f32[8,128]{1,0:T(8,128)S(1)}, u32[]{:S(2)}, u32[]{:S(2)}) %collective-permute-start.29) | collective-permute-done | bytes 4128 | tf_op jit(solution)/shard_map/ppermute | solution.py:43
  (51 shorter events, 25.2 us)
Async XLA Ops:
  0.6 13.8 %collective-permute-start.5 = (f32[32,128,128]{2,1,0:T(8,128)}, f32[32,128,128]{2,1,0:T(8,128)S(1)}, u32[]{:S(2)}, u32[]{:S(2)}) collective-permute-start(f32[32,128,128]{2,1,0:T(8,128)} %bitcast.5), channel_id=1, source_target_pairs={{4,0},{0,4},{5,1},{1,5},{6,2},{2,6},{7,3},{3,7},{12,8},{8,12},{13,... | collective-permute-start | bytes 6291464 | tf_op jit(solution)/shard_map/ppermute | solution.py:31
  2.7 10.2 %copy-start.1 = (f32[104,128]{1,0:T(8,128)S(1)}, f32[104,128]{1,0:T(8,128)}, u32[]{:S(2)}) copy-start(f32[104,128]{1,0:T(8,128)} %shard_map.131.refs_4_) | copy-start | bytes 159748
  2.7 8.7 %collective-permute-start = (f32[104,128]{1,0:T(8,128)}, f32[104,128]{1,0:T(8,128)S(1)}, u32[]{:S(2)}, u32[]{:S(2)}) collective-permute-start(f32[104,128]{1,0:T(8,128)} %shard_map.131.refs_4_), channel_id=1, source_target_pairs={{3,0},{2,1},{1,2},{0,3},{7,4},{6,5},{5,6},{4,7},{11,8},{10,9},{9,1... | collective-permute-start | bytes 159752 | tf_op jit(solution)/shard_map/ppermute | solution.py:31
  7.4 5.5 %collective-permute-start.1 = (f32[104,128]{1,0:T(8,128)}, f32[104,128]{1,0:T(8,128)S(1)}, u32[]{:S(2)}, u32[]{:S(2)}) collective-permute-start(f32[104,128]{1,0:T(8,128)} %shard_map.131.refs_4_), channel_id=1, source_target_pairs={{2,0},{3,1},{0,2},{1,3},{6,4},{7,5},{4,6},{5,7},{10,8},{11,9},{8,1... | collective-permute-start | bytes 159752 | tf_op jit(solution)/shard_map/ppermute | solution.py:31
  7.4 5.5 %collective-permute-start.2 = (f32[104,128]{1,0:T(8,128)}, f32[104,128]{1,0:T(8,128)S(1)}, u32[]{:S(2)}, u32[]{:S(2)}) collective-permute-start(f32[104,128]{1,0:T(8,128)} %shard_map.131.refs_4_), channel_id=1, source_target_pairs={{1,0},{0,1},{3,2},{2,3},{5,4},{4,5},{7,6},{6,7},{9,8},{8,9},{11,10... | collective-permute-start | bytes 159752 | tf_op jit(solution)/shard_map/ppermute | solution.py:31
  9.7 3.3 %collective-permute-start.4 = (f32[392,128]{1,0:T(8,128)}, f32[392,128]{1,0:T(8,128)S(1)}, u32[]{:S(2)}, u32[]{:S(2)}) collective-permute-start(f32[392,128]{1,0:T(8,128)} %shard_map.133.refs_2_.refs_6_.refs_7_.refs_8_), channel_id=1, source_target_pairs={{4,0},{0,4},{5,1},{1,5},{6,2},{2,6},{7,3},{3,7},{12,8},{8,12},{13,... | collective-permute-start | bytes 602120 | tf_op jit(solution)/shard_map/ppermute | solution.py:31
  13.0 1.5 %collective-permute-start.3 = (f32[392,128]{1,0:T(8,128)S(1)}, f32[392,128]{1,0:T(8,128)S(1)}, u32[]{:S(2)}, u32[]{:S(2)}) collective-permute-start(f32[392,128]{1,0:T(8,128)S(1)} %shard_map.132.refs_0_.refs_5_), channel_id=1, source_target_pairs={{4,0},{0,4},{5,1},{1,5},{6,2},{2,6},{7,3},{3,7},{12,8},{8,12},{13,... | collective-permute-start | bytes 602120 | tf_op jit(solution)/shard_map/ppermute | solution.py:31
  15.7 4.6 %collective-permute-start.6 = (f32[16,128]{1,0:T(8,128)S(1)}, f32[16,128]{1,0:T(8,128)S(1)}, u32[]{:S(2)}, u32[]{:S(2)}) collective-permute-start(f32[16,128]{1,0:T(8,128)S(1)} %get-tuple-element.41.refs_1_), channel_id=1, source_target_pairs={{16,0},{24,8},{0,16},{8,24},{17,1},{25,9},{1,17},{9,25},{18,2},{26... | collective-permute-start | bytes 24584 | tf_op jit(solution)/shard_map/ppermute | solution.py:48
  17.3 4.5 %collective-permute-start.7 = (f32[16,128]{1,0:T(8,128)S(1)}, f32[16,128]{1,0:T(8,128)S(1)}, u32[]{:S(2)}, u32[]{:S(2)}) collective-permute-start(f32[16,128]{1,0:T(8,128)S(1)} %get-tuple-element.41.refs_1_), channel_id=1, source_target_pairs={{24,0},{16,8},{8,16},{0,24},{25,1},{17,9},{9,17},{1,25},{26,2},{18... | collective-permute-start | bytes 24584 | tf_op jit(solution)/shard_map/ppermute | solution.py:43
  18.7 3.7 %collective-permute-start.8 = (f32[16,128]{1,0:T(8,128)S(1)}, f32[16,128]{1,0:T(8,128)S(1)}, u32[]{:S(2)}, u32[]{:S(2)}) collective-permute-start(f32[16,128]{1,0:T(8,128)S(1)} %get-tuple-element.41.refs_1_), channel_id=1, source_target_pairs={{8,0},{0,8},{24,16},{16,24},{9,1},{1,9},{25,17},{17,25},{10,2},{2,... | collective-permute-start | bytes 24584 | tf_op jit(solution)/shard_map/ppermute | solution.py:43
  23.2 6.1 %collective-permute-start.10 = (f32[72,128]{1,0:T(8,128)S(1)}, f32[72,128]{1,0:T(8,128)S(1)}, u32[]{:S(2)}, u32[]{:S(2)}) collective-permute-start(f32[72,128]{1,0:T(8,128)S(1)} %get-tuple-element.47.refs_4_), channel_id=1, source_target_pairs={{3,0},{2,1},{1,2},{0,3},{7,4},{6,5},{5,6},{4,7},{11,8},{10,9},{9,1... | collective-permute-start | bytes 110600 | tf_op jit(solution)/shard_map/ppermute | solution.py:31
  25.7 4.9 %collective-permute-start.11 = (f32[72,128]{1,0:T(8,128)S(1)}, f32[72,128]{1,0:T(8,128)S(1)}, u32[]{:S(2)}, u32[]{:S(2)}) collective-permute-start(f32[72,128]{1,0:T(8,128)S(1)} %get-tuple-element.47.refs_4_), channel_id=1, source_target_pairs={{2,0},{3,1},{0,2},{1,3},{6,4},{7,5},{4,6},{5,7},{10,8},{11,9},{8,1... | collective-permute-start | bytes 110600 | tf_op jit(solution)/shard_map/ppermute | solution.py:31
  26.0 4.6 %collective-permute-start.9 = (f32[72,128]{1,0:T(8,128)S(1)}, f32[72,128]{1,0:T(8,128)S(1)}, u32[]{:S(2)}, u32[]{:S(2)}) collective-permute-start(f32[72,128]{1,0:T(8,128)S(1)} %get-tuple-element.47.refs_4_), channel_id=1, source_target_pairs={{1,0},{0,1},{3,2},{2,3},{5,4},{4,5},{7,6},{6,7},{9,8},{8,9},{11,10... | collective-permute-start | bytes 110600 | tf_op jit(solution)/shard_map/ppermute | solution.py:31
  31.8 4.6 %collective-permute-start.12 = (f32[8,128]{1,0:T(8,128)S(1)}, f32[8,128]{1,0:T(8,128)S(1)}, u32[]{:S(2)}, u32[]{:S(2)}) collective-permute-start(f32[8,128]{1,0:T(8,128)S(1)} %get-tuple-element.51.refs_2_), channel_id=1, source_target_pairs={{24,0},{16,8},{8,16},{0,24},{25,1},{17,9},{9,17},{1,25},{26,2},{18... | collective-permute-start | bytes 12296 | tf_op jit(solution)/shard_map/ppermute | solution.py:43
  33.3 3.6 %collective-permute-start.13 = (f32[8,128]{1,0:T(8,128)S(1)}, f32[8,128]{1,0:T(8,128)S(1)}, u32[]{:S(2)}, u32[]{:S(2)}) collective-permute-start(f32[8,128]{1,0:T(8,128)S(1)} %get-tuple-element.51.refs_2_), channel_id=1, source_target_pairs={{8,0},{0,8},{24,16},{16,24},{9,1},{1,9},{25,17},{17,25},{10,2},{2,... | collective-permute-start | bytes 12296 | tf_op jit(solution)/shard_map/ppermute | solution.py:43
  37.8 5.8 %collective-permute-start.14 = (f32[72,128]{1,0:T(8,128)S(1)}, f32[72,128]{1,0:T(8,128)S(1)}, u32[]{:S(2)}, u32[]{:S(2)}) collective-permute-start(f32[72,128]{1,0:T(8,128)S(1)} %get-tuple-element.54.refs_4_), channel_id=1, source_target_pairs={{3,0},{2,1},{1,2},{0,3},{7,4},{6,5},{5,6},{4,7},{11,8},{10,9},{9,1... | collective-permute-start | bytes 110600 | tf_op jit(solution)/shard_map/ppermute | solution.py:31
  39.7 5.3 %collective-permute-start.15 = (f32[72,128]{1,0:T(8,128)S(1)}, f32[72,128]{1,0:T(8,128)S(1)}, u32[]{:S(2)}, u32[]{:S(2)}) collective-permute-start(f32[72,128]{1,0:T(8,128)S(1)} %get-tuple-element.54.refs_4_), channel_id=1, source_target_pairs={{2,0},{3,1},{0,2},{1,3},{6,4},{7,5},{4,6},{5,7},{10,8},{11,9},{8,1... | collective-permute-start | bytes 110600 | tf_op jit(solution)/shard_map/ppermute | solution.py:31
  40.3 4.6 %collective-permute-start.16 = (f32[72,128]{1,0:T(8,128)S(1)}, f32[72,128]{1,0:T(8,128)S(1)}, u32[]{:S(2)}, u32[]{:S(2)}) collective-permute-start(f32[72,128]{1,0:T(8,128)S(1)} %get-tuple-element.54.refs_4_), channel_id=1, source_target_pairs={{1,0},{0,1},{3,2},{2,3},{5,4},{4,5},{7,6},{6,7},{9,8},{8,9},{11,10... | collective-permute-start | bytes 110600 | tf_op jit(solution)/shard_map/ppermute | solution.py:31
  46.2 3.7 %collective-permute-start.17 = (f32[8,128]{1,0:T(8,128)S(1)}, f32[8,128]{1,0:T(8,128)S(1)}, u32[]{:S(2)}, u32[]{:S(2)}) collective-permute-start(f32[8,128]{1,0:T(8,128)S(1)} %get-tuple-element.57.refs_2_), channel_id=1, source_target_pairs={{16,0},{24,8},{0,16},{8,24},{17,1},{25,9},{1,17},{9,25},{18,2},{26... | collective-permute-start | bytes 12296 | tf_op jit(solution)/shard_map/ppermute | solution.py:48
  47.2 4.5 %collective-permute-start.18 = (f32[8,128]{1,0:T(8,128)S(1)}, f32[8,128]{1,0:T(8,128)S(1)}, u32[]{:S(2)}, u32[]{:S(2)}) collective-permute-start(f32[8,128]{1,0:T(8,128)S(1)} %get-tuple-element.57.refs_2_), channel_id=1, source_target_pairs={{24,0},{16,8},{8,16},{0,24},{25,1},{17,9},{9,17},{1,25},{26,2},{18... | collective-permute-start | bytes 12296 | tf_op jit(solution)/shard_map/ppermute | solution.py:43
  49.2 3.6 %collective-permute-start.19 = (f32[8,128]{1,0:T(8,128)S(1)}, f32[8,128]{1,0:T(8,128)S(1)}, u32[]{:S(2)}, u32[]{:S(2)}) collective-permute-start(f32[8,128]{1,0:T(8,128)S(1)} %get-tuple-element.57.refs_2_), channel_id=1, source_target_pairs={{8,0},{0,8},{24,16},{16,24},{9,1},{1,9},{25,17},{17,25},{10,2},{2,... | collective-permute-start | bytes 12296 | tf_op jit(solution)/shard_map/ppermute | solution.py:43
  53.7 5.8 %collective-permute-start.20 = (f32[72,128]{1,0:T(8,128)S(1)}, f32[72,128]{1,0:T(8,128)S(1)}, u32[]{:S(2)}, u32[]{:S(2)}) collective-permute-start(f32[72,128]{1,0:T(8,128)S(1)} %get-tuple-element.60.refs_4_), channel_id=1, source_target_pairs={{3,0},{2,1},{1,2},{0,3},{7,4},{6,5},{5,6},{4,7},{11,8},{10,9},{9,1... | collective-permute-start | bytes 110600 | tf_op jit(solution)/shard_map/ppermute | solution.py:31
  55.7 5.0 %collective-permute-start.21 = (f32[72,128]{1,0:T(8,128)S(1)}, f32[72,128]{1,0:T(8,128)S(1)}, u32[]{:S(2)}, u32[]{:S(2)}) collective-permute-start(f32[72,128]{1,0:T(8,128)S(1)} %get-tuple-element.60.refs_4_), channel_id=1, source_target_pairs={{2,0},{3,1},{0,2},{1,3},{6,4},{7,5},{4,6},{5,7},{10,8},{11,9},{8,1... | collective-permute-start | bytes 110600 | tf_op jit(solution)/shard_map/ppermute | solution.py:31
  56.4 4.4 %collective-permute-start.22 = (f32[72,128]{1,0:T(8,128)S(1)}, f32[72,128]{1,0:T(8,128)S(1)}, u32[]{:S(2)}, u32[]{:S(2)}) collective-permute-start(f32[72,128]{1,0:T(8,128)S(1)} %get-tuple-element.60.refs_4_), channel_id=1, source_target_pairs={{1,0},{0,1},{3,2},{2,3},{5,4},{4,5},{7,6},{6,7},{9,8},{8,9},{11,10... | collective-permute-start | bytes 110600 | tf_op jit(solution)/shard_map/ppermute | solution.py:31
  62.0 4.6 %collective-permute-start.23 = (f32[8,128]{1,0:T(8,128)S(1)}, f32[8,128]{1,0:T(8,128)S(1)}, u32[]{:S(2)}, u32[]{:S(2)}) collective-permute-start(f32[8,128]{1,0:T(8,128)S(1)} %get-tuple-element.63.refs_2_), channel_id=1, source_target_pairs={{24,0},{16,8},{8,16},{0,24},{25,1},{17,9},{9,17},{1,25},{26,2},{18... | collective-permute-start | bytes 12296 | tf_op jit(solution)/shard_map/ppermute | solution.py:43
  63.0 3.6 %collective-permute-start.24 = (f32[8,128]{1,0:T(8,128)S(1)}, f32[8,128]{1,0:T(8,128)S(1)}, u32[]{:S(2)}, u32[]{:S(2)}) collective-permute-start(f32[8,128]{1,0:T(8,128)S(1)} %get-tuple-element.63.refs_2_), channel_id=1, source_target_pairs={{8,0},{0,8},{24,16},{16,24},{9,1},{1,9},{25,17},{17,25},{10,2},{2,... | collective-permute-start | bytes 12296 | tf_op jit(solution)/shard_map/ppermute | solution.py:43
  67.4 5.8 %collective-permute-start.25 = (f32[72,128]{1,0:T(8,128)S(1)}, f32[72,128]{1,0:T(8,128)S(1)}, u32[]{:S(2)}, u32[]{:S(2)}) collective-permute-start(f32[72,128]{1,0:T(8,128)S(1)} %get-tuple-element.66.refs_4_), channel_id=1, source_target_pairs={{3,0},{2,1},{1,2},{0,3},{7,4},{6,5},{5,6},{4,7},{11,8},{10,9},{9,1... | collective-permute-start | bytes 110600 | tf_op jit(solution)/shard_map/ppermute | solution.py:31
  69.3 5.3 %collective-permute-start.26 = (f32[72,128]{1,0:T(8,128)S(1)}, f32[72,128]{1,0:T(8,128)S(1)}, u32[]{:S(2)}, u32[]{:S(2)}) collective-permute-start(f32[72,128]{1,0:T(8,128)S(1)} %get-tuple-element.66.refs_4_), channel_id=1, source_target_pairs={{2,0},{3,1},{0,2},{1,3},{6,4},{7,5},{4,6},{5,7},{10,8},{11,9},{8,1... | collective-permute-start | bytes 110600 | tf_op jit(solution)/shard_map/ppermute | solution.py:31
  70.3 4.3 %collective-permute-start.27 = (f32[72,128]{1,0:T(8,128)S(1)}, f32[72,128]{1,0:T(8,128)S(1)}, u32[]{:S(2)}, u32[]{:S(2)}) collective-permute-start(f32[72,128]{1,0:T(8,128)S(1)} %get-tuple-element.66.refs_4_), channel_id=1, source_target_pairs={{1,0},{0,1},{3,2},{2,3},{5,4},{4,5},{7,6},{6,7},{9,8},{8,9},{11,10... | collective-permute-start | bytes 110600 | tf_op jit(solution)/shard_map/ppermute | solution.py:31
  75.0 4.1 %collective-permute-start.28 = (f32[8,128]{1,0:T(8,128)S(1)}, f32[8,128]{1,0:T(8,128)S(1)}, u32[]{:S(2)}, u32[]{:S(2)}) collective-permute-start(f32[8,128]{1,0:T(8,128)S(1)} %get-tuple-element.72.refs_2_), channel_id=1, source_target_pairs={{16,0},{24,8},{0,16},{8,24},{17,1},{25,9},{1,17},{9,25},{18,2},{26... | collective-permute-start | bytes 12296 | tf_op jit(solution)/shard_map/ppermute | solution.py:48
  76.0 4.5 %collective-permute-start.29 = (f32[8,128]{1,0:T(8,128)S(1)}, f32[8,128]{1,0:T(8,128)S(1)}, u32[]{:S(2)}, u32[]{:S(2)}) collective-permute-start(f32[8,128]{1,0:T(8,128)S(1)} %get-tuple-element.72.refs_2_), channel_id=1, source_target_pairs={{24,0},{16,8},{8,16},{0,24},{25,1},{17,9},{9,17},{1,25},{26,2},{18... | collective-permute-start | bytes 12296 | tf_op jit(solution)/shard_map/ppermute | solution.py:43
  77.5 3.6 %collective-permute-start.30 = (f32[8,128]{1,0:T(8,128)S(1)}, f32[8,128]{1,0:T(8,128)S(1)}, u32[]{:S(2)}, u32[]{:S(2)}) collective-permute-start(f32[8,128]{1,0:T(8,128)S(1)} %get-tuple-element.72.refs_2_), channel_id=1, source_target_pairs={{8,0},{0,8},{24,16},{16,24},{9,1},{1,9},{25,17},{17,25},{10,2},{2,... | collective-permute-start | bytes 12296 | tf_op jit(solution)/shard_map/ppermute | solution.py:43
  (1 other events, 4.7 us)

commit v5 on v4

--- a/solution.py
+++ b/solution.py
@@ -596,7 +596,7 @@
         part(first_kernel, z),
         (*shared, *halves, *tiles[1:], wide),
         [line(z.nr * z.rows), line(4 * z.xrows), line(z.xrows), line(z.hop_first)],
-        [products, line(up(3 * listed, 8))],
+        [products, line(up(3 * listed, 8) + 8)],
     )
     turned, sibling_wide, sibling_turned = call(
         z,
@@ -621,7 +621,7 @@
             part(primal_kernel, z, starts, first, ends),
             operands,
             shapes,
-            [line(z.xrows), line(z.xrows), line(up(z.listed, 8)), line(up(3 * listed, 8))],
+            [line(z.xrows), line(z.xrows), line(up(z.listed, 8)), line(up(3 * listed, 8) + 8)],
         )
         x_next, zmsg = outs[:2]
         if starts:
@@ -644,7 +644,7 @@
             part(dual_kernel, z, ends, order),
             operands + ([y_begin] if ends else []),
             [line(z.nr * z.rows), line(z.xrows), line(z.hop)],
-            [products, line(up(3 * listed, 8))],
+            [products, line(up(3 * listed, 8) + 8)],
         )
         y = y_next
         if ends:

time: 82 us -> 81.9 us (level)
  no operation moved by 1% of the time
where the time goes in v5:
time: 81.9 us; the launch traced here: 81.7 us
  starting transfers between devices  39.4 us (48%)
  waiting for transfers between devices  25.7 us (31%)
  Pallas kernels  15.8 us (19%)
    ppermute x18, starting transfers between devices, from_peer(): return lax.ppermute(x, axis, pairs)  23.7 us
    pallas_call x16, Pallas kernels, call(): pl.pallas_call(kernel, out_shape=[jax.ShapeDtypeStruct(s, kind) for s, ki...  15.8 us
    ppermute x18, waiting for transfers between devices, from_peer(): return lax.ppermute(x, axis, pairs)  13.9 us
    ppermute x10, starting transfers between devices, period_exchange(): lax.ppermute(x, 'period', [(m[i], i) for i in range(n)])  12 us
    ppermute x10, waiting for transfers between devices, period_exchange(): lax.ppermute(x, 'period', [(m[i], i) for i in range(n)])  11.7 us
    ppermute x3, starting transfers between devices, period_exchange(): lax.ppermute(x, 'period', [((i + s) % n, i) for i in range(n)])  3.67 us
  transfers between devices with their start and end apart: 31, of which 21 were waited for; matrix products, arithmetic and copies ran while one was open for 0% of the time, Pallas kernels for 8%

profile of v5, /device:TPU:0, one launch (start us, length us, event | category | flops | bytes accessed | tf_op | source)
XLA Modules:
  0.0 81.7 jit_solution(1835256454807543898)
XLA Ops:
  1.1 1.6 %shard_map.131.refs_4_ = f32[104,128]{1,0:T(8,128)} custom-call(f32[32,128]{1,0:T(8,128)} %dual_at.1, f32[32,128]{1,0:T(8,128)} %rhs_at.1, s32[32,128]{1,0:T(8,128)} %rkind_at.1, f32[64,128]{1,0:T(8,128)} %obj_at.3, s32[1,32]{1,0:T(1,128)} %bitcast.8), custom_call_target="tpu_custom_call" | custom-call | tf_op jit(solution)/shard_map/pallas_call | solution.py:506
  2.7 4.7 %collective-permute-start = (f32[104,128]{1,0:T(8,128)}, f32[104,128]{1,0:T(8,128)S(1)}, u32[]{:S(2)}, u32[]{:S(2)}) collective-permute-start(f32[104,128]{1,0:T(8,128)} %shard_map.131.refs_4_), channel_id=1, source_target_pairs={{3,0},{2,1},{1,2},{0,3},{7,4},{6,5},{5,6},{4,7},{11,8},{10,9},{9,1... | collective-permute-start | bytes 159752 | tf_op jit(solution)/shard_map/ppermute | solution.py:31
  8.0 1.7 %shard_map.133.refs_2_.refs_6_.refs_7_.refs_8_ = f32[392,128]{1,0:T(8,128)} custom-call(f32[64,128]{1,0:T(8,128)} %x_at.1, f32[64,128]{1,0:T(8,128)} %obj_at.3, f32[64,128]{1,0:T(8,128)} %ub_at.1, s32[64,128]{1,0:T(8,128)} %ckind_at.1, s32[1,32]{1,0:T(1,128)} %bitcast.9, f32[128,128]{1,0:T(8,128)} %bitcast.7), custom_call_target="tpu_custom_call" | custom-call | tf_op jit(solution)/shard_map/pallas_call | solution.py:506
  9.8 1.6 %shard_map.130 = (f32[32,128,128]{2,1,0:T(8,128)S(1)}, bf16[32,128,256]{2,1,0:T(8,128)(2,1)S(1)}, f32[8,128]{1,0:T(8,128)S(1)}) custom-call(f32[32,128,128]{2,1,0:T(8,128)} %bitcast.6), custom_call_target="tpu_custom_call" | custom-call | tf_op jit(solution)/shard_map/pallas_call | solution.py:506
  11.5 1.4 %collective-permute-done.1.refs_2_ = f32[104,128]{1,0:T(8,128)S(1)} collective-permute-done((f32[104,128]{1,0:T(8,128)}, f32[104,128]{1,0:T(8,128)S(1)}, u32[]{:S(2)}, u32[]{:S(2)}) %collective-permute-start.1) | collective-permute-done | bytes 53280 | tf_op jit(solution)/shard_map/ppermute | solution.py:31
  13.0 1.4 %collective-permute-done.3.refs_1_.refs_6_ = f32[392,128]{1,0:T(8,128)S(1)} collective-permute-done((f32[392,128]{1,0:T(8,128)S(1)}, f32[392,128]{1,0:T(8,128)S(1)}, u32[]{:S(2)}, u32[]{:S(2)}) %collective-permute-start.3) | collective-permute-done | bytes 200736 | tf_op jit(solution)/shard_map/ppermute | solution.py:31
  15.7 1.6 %collective-permute-start.6 = (f32[16,128]{1,0:T(8,128)S(1)}, f32[16,128]{1,0:T(8,128)S(1)}, u32[]{:S(2)}, u32[]{:S(2)}) collective-permute-start(f32[16,128]{1,0:T(8,128)S(1)} %get-tuple-element.41.refs_1_), channel_id=1, source_target_pairs={{16,0},{24,8},{0,16},{8,24},{17,1},{25,9},{1,17},{9,25},{18,2},{26... | collective-permute-start | bytes 24584 | tf_op jit(solution)/shard_map/ppermute | solution.py:48
  17.3 1.4 %collective-permute-start.7 = (f32[16,128]{1,0:T(8,128)S(1)}, f32[16,128]{1,0:T(8,128)S(1)}, u32[]{:S(2)}, u32[]{:S(2)}) collective-permute-start(f32[16,128]{1,0:T(8,128)S(1)} %get-tuple-element.41.refs_1_), channel_id=1, source_target_pairs={{24,0},{16,8},{8,16},{0,24},{25,1},{17,9},{9,17},{1,25},{26,2},{18... | collective-permute-start | bytes 24584 | tf_op jit(solution)/shard_map/ppermute | solution.py:43
  20.3 1.5 %collective-permute-done.7.refs_3_ = f32[16,128]{1,0:T(8,128)S(1)} collective-permute-done((f32[16,128]{1,0:T(8,128)S(1)}, f32[16,128]{1,0:T(8,128)S(1)}, u32[]{:S(2)}, u32[]{:S(2)}) %collective-permute-start.7) | collective-permute-done | bytes 8224 | tf_op jit(solution)/shard_map/ppermute | solution.py:43
  23.2 2.5 %collective-permute-start.10 = (f32[72,128]{1,0:T(8,128)S(1)}, f32[72,128]{1,0:T(8,128)S(1)}, u32[]{:S(2)}, u32[]{:S(2)}) collective-permute-start(f32[72,128]{1,0:T(8,128)S(1)} %get-tuple-element.47.refs_4_), channel_id=1, source_target_pairs={{3,0},{2,1},{1,2},{0,3},{7,4},{6,5},{5,6},{4,7},{11,8},{10,9},{9,1... | collective-permute-start | bytes 110600 | tf_op jit(solution)/shard_map/ppermute | solution.py:31
  26.0 1.6 %collective-permute-start.9 = (f32[72,128]{1,0:T(8,128)S(1)}, f32[72,128]{1,0:T(8,128)S(1)}, u32[]{:S(2)}, u32[]{:S(2)}) collective-permute-start(f32[72,128]{1,0:T(8,128)S(1)} %get-tuple-element.47.refs_4_), channel_id=1, source_target_pairs={{1,0},{0,1},{3,2},{2,3},{5,4},{4,5},{7,6},{6,7},{9,8},{8,9},{11,10... | collective-permute-start | bytes 110600 | tf_op jit(solution)/shard_map/ppermute | solution.py:31
  27.6 1.6 %collective-permute-done.10.refs_2_ = f32[72,128]{1,0:T(8,128)S(1)} collective-permute-done((f32[72,128]{1,0:T(8,128)S(1)}, f32[72,128]{1,0:T(8,128)S(1)}, u32[]{:S(2)}, u32[]{:S(2)}) %collective-permute-start.10) | collective-permute-done | bytes 36896 | tf_op jit(solution)/shard_map/ppermute | solution.py:31
  29.2 1.3 %collective-permute-done.11.refs_3_ = f32[72,128]{1,0:T(8,128)S(1)} collective-permute-done((f32[72,128]{1,0:T(8,128)S(1)}, f32[72,128]{1,0:T(8,128)S(1)}, u32[]{:S(2)}, u32[]{:S(2)}) %collective-permute-start.11) | collective-permute-done | bytes 36896 | tf_op jit(solution)/shard_map/ppermute | solution.py:31
  31.8 1.6 %collective-permute-start.12 = (f32[8,128]{1,0:T(8,128)S(1)}, f32[8,128]{1,0:T(8,128)S(1)}, u32[]{:S(2)}, u32[]{:S(2)}) collective-permute-start(f32[8,128]{1,0:T(8,128)S(1)} %get-tuple-element.51.refs_2_), channel_id=1, source_target_pairs={{24,0},{16,8},{8,16},{0,24},{25,1},{17,9},{9,17},{1,25},{26,2},{18... | collective-permute-start | bytes 12296 | tf_op jit(solution)/shard_map/ppermute | solution.py:43
  33.3 1.5 %collective-permute-start.13 = (f32[8,128]{1,0:T(8,128)S(1)}, f32[8,128]{1,0:T(8,128)S(1)}, u32[]{:S(2)}, u32[]{:S(2)}) collective-permute-start(f32[8,128]{1,0:T(8,128)S(1)} %get-tuple-element.51.refs_2_), channel_id=1, source_target_pairs={{8,0},{0,8},{24,16},{16,24},{9,1},{1,9},{25,17},{17,25},{10,2},{2,... | collective-permute-start | bytes 12296 | tf_op jit(solution)/shard_map/ppermute | solution.py:43
  34.8 1.5 %collective-permute-done.12.refs_3_ = f32[8,128]{1,0:T(8,128)S(1)} collective-permute-done((f32[8,128]{1,0:T(8,128)S(1)}, f32[8,128]{1,0:T(8,128)S(1)}, u32[]{:S(2)}, u32[]{:S(2)}) %collective-permute-start.12) | collective-permute-done | bytes 4128 | tf_op jit(solution)/shard_map/ppermute | solution.py:43
  37.8 1.9 %collective-permute-start.14 = (f32[72,128]{1,0:T(8,128)S(1)}, f32[72,128]{1,0:T(8,128)S(1)}, u32[]{:S(2)}, u32[]{:S(2)}) collective-permute-start(f32[72,128]{1,0:T(8,128)S(1)} %get-tuple-element.54.refs_4_), channel_id=1, source_target_pairs={{3,0},{2,1},{1,2},{0,3},{7,4},{6,5},{5,6},{4,7},{11,8},{10,9},{9,1... | collective-permute-start | bytes 110600 | tf_op jit(solution)/shard_map/ppermute | solution.py:31
  40.3 1.9 %collective-permute-start.16 = (f32[72,128]{1,0:T(8,128)S(1)}, f32[72,128]{1,0:T(8,128)S(1)}, u32[]{:S(2)}, u32[]{:S(2)}) collective-permute-start(f32[72,128]{1,0:T(8,128)S(1)} %get-tuple-element.54.refs_4_), channel_id=1, source_target_pairs={{1,0},{0,1},{3,2},{2,3},{5,4},{4,5},{7,6},{6,7},{9,8},{8,9},{11,10... | collective-permute-start | bytes 110600 | tf_op jit(solution)/shard_map/ppermute | solution.py:31
  42.2 1.4 %collective-permute-done.14.refs_1_ = f32[72,128]{1,0:T(8,128)S(1)} collective-permute-done((f32[72,128]{1,0:T(8,128)S(1)}, f32[72,128]{1,0:T(8,128)S(1)}, u32[]{:S(2)}, u32[]{:S(2)}) %collective-permute-start.14) | collective-permute-done | bytes 36896 | tf_op jit(solution)/shard_map/ppermute | solution.py:31
  43.6 1.3 %collective-permute-done.15.refs_2_ = f32[72,128]{1,0:T(8,128)S(1)} collective-permute-done((f32[72,128]{1,0:T(8,128)S(1)}, f32[72,128]{1,0:T(8,128)S(1)}, u32[]{:S(2)}, u32[]{:S(2)}) %collective-permute-start.15) | collective-permute-done | bytes 36896 | tf_op jit(solution)/shard_map/ppermute | solution.py:31
  47.2 2.0 %collective-permute-start.18 = (f32[8,128]{1,0:T(8,128)S(1)}, f32[8,128]{1,0:T(8,128)S(1)}, u32[]{:S(2)}, u32[]{:S(2)}) collective-permute-start(f32[8,128]{1,0:T(8,128)S(1)} %get-tuple-element.57.refs_2_), channel_id=1, source_target_pairs={{24,0},{16,8},{8,16},{0,24},{25,1},{17,9},{9,17},{1,25},{26,2},{18... | collective-permute-start | bytes 12296 | tf_op jit(solution)/shard_map/ppermute | solution.py:43
  49.9 1.8 %collective-permute-done.18.refs_4_ = f32[8,128]{1,0:T(8,128)S(1)} collective-permute-done((f32[8,128]{1,0:T(8,128)S(1)}, f32[8,128]{1,0:T(8,128)S(1)}, u32[]{:S(2)}, u32[]{:S(2)}) %collective-permute-start.18) | collective-permute-done | bytes 4128 | tf_op jit(solution)/shard_map/ppermute | solution.py:43
  53.7 2.0 %collective-permute-start.20 = (f32[72,128]{1,0:T(8,128)S(1)}, f32[72,128]{1,0:T(8,128)S(1)}, u32[]{:S(2)}, u32[]{:S(2)}) collective-permute-start(f32[72,128]{1,0:T(8,128)S(1)} %get-tuple-element.60.refs_4_), channel_id=1, source_target_pairs={{3,0},{2,1},{1,2},{0,3},{7,4},{6,5},{5,6},{4,7},{11,8},{10,9},{9,1... | collective-permute-start | bytes 110600 | tf_op jit(solution)/shard_map/ppermute | solution.py:31
  56.4 1.7 %collective-permute-start.22 = (f32[72,128]{1,0:T(8,128)S(1)}, f32[72,128]{1,0:T(8,128)S(1)}, u32[]{:S(2)}, u32[]{:S(2)}) collective-permute-start(f32[72,128]{1,0:T(8,128)S(1)} %get-tuple-element.60.refs_4_), channel_id=1, source_target_pairs={{1,0},{0,1},{3,2},{2,3},{5,4},{4,5},{7,6},{6,7},{9,8},{8,9},{11,10... | collective-permute-start | bytes 110600 | tf_op jit(solution)/shard_map/ppermute | solution.py:31
  58.1 1.4 %collective-permute-done.20.refs_1_ = f32[72,128]{1,0:T(8,128)S(1)} collective-permute-done((f32[72,128]{1,0:T(8,128)S(1)}, f32[72,128]{1,0:T(8,128)S(1)}, u32[]{:S(2)}, u32[]{:S(2)}) %collective-permute-start.20) | collective-permute-done | bytes 36896 | tf_op jit(solution)/shard_map/ppermute | solution.py:31
  64.0 2.5 %collective-permute-done.23.refs_3_ = f32[8,128]{1,0:T(8,128)S(1)} collective-permute-done((f32[8,128]{1,0:T(8,128)S(1)}, f32[8,128]{1,0:T(8,128)S(1)}, u32[]{:S(2)}, u32[]{:S(2)}) %collective-permute-start.23) | collective-permute-done | bytes 4128 | tf_op jit(solution)/shard_map/ppermute | solution.py:43
  67.4 1.9 %collective-permute-start.25 = (f32[72,128]{1,0:T(8,128)S(1)}, f32[72,128]{1,0:T(8,128)S(1)}, u32[]{:S(2)}, u32[]{:S(2)}) collective-permute-start(f32[72,128]{1,0:T(8,128)S(1)} %get-tuple-element.66.refs_4_), channel_id=1, source_target_pairs={{3,0},{2,1},{1,2},{0,3},{7,4},{6,5},{5,6},{4,7},{11,8},{10,9},{9,1... | collective-permute-start | bytes 110600 | tf_op jit(solution)/shard_map/ppermute | solution.py:31
  70.3 1.5 %collective-permute-start.27 = (f32[72,128]{1,0:T(8,128)S(1)}, f32[72,128]{1,0:T(8,128)S(1)}, u32[]{:S(2)}, u32[]{:S(2)}) collective-permute-start(f32[72,128]{1,0:T(8,128)S(1)} %get-tuple-element.66.refs_4_), channel_id=1, source_target_pairs={{1,0},{0,1},{3,2},{2,3},{5,4},{4,5},{7,6},{6,7},{9,8},{8,9},{11,10... | collective-permute-start | bytes 110600 | tf_op jit(solution)/shard_map/ppermute | solution.py:31
  71.8 1.4 %collective-permute-done.25.refs_1_ = f32[72,128]{1,0:T(8,128)S(1)} collective-permute-done((f32[72,128]{1,0:T(8,128)S(1)}, f32[72,128]{1,0:T(8,128)S(1)}, u32[]{:S(2)}, u32[]{:S(2)}) %collective-permute-start.25) | collective-permute-done | bytes 36896 | tf_op jit(solution)/shard_map/ppermute | solution.py:31
  73.2 1.4 %collective-permute-done.26.refs_2_ = f32[72,128]{1,0:T(8,128)S(1)} collective-permute-done((f32[72,128]{1,0:T(8,128)S(1)}, f32[72,128]{1,0:T(8,128)S(1)}, u32[]{:S(2)}, u32[]{:S(2)}) %collective-permute-start.26) | collective-permute-done | bytes 36896 | tf_op jit(solution)/shard_map/ppermute | solution.py:31
  76.0 1.4 %collective-permute-start.29 = (f32[8,128]{1,0:T(8,128)S(1)}, f32[8,128]{1,0:T(8,128)S(1)}, u32[]{:S(2)}, u32[]{:S(2)}) collective-permute-start(f32[8,128]{1,0:T(8,128)S(1)} %get-tuple-element.72.refs_2_), channel_id=1, source_target_pairs={{24,0},{16,8},{8,16},{0,24},{25,1},{17,9},{9,17},{1,25},{26,2},{18... | collective-permute-start | bytes 12296 | tf_op jit(solution)/shard_map/ppermute | solution.py:43
  79.1 1.5 %collective-permute-done.29.refs_4_ = f32[8,128]{1,0:T(8,128)S(1)} collective-permute-done((f32[8,128]{1,0:T(8,128)S(1)}, f32[8,128]{1,0:T(8,128)S(1)}, u32[]{:S(2)}, u32[]{:S(2)}) %collective-permute-start.29) | collective-permute-done | bytes 4128 | tf_op jit(solution)/shard_map/ppermute | solution.py:43
  (51 shorter events, 25.2 us)
Async XLA Ops:
  0.6 13.8 %collective-permute-start.5 = (f32[32,128,128]{2,1,0:T(8,128)}, f32[32,128,128]{2,1,0:T(8,128)S(1)}, u32[]{:S(2)}, u32[]{:S(2)}) collective-permute-start(f32[32,128,128]{2,1,0:T(8,128)} %bitcast.5), channel_id=1, source_target_pairs={{4,0},{0,4},{5,1},{1,5},{6,2},{2,6},{7,3},{3,7},{12,8},{8,12},{13,... | collective-permute-start | bytes 6291464 | tf_op jit(solution)/shard_map/ppermute | solution.py:31
  2.7 10.2 %copy-start.1 = (f32[104,128]{1,0:T(8,128)S(1)}, f32[104,128]{1,0:T(8,128)}, u32[]{:S(2)}) copy-start(f32[104,128]{1,0:T(8,128)} %shard_map.131.refs_4_) | copy-start | bytes 159748
  2.7 8.7 %collective-permute-start = (f32[104,128]{1,0:T(8,128)}, f32[104,128]{1,0:T(8,128)S(1)}, u32[]{:S(2)}, u32[]{:S(2)}) collective-permute-start(f32[104,128]{1,0:T(8,128)} %shard_map.131.refs_4_), channel_id=1, source_target_pairs={{3,0},{2,1},{1,2},{0,3},{7,4},{6,5},{5,6},{4,7},{11,8},{10,9},{9,1... | collective-permute-start | bytes 159752 | tf_op jit(solution)/shard_map/ppermute | solution.py:31
  7.4 5.5 %collective-permute-start.1 = (f32[104,128]{1,0:T(8,128)}, f32[104,128]{1,0:T(8,128)S(1)}, u32[]{:S(2)}, u32[]{:S(2)}) collective-permute-start(f32[104,128]{1,0:T(8,128)} %shard_map.131.refs_4_), channel_id=1, source_target_pairs={{2,0},{3,1},{0,2},{1,3},{6,4},{7,5},{4,6},{5,7},{10,8},{11,9},{8,1... | collective-permute-start | bytes 159752 | tf_op jit(solution)/shard_map/ppermute | solution.py:31
  7.4 5.5 %collective-permute-start.2 = (f32[104,128]{1,0:T(8,128)}, f32[104,128]{1,0:T(8,128)S(1)}, u32[]{:S(2)}, u32[]{:S(2)}) collective-permute-start(f32[104,128]{1,0:T(8,128)} %shard_map.131.refs_4_), channel_id=1, source_target_pairs={{1,0},{0,1},{3,2},{2,3},{5,4},{4,5},{7,6},{6,7},{9,8},{8,9},{11,10... | collective-permute-start | bytes 159752 | tf_op jit(solution)/shard_map/ppermute | solution.py:31
  9.7 3.3 %collective-permute-start.4 = (f32[392,128]{1,0:T(8,128)}, f32[392,128]{1,0:T(8,128)S(1)}, u32[]{:S(2)}, u32[]{:S(2)}) collective-permute-start(f32[392,128]{1,0:T(8,128)} %shard_map.133.refs_2_.refs_6_.refs_7_.refs_8_), channel_id=1, source_target_pairs={{4,0},{0,4},{5,1},{1,5},{6,2},{2,6},{7,3},{3,7},{12,8},{8,12},{13,... | collective-permute-start | bytes 602120 | tf_op jit(solution)/shard_map/ppermute | solution.py:31
  13.0 1.5 %collective-permute-start.3 = (f32[392,128]{1,0:T(8,128)S(1)}, f32[392,128]{1,0:T(8,128)S(1)}, u32[]{:S(2)}, u32[]{:S(2)}) collective-permute-start(f32[392,128]{1,0:T(8,128)S(1)} %shard_map.132.refs_0_.refs_5_), channel_id=1, source_target_pairs={{4,0},{0,4},{5,1},{1,5},{6,2},{2,6},{7,3},{3,7},{12,8},{8,12},{13,... | collective-permute-start | bytes 602120 | tf_op jit(solution)/shard_map/ppermute | solution.py:31
  15.7 4.6 %collective-permute-start.6 = (f32[16,128]{1,0:T(8,128)S(1)}, f32[16,128]{1,0:T(8,128)S(1)}, u32[]{:S(2)}, u32[]{:S(2)}) collective-permute-start(f32[16,128]{1,0:T(8,128)S(1)} %get-tuple-element.41.refs_1_), channel_id=1, source_target_pairs={{16,0},{24,8},{0,16},{8,24},{17,1},{25,9},{1,17},{9,25},{18,2},{26... | collective-permute-start | bytes 24584 | tf_op jit(solution)/shard_map/ppermute | solution.py:48
  17.3 4.5 %collective-permute-start.7 = (f32[16,128]{1,0:T(8,128)S(1)}, f32[16,128]{1,0:T(8,128)S(1)}, u32[]{:S(2)}, u32[]{:S(2)}) collective-permute-start(f32[16,128]{1,0:T(8,128)S(1)} %get-tuple-element.41.refs_1_), channel_id=1, source_target_pairs={{24,0},{16,8},{8,16},{0,24},{25,1},{17,9},{9,17},{1,25},{26,2},{18... | collective-permute-start | bytes 24584 | tf_op jit(solution)/shard_map/ppermute | solution.py:43
  18.7 3.7 %collective-permute-start.8 = (f32[16,128]{1,0:T(8,128)S(1)}, f32[16,128]{1,0:T(8,128)S(1)}, u32[]{:S(2)}, u32[]{:S(2)}) collective-permute-start(f32[16,128]{1,0:T(8,128)S(1)} %get-tuple-element.41.refs_1_), channel_id=1, source_target_pairs={{8,0},{0,8},{24,16},{16,24},{9,1},{1,9},{25,17},{17,25},{10,2},{2,... | collective-permute-start | bytes 24584 | tf_op jit(solution)/shard_map/ppermute | solution.py:43
  23.2 6.1 %collective-permute-start.10 = (f32[72,128]{1,0:T(8,128)S(1)}, f32[72,128]{1,0:T(8,128)S(1)}, u32[]{:S(2)}, u32[]{:S(2)}) collective-permute-start(f32[72,128]{1,0:T(8,128)S(1)} %get-tuple-element.47.refs_4_), channel_id=1, source_target_pairs={{3,0},{2,1},{1,2},{0,3},{7,4},{6,5},{5,6},{4,7},{11,8},{10,9},{9,1... | collective-permute-start | bytes 110600 | tf_op jit(solution)/shard_map/ppermute | solution.py:31
  25.7 4.9 %collective-permute-start.11 = (f32[72,128]{1,0:T(8,128)S(1)}, f32[72,128]{1,0:T(8,128)S(1)}, u32[]{:S(2)}, u32[]{:S(2)}) collective-permute-start(f32[72,128]{1,0:T(8,128)S(1)} %get-tuple-element.47.refs_4_), channel_id=1, source_target_pairs={{2,0},{3,1},{0,2},{1,3},{6,4},{7,5},{4,6},{5,7},{10,8},{11,9},{8,1... | collective-permute-start | bytes 110600 | tf_op jit(solution)/shard_map/ppermute | solution.py:31
  26.0 4.6 %collective-permute-start.9 = (f32[72,128]{1,0:T(8,128)S(1)}, f32[72,128]{1,0:T(8,128)S(1)}, u32[]{:S(2)}, u32[]{:S(2)}) collective-permute-start(f32[72,128]{1,0:T(8,128)S(1)} %get-tuple-element.47.refs_4_), channel_id=1, source_target_pairs={{1,0},{0,1},{3,2},{2,3},{5,4},{4,5},{7,6},{6,7},{9,8},{8,9},{11,10... | collective-permute-start | bytes 110600 | tf_op jit(solution)/shard_map/ppermute | solution.py:31
  31.8 4.6 %collective-permute-start.12 = (f32[8,128]{1,0:T(8,128)S(1)}, f32[8,128]{1,0:T(8,128)S(1)}, u32[]{:S(2)}, u32[]{:S(2)}) collective-permute-start(f32[8,128]{1,0:T(8,128)S(1)} %get-tuple-element.51.refs_2_), channel_id=1, source_target_pairs={{24,0},{16,8},{8,16},{0,24},{25,1},{17,9},{9,17},{1,25},{26,2},{18... | collective-permute-start | bytes 12296 | tf_op jit(solution)/shard_map/ppermute | solution.py:43
  33.3 3.6 %collective-permute-start.13 = (f32[8,128]{1,0:T(8,128)S(1)}, f32[8,128]{1,0:T(8,128)S(1)}, u32[]{:S(2)}, u32[]{:S(2)}) collective-permute-start(f32[8,128]{1,0:T(8,128)S(1)} %get-tuple-element.51.refs_2_), channel_id=1, source_target_pairs={{8,0},{0,8},{24,16},{16,24},{9,1},{1,9},{25,17},{17,25},{10,2},{2,... | collective-permute-start | bytes 12296 | tf_op jit(solution)/shard_map/ppermute | solution.py:43
  37.8 5.8 %collective-permute-start.14 = (f32[72,128]{1,0:T(8,128)S(1)}, f32[72,128]{1,0:T(8,128)S(1)}, u32[]{:S(2)}, u32[]{:S(2)}) collective-permute-start(f32[72,128]{1,0:T(8,128)S(1)} %get-tuple-element.54.refs_4_), channel_id=1, source_target_pairs={{3,0},{2,1},{1,2},{0,3},{7,4},{6,5},{5,6},{4,7},{11,8},{10,9},{9,1... | collective-permute-start | bytes 110600 | tf_op jit(solution)/shard_map/ppermute | solution.py:31
  39.7 5.3 %collective-permute-start.15 = (f32[72,128]{1,0:T(8,128)S(1)}, f32[72,128]{1,0:T(8,128)S(1)}, u32[]{:S(2)}, u32[]{:S(2)}) collective-permute-start(f32[72,128]{1,0:T(8,128)S(1)} %get-tuple-element.54.refs_4_), channel_id=1, source_target_pairs={{2,0},{3,1},{0,2},{1,3},{6,4},{7,5},{4,6},{5,7},{10,8},{11,9},{8,1... | collective-permute-start | bytes 110600 | tf_op jit(solution)/shard_map/ppermute | solution.py:31
  40.3 4.6 %collective-permute-start.16 = (f32[72,128]{1,0:T(8,128)S(1)}, f32[72,128]{1,0:T(8,128)S(1)}, u32[]{:S(2)}, u32[]{:S(2)}) collective-permute-start(f32[72,128]{1,0:T(8,128)S(1)} %get-tuple-element.54.refs_4_), channel_id=1, source_target_pairs={{1,0},{0,1},{3,2},{2,3},{5,4},{4,5},{7,6},{6,7},{9,8},{8,9},{11,10... | collective-permute-start | bytes 110600 | tf_op jit(solution)/shard_map/ppermute | solution.py:31
  46.2 3.7 %collective-permute-start.17 = (f32[8,128]{1,0:T(8,128)S(1)}, f32[8,128]{1,0:T(8,128)S(1)}, u32[]{:S(2)}, u32[]{:S(2)}) collective-permute-start(f32[8,128]{1,0:T(8,128)S(1)} %get-tuple-element.57.refs_2_), channel_id=1, source_target_pairs={{16,0},{24,8},{0,16},{8,24},{17,1},{25,9},{1,17},{9,25},{18,2},{26... | collective-permute-start | bytes 12296 | tf_op jit(solution)/shard_map/ppermute | solution.py:48
  47.2 4.5 %collective-permute-start.18 = (f32[8,128]{1,0:T(8,128)S(1)}, f32[8,128]{1,0:T(8,128)S(1)}, u32[]{:S(2)}, u32[]{:S(2)}) collective-permute-start(f32[8,128]{1,0:T(8,128)S(1)} %get-tuple-element.57.refs_2_), channel_id=1, source_target_pairs={{24,0},{16,8},{8,16},{0,24},{25,1},{17,9},{9,17},{1,25},{26,2},{18... | collective-permute-start | bytes 12296 | tf_op jit(solution)/shard_map/ppermute | solution.py:43
  49.2 3.6 %collective-permute-start.19 = (f32[8,128]{1,0:T(8,128)S(1)}, f32[8,128]{1,0:T(8,128)S(1)}, u32[]{:S(2)}, u32[]{:S(2)}) collective-permute-start(f32[8,128]{1,0:T(8,128)S(1)} %get-tuple-element.57.refs_2_), channel_id=1, source_target_pairs={{8,0},{0,8},{24,16},{16,24},{9,1},{1,9},{25,17},{17,25},{10,2},{2,... | collective-permute-start | bytes 12296 | tf_op jit(solution)/shard_map/ppermute | solution.py:43
  53.7 5.8 %collective-permute-start.20 = (f32[72,128]{1,0:T(8,128)S(1)}, f32[72,128]{1,0:T(8,128)S(1)}, u32[]{:S(2)}, u32[]{:S(2)}) collective-permute-start(f32[72,128]{1,0:T(8,128)S(1)} %get-tuple-element.60.refs_4_), channel_id=1, source_target_pairs={{3,0},{2,1},{1,2},{0,3},{7,4},{6,5},{5,6},{4,7},{11,8},{10,9},{9,1... | collective-permute-start | bytes 110600 | tf_op jit(solution)/shard_map/ppermute | solution.py:31
  55.7 5.0 %collective-permute-start.21 = (f32[72,128]{1,0:T(8,128)S(1)}, f32[72,128]{1,0:T(8,128)S(1)}, u32[]{:S(2)}, u32[]{:S(2)}) collective-permute-start(f32[72,128]{1,0:T(8,128)S(1)} %get-tuple-element.60.refs_4_), channel_id=1, source_target_pairs={{2,0},{3,1},{0,2},{1,3},{6,4},{7,5},{4,6},{5,7},{10,8},{11,9},{8,1... | collective-permute-start | bytes 110600 | tf_op jit(solution)/shard_map/ppermute | solution.py:31
  56.4 4.4 %collective-permute-start.22 = (f32[72,128]{1,0:T(8,128)S(1)}, f32[72,128]{1,0:T(8,128)S(1)}, u32[]{:S(2)}, u32[]{:S(2)}) collective-permute-start(f32[72,128]{1,0:T(8,128)S(1)} %get-tuple-element.60.refs_4_), channel_id=1, source_target_pairs={{1,0},{0,1},{3,2},{2,3},{5,4},{4,5},{7,6},{6,7},{9,8},{8,9},{11,10... | collective-permute-start | bytes 110600 | tf_op jit(solution)/shard_map/ppermute | solution.py:31
  62.0 4.6 %collective-permute-start.23 = (f32[8,128]{1,0:T(8,128)S(1)}, f32[8,128]{1,0:T(8,128)S(1)}, u32[]{:S(2)}, u32[]{:S(2)}) collective-permute-start(f32[8,128]{1,0:T(8,128)S(1)} %get-tuple-element.63.refs_2_), channel_id=1, source_target_pairs={{24,0},{16,8},{8,16},{0,24},{25,1},{17,9},{9,17},{1,25},{26,2},{18... | collective-permute-start | bytes 12296 | tf_op jit(solution)/shard_map/ppermute | solution.py:43
  63.0 3.6 %collective-permute-start.24 = (f32[8,128]{1,0:T(8,128)S(1)}, f32[8,128]{1,0:T(8,128)S(1)}, u32[]{:S(2)}, u32[]{:S(2)}) collective-permute-start(f32[8,128]{1,0:T(8,128)S(1)} %get-tuple-element.63.refs_2_), channel_id=1, source_target_pairs={{8,0},{0,8},{24,16},{16,24},{9,1},{1,9},{25,17},{17,25},{10,2},{2,... | collective-permute-start | bytes 12296 | tf_op jit(solution)/shard_map/ppermute | solution.py:43
  67.4 5.8 %collective-permute-start.25 = (f32[72,128]{1,0:T(8,128)S(1)}, f32[72,128]{1,0:T(8,128)S(1)}, u32[]{:S(2)}, u32[]{:S(2)}) collective-permute-start(f32[72,128]{1,0:T(8,128)S(1)} %get-tuple-element.66.refs_4_), channel_id=1, source_target_pairs={{3,0},{2,1},{1,2},{0,3},{7,4},{6,5},{5,6},{4,7},{11,8},{10,9},{9,1... | collective-permute-start | bytes 110600 | tf_op jit(solution)/shard_map/ppermute | solution.py:31
  69.3 5.3 %collective-permute-start.26 = (f32[72,128]{1,0:T(8,128)S(1)}, f32[72,128]{1,0:T(8,128)S(1)}, u32[]{:S(2)}, u32[]{:S(2)}) collective-permute-start(f32[72,128]{1,0:T(8,128)S(1)} %get-tuple-element.66.refs_4_), channel_id=1, source_target_pairs={{2,0},{3,1},{0,2},{1,3},{6,4},{7,5},{4,6},{5,7},{10,8},{11,9},{8,1... | collective-permute-start | bytes 110600 | tf_op jit(solution)/shard_map/ppermute | solution.py:31
  70.3 4.3 %collective-permute-start.27 = (f32[72,128]{1,0:T(8,128)S(1)}, f32[72,128]{1,0:T(8,128)S(1)}, u32[]{:S(2)}, u32[]{:S(2)}) collective-permute-start(f32[72,128]{1,0:T(8,128)S(1)} %get-tuple-element.66.refs_4_), channel_id=1, source_target_pairs={{1,0},{0,1},{3,2},{2,3},{5,4},{4,5},{7,6},{6,7},{9,8},{8,9},{11,10... | collective-permute-start | bytes 110600 | tf_op jit(solution)/shard_map/ppermute | solution.py:31
  75.0 4.1 %collective-permute-start.28 = (f32[8,128]{1,0:T(8,128)S(1)}, f32[8,128]{1,0:T(8,128)S(1)}, u32[]{:S(2)}, u32[]{:S(2)}) collective-permute-start(f32[8,128]{1,0:T(8,128)S(1)} %get-tuple-element.72.refs_2_), channel_id=1, source_target_pairs={{16,0},{24,8},{0,16},{8,24},{17,1},{25,9},{1,17},{9,25},{18,2},{26... | collective-permute-start | bytes 12296 | tf_op jit(solution)/shard_map/ppermute | solution.py:48
  76.0 4.5 %collective-permute-start.29 = (f32[8,128]{1,0:T(8,128)S(1)}, f32[8,128]{1,0:T(8,128)S(1)}, u32[]{:S(2)}, u32[]{:S(2)}) collective-permute-start(f32[8,128]{1,0:T(8,128)S(1)} %get-tuple-element.72.refs_2_), channel_id=1, source_target_pairs={{24,0},{16,8},{8,16},{0,24},{25,1},{17,9},{9,17},{1,25},{26,2},{18... | collective-permute-start | bytes 12296 | tf_op jit(solution)/shard_map/ppermute | solution.py:43
  77.5 3.6 %collective-permute-start.30 = (f32[8,128]{1,0:T(8,128)S(1)}, f32[8,128]{1,0:T(8,128)S(1)}, u32[]{:S(2)}, u32[]{:S(2)}) collective-permute-start(f32[8,128]{1,0:T(8,128)S(1)} %get-tuple-element.72.refs_2_), channel_id=1, source_target_pairs={{8,0},{0,8},{24,16},{16,24},{9,1},{1,9},{25,17},{17,25},{10,2},{2,... | collective-permute-start | bytes 12296 | tf_op jit(solution)/shard_map/ppermute | solution.py:43
  (1 other events, 4.7 us)
